TPU v7x, 32 devices: a whole 2x2x4 slice. The times are simulated.
32 devices in a mesh: rows: 4 (over x, core), cols: 8 (over z, y).
Axes of the slice: x: 2, y: 2, z: 4, core: 2. Of those that a mesh axis runs over, the one named last changes fastest.
Arguments:
- tokens: bfloat16 [8192, 2048], P('rows', 'cols'), may hold values from -6 to 6
- segment_ids: int32 [4, 2048], P('rows'), may hold values from 0 to 7, never falling along the last dimension, each value on 1 to 1024 neighbouring positions
- w_query: bfloat16 [2048, 2048], P('rows', 'cols'), may hold values from -0.125 to 0.125
- w_key: bfloat16 [2048, 2048], P('rows', 'cols'), may hold values from -0.125 to 0.125
- w_value: bfloat16 [2048, 2048], P('rows', 'cols'), may hold values from -0.125 to 0.125
- w_out: bfloat16 [2048, 2048], P('cols', 'rows'), may hold values from -0.125 to 0.125
- w_gate: bfloat16 [2048, 8192], P('rows', 'cols'), may hold values from -0.125 to 0.125
- w_up: bfloat16 [2048, 8192], P('rows', 'cols'), may hold values from -0.125 to 0.125
- w_down: bfloat16 [8192, 2048], P('cols', 'rows'), may hold values from -0.0625 to 0.0625
- q_gain: float32 [2048], P('cols'), may hold values from 0.1 to 1.9
- k_gain: float32 [2048], P('cols'), may hold values from 0.1 to 1.9
- attn_gain: float32 [2048], P('cols'), may hold values from 0.1 to 1.9
- ffn_gain: float32 [2048], P('cols'), may hold values from 0.1 to 1.9
- out_grad: bfloat16 [8192, 2048], P('rows', 'cols'), may hold values from -6 to 6
Outputs:
- layer_out: bfloat16 [8192, 2048], P('rows', 'cols')
- input_grad: bfloat16 [8192, 2048], P('rows', 'cols')
- grad_query: float32 [2048, 2048], P('rows', 'cols')
- grad_key: float32 [2048, 2048], P('rows', 'cols')
- grad_value: float32 [2048, 2048], P('rows', 'cols')
- grad_out: float32 [2048, 2048], P('cols', 'rows')
- grad_gate: float32 [2048, 8192], P('rows', 'cols')
- grad_up: float32 [2048, 8192], P('rows', 'cols')
- grad_down: float32 [8192, 2048], P('cols', 'rows')
- grad_q_gain: float32 [2048], P('cols')
- grad_k_gain: float32 [2048], P('cols')
- grad_attn_gain: float32 [2048], P('cols')
- grad_ffn_gain: float32 [2048], P('cols')
Inputs may be any that keep to these rules, and one draw needn't show every extreme that they name: `segment_ids`: within a sequence the ids never fall; every id from 0 to 7 is used and names 1 to 1024 consecutive tokens.
All inputs are finite; a program needn't handle non-finite values.
Results may differ from a plain program's by a relative error of at most 0.019.
Values may be sent and summed in bfloat16 or wider, within the bound.
No kernel may reach another device: no remote copies, remote signals or barrier semaphores. Data moves between devices by JAX's collectives and lax.ppermute only.
A program may use at most 256 MiB of HBM per device.

v0:
```python
import jax
import jax.numpy as jnp
from jax import lax
from jax.sharding import PartitionSpec as P

D = 2048
HEAD_DIM = 128


EPS = 1e-06
THETA = 500000.0
MASKED = -1e30


def rotation(length, width):
    halfway = width // 2
    rates = THETA ** (-2.0 * jnp.arange(halfway, dtype=jnp.float32) / width)
    angles = jnp.arange(length, dtype=jnp.float32)[:, None] * rates[None, :]
    return (jnp.cos(angles)[:, None, :], jnp.sin(angles)[:, None, :])


def rotate(values, cosine, sine_part, turning):
    halfway = values.shape[-1] // 2
    former = values[..., :halfway]
    latter = values[..., halfway:]
    return jnp.concatenate(
        [
            former * cosine - turning * latter * sine_part,
            latter * cosine + turning * former * sine_part,
        ],
        axis=-1,
    )


def spread_features(values):
    return lax.all_gather(values, "cols", axis=1, tiled=True)


def reduce_features(values):
    return lax.psum_scatter(values, "cols", scatter_dimension=1, tiled=True)


def token_totals(stacked):
    return lax.psum(stacked, "cols")


def attention_weights(w_query, w_key, w_value, w_out):
    return (
        lax.all_gather(w_query, "rows", axis=0, tiled=True),
        lax.all_gather(w_key, "rows", axis=0, tiled=True),
        lax.all_gather(w_value, "rows", axis=0, tiled=True),
        lax.all_gather(w_out, "rows", axis=1, tiled=True),
    )


def feedforward_weights(w_gate, w_up, w_down):
    return (
        lax.all_gather(w_gate, "rows", axis=0, tiled=True),
        lax.all_gather(w_up, "rows", axis=0, tiled=True),
        lax.all_gather(w_down, "rows", axis=1, tiled=True),
    )


def allowed_mask(segment, offset, reach, block_rows):
    query_seg = segment[offset:reach]
    key_seg = segment[:reach]
    query_pos = offset + jnp.arange(block_rows, dtype=jnp.int32)
    key_pos = jnp.arange(reach, dtype=jnp.int32)
    return (query_seg[:, None] == key_seg[None, :]) & (key_pos[None, :] <= query_pos[:, None])


def forward_block(queries, keys_here, values_here, allowed):
    scores = jnp.einsum("qhd,khd->hqk", queries, keys_here, preferred_element_type=jnp.float32)
    scores = jnp.where(allowed[None], scores, MASKED)
    row_max = jnp.max(scores, axis=-1, keepdims=True)
    weights = jnp.exp(scores - row_max)
    totals = jnp.sum(weights, axis=-1, keepdims=True)
    attended = jnp.einsum(
        "hqk,khd->qhd",
        (weights / totals).astype(jnp.bfloat16),
        values_here,
        preferred_element_type=jnp.float32,
    )
    return (attended, row_max + jnp.log(totals))


def backward_block(queries, keys_here, values_here, allowed, log_total, grads_here):
    scores = jnp.einsum("qhd,khd->hqk", queries, keys_here, preferred_element_type=jnp.float32)
    weights = jnp.where(allowed[None], jnp.exp(scores - log_total), 0.0)
    weight_back = jnp.einsum(
        "qhd,khd->hqk", grads_here, values_here, preferred_element_type=jnp.float32
    )
    delta = jnp.sum(weights * weight_back, axis=-1, keepdims=True)
    score_back = (weights * (weight_back - delta)).astype(jnp.bfloat16)
    query_grad = jnp.einsum(
        "hqk,khd->qhd", score_back, keys_here, preferred_element_type=jnp.float32
    )
    key_grad = jnp.einsum("hqk,qhd->khd", score_back, queries, preferred_element_type=jnp.float32)
    value_grad = jnp.einsum(
        "hqk,qhd->khd", weights.astype(jnp.bfloat16), grads_here, preferred_element_type=jnp.float32
    )
    return (query_grad, key_grad, value_grad)


def norm_back(cot_hat, raw, scale_rows, gain, total):
    return scale_rows * (cot_hat * gain) - raw * scale_rows**3 * (total[:, None] / D)


def per_device(
    tokens,
    segment_ids,
    w_query,
    w_key,
    w_value,
    w_out,
    w_gate,
    w_up,
    w_down,
    q_gain,
    k_gain,
    attn_gain,
    ffn_gain,
    out_grad,
):
    seq_count, seq_len = segment_ids.shape
    token_rows = tokens.shape[0]
    local = tokens.shape[1]
    heads_here = local // HEAD_DIM
    scale = HEAD_DIM ** (-0.5)
    block_rows = min(512, seq_len)
    block_count = seq_len // block_rows
    cosine, sine_part = rotation(seq_len, HEAD_DIM)
    shaped = (seq_count, seq_len, heads_here, HEAD_DIM)
    tokens_wide = spread_features(tokens)
    full_query, full_key, full_value, full_out = attention_weights(w_query, w_key, w_value, w_out)
    query_raw = jnp.dot(tokens_wide, full_query, preferred_element_type=jnp.float32)
    key_raw = jnp.dot(tokens_wide, full_key, preferred_element_type=jnp.float32)
    value_low = jnp.dot(tokens_wide, full_value, preferred_element_type=jnp.float32).astype(
        jnp.bfloat16
    )
    qk_stats = token_totals(
        jnp.stack([jnp.sum(query_raw * query_raw, axis=1), jnp.sum(key_raw * key_raw, axis=1)])
    )
    query_scale = lax.rsqrt(qk_stats[0] / D + EPS)[:, None]
    key_scale = lax.rsqrt(qk_stats[1] / D + EPS)[:, None]
    query_low = (
        rotate((query_raw * query_scale * q_gain).reshape(shaped), cosine, sine_part, 1.0) * scale
    ).astype(jnp.bfloat16)
    key_low = rotate((key_raw * key_scale * k_gain).reshape(shaped), cosine, sine_part, 1.0).astype(
        jnp.bfloat16
    )
    value_seq = value_low.reshape(shaped)
    sequence = 0
    pieces = []
    lse_pieces = []
    for index in range(block_count):
        offset = index * block_rows
        reach = offset + block_rows
        allowed = allowed_mask(segment_ids[sequence], offset, reach, block_rows)
        attended, log_total = forward_block(
            query_low[sequence, offset:reach],
            key_low[sequence, :reach],
            value_seq[sequence, :reach],
            allowed,
        )
        pieces.append(attended)
        lse_pieces.append(log_total)
    attended_all = [jnp.concatenate(pieces, axis=0)]
    log_totals = [lse_pieces]
    attn_low = jnp.stack(attended_all).reshape(token_rows, local).astype(jnp.bfloat16)
    attn_sum = reduce_features(jnp.dot(attn_low, full_out, preferred_element_type=jnp.float32))
    attn_stats = token_totals(jnp.stack([jnp.sum(attn_sum * attn_sum, axis=1)]))
    attn_scale = lax.rsqrt(attn_stats[0] / D + EPS)[:, None]
    hidden = tokens.astype(jnp.float32) + attn_sum * attn_scale * attn_gain
    hidden_wide = spread_features(hidden.astype(jnp.bfloat16))
    full_gate, full_up, full_down = feedforward_weights(w_gate, w_up, w_down)
    gate = jnp.dot(hidden_wide, full_gate, preferred_element_type=jnp.float32)
    upward = jnp.dot(hidden_wide, full_up, preferred_element_type=jnp.float32)
    gate_sig = jax.nn.sigmoid(gate)
    mixed_low = (gate * gate_sig * upward).astype(jnp.bfloat16)
    ffn_sum = reduce_features(jnp.dot(mixed_low, full_down, preferred_element_type=jnp.float32))
    ffn_stats = token_totals(jnp.stack([jnp.sum(ffn_sum * ffn_sum, axis=1)]))
    ffn_scale = lax.rsqrt(ffn_stats[0] / D + EPS)[:, None]
    layer_out = (hidden + ffn_sum * ffn_scale * ffn_gain).astype(jnp.bfloat16)
    out_cot = out_grad.astype(jnp.float32)
    grad_ffn_gain = jnp.sum(out_cot * ffn_sum * ffn_scale, axis=0)
    ffn_total = token_totals(jnp.stack([jnp.sum(out_cot * ffn_gain * ffn_sum, axis=1)]))
    ffn_back = norm_back(out_cot, ffn_sum, ffn_scale, ffn_gain, ffn_total[0]).astype(jnp.bfloat16)
    ffn_back_wide = spread_features(ffn_back)
    back_gate, back_up, back_down = feedforward_weights(w_gate, w_up, w_down)
    mixed_back = jnp.einsum(
        "td,fd->tf", ffn_back_wide, back_down, preferred_element_type=jnp.float32
    )
    grad_down = jnp.einsum(
        "tf,td->fd", mixed_low, ffn_back_wide, preferred_element_type=jnp.float32
    )
    gate_back = (mixed_back * upward * gate_sig * (1.0 + gate * (1.0 - gate_sig))).astype(
        jnp.bfloat16
    )
    up_back = (mixed_back * gate * gate_sig).astype(jnp.bfloat16)
    hidden_terms = jnp.einsum(
        "tf,df->td", gate_back, back_gate, preferred_element_type=jnp.float32
    ) + jnp.einsum("tf,df->td", up_back, back_up, preferred_element_type=jnp.float32)
    grad_gate = jnp.einsum("td,tf->df", hidden_wide, gate_back, preferred_element_type=jnp.float32)
    grad_up = jnp.einsum("td,tf->df", hidden_wide, up_back, preferred_element_type=jnp.float32)
    grad_gate, grad_up, grad_down = (
        lax.psum_scatter(
            grad_gate.astype(jnp.bfloat16), "rows", scatter_dimension=0, tiled=True
        ).astype(jnp.float32),
        lax.psum_scatter(
            grad_up.astype(jnp.bfloat16), "rows", scatter_dimension=0, tiled=True
        ).astype(jnp.float32),
        lax.psum_scatter(
            grad_down.astype(jnp.bfloat16), "rows", scatter_dimension=1, tiled=True
        ).astype(jnp.float32),
    )
    hidden_cot = out_cot + reduce_features(hidden_terms)
    grad_attn_gain = jnp.sum(hidden_cot * attn_sum * attn_scale, axis=0)
    attn_total = token_totals(jnp.stack([jnp.sum(hidden_cot * attn_gain * attn_sum, axis=1)]))
    attn_back = norm_back(hidden_cot, attn_sum, attn_scale, attn_gain, attn_total[0]).astype(
        jnp.bfloat16
    )
    attn_back_wide = spread_features(attn_back)
    back_query, back_key, back_value, back_out = attention_weights(w_query, w_key, w_value, w_out)
    out_back = jnp.einsum(
        "td,ld->tl", attn_back_wide, back_out, preferred_element_type=jnp.float32
    ).astype(jnp.bfloat16)
    grad_out = jnp.einsum("tl,td->ld", attn_low, attn_back_wide, preferred_element_type=jnp.float32)
    out_back_seq = out_back.reshape(shaped)
    sequence = 0
    query_pieces = []
    key_accum = jnp.zeros((seq_len, heads_here, HEAD_DIM), jnp.float32)
    value_accum = jnp.zeros((seq_len, heads_here, HEAD_DIM), jnp.float32)
    for index in range(block_count):
        offset = index * block_rows
        reach = offset + block_rows
        allowed = allowed_mask(segment_ids[sequence], offset, reach, block_rows)
        query_part, key_part, value_part = backward_block(
            query_low[sequence, offset:reach],
            key_low[sequence, :reach],
            value_seq[sequence, :reach],
            allowed,
            log_totals[sequence][index],
            out_back_seq[sequence, offset:reach],
        )
        query_pieces.append(query_part)
        key_accum = key_accum.at[:reach].add(key_part)
        value_accum = value_accum.at[:reach].add(value_part)
    query_grads = [jnp.concatenate(query_pieces, axis=0)]
    key_grads = [key_accum]
    value_grads = [value_accum]
    query_hat = rotate(jnp.stack(query_grads) * scale, cosine, sine_part, -1.0).reshape(
        token_rows, local
    )
    key_hat = rotate(jnp.stack(key_grads), cosine, sine_part, -1.0).reshape(token_rows, local)
    value_back = jnp.stack(value_grads).reshape(token_rows, local).astype(jnp.bfloat16)
    grad_q_gain = jnp.sum(query_hat * query_raw * query_scale, axis=0)
    grad_k_gain = jnp.sum(key_hat * key_raw * key_scale, axis=0)
    qk_totals = token_totals(
        jnp.stack(
            [
                jnp.sum(query_hat * q_gain * query_raw, axis=1),
                jnp.sum(key_hat * k_gain * key_raw, axis=1),
            ]
        )
    )
    query_back = norm_back(query_hat, query_raw, query_scale, q_gain, qk_totals[0]).astype(
        jnp.bfloat16
    )
    key_back = norm_back(key_hat, key_raw, key_scale, k_gain, qk_totals[1]).astype(jnp.bfloat16)
    input_terms = (
        jnp.einsum("tl,dl->td", query_back, back_query, preferred_element_type=jnp.float32)
        + jnp.einsum("tl,dl->td", key_back, back_key, preferred_element_type=jnp.float32)
        + jnp.einsum("tl,dl->td", value_back, back_value, preferred_element_type=jnp.float32)
    )
    grad_query = jnp.einsum(
        "td,tl->dl", tokens_wide, query_back, preferred_element_type=jnp.float32
    )
    grad_key = jnp.einsum("td,tl->dl", tokens_wide, key_back, preferred_element_type=jnp.float32)
    grad_value = jnp.einsum(
        "td,tl->dl", tokens_wide, value_back, preferred_element_type=jnp.float32
    )
    grad_query, grad_key, grad_value, grad_out = (
        lax.psum_scatter(
            grad_query.astype(jnp.bfloat16), "rows", scatter_dimension=0, tiled=True
        ).astype(jnp.float32),
        lax.psum_scatter(
            grad_key.astype(jnp.bfloat16), "rows", scatter_dimension=0, tiled=True
        ).astype(jnp.float32),
        lax.psum_scatter(
            grad_value.astype(jnp.bfloat16), "rows", scatter_dimension=0, tiled=True
        ).astype(jnp.float32),
        lax.psum_scatter(
            grad_out.astype(jnp.bfloat16), "rows", scatter_dimension=1, tiled=True
        ).astype(jnp.float32),
    )
    input_grad = (hidden_cot + reduce_features(input_terms)).astype(jnp.bfloat16)
    grad_q_gain, grad_k_gain, grad_attn_gain, grad_ffn_gain = lax.psum(
        (grad_q_gain, grad_k_gain, grad_attn_gain, grad_ffn_gain), "rows"
    )
    return (
        layer_out,
        input_grad,
        grad_query,
        grad_key,
        grad_value,
        grad_out,
        grad_gate,
        grad_up,
        grad_down,
        grad_q_gain,
        grad_k_gain,
        grad_attn_gain,
        grad_ffn_gain,
    )


def solution(mesh):
    in_specs = (
        P("rows", "cols"),
        P("rows", None),
        P("rows", "cols"),
        P("rows", "cols"),
        P("rows", "cols"),
        P("cols", "rows"),
        P("rows", "cols"),
        P("rows", "cols"),
        P("cols", "rows"),
        P("cols"),
        P("cols"),
        P("cols"),
        P("cols"),
        P("rows", "cols"),
    )
    out_specs = (
        P("rows", "cols"),
        P("rows", "cols"),
        P("rows", "cols"),
        P("rows", "cols"),
        P("rows", "cols"),
        P("cols", "rows"),
        P("rows", "cols"),
        P("rows", "cols"),
        P("cols", "rows"),
        P("cols"),
        P("cols"),
        P("cols"),
        P("cols"),
    )
    return jax.shard_map(
        per_device, mesh=mesh, in_specs=in_specs, out_specs=out_specs, check_vma=False
    )
```

profile of v0, /device:TPU:0, one launch (start us, length us, event | category | flops | bytes accessed | tf_op | source)
XLA Modules:
  0.0 2292.2 jit_solution(7996972238807542942)
XLA Ops:
  10.7 5.1 broadcast_multiply_fusion
  20.3 8.7 all-gather.16.cloned.1.call-done
  29.0 127.5 %all-gather.12.cloned.1.call-done = bf16[2048,2048]{1,0:T(8,128)(2,1)} async-done(((bf16[2048,256]{1,0:T(8,128)(2,1)}), bf16[2048,2048]{1,0:T(8,128)(2,1)}) %all-gather.12.cloned.1.call-update) | async-done | bytes 8388624 | tf_op jit(solution)/shard_map/all_gather | solution.py:36
  156.6 6.0 multiply_reduce_fusion.11
  162.6 10.4 all-gather.18.cloned.1.call-done
  173.1 7.3 multiply_reduce_fusion.10
  180.4 37.6 %psum.70 = f32[2,2048]{1,0:T(2,128)S(1)} all-reduce(f32[2,2048]{1,0:T(2,128)S(1)} %pad_maximum_fusion.7), channel_id=1, replica_groups=mesh['rows'=4,'cols'=8] {'cols'}, use_global_device_ids=true, to_apply=%region_2.0 | all-reduce | flops 4096 | bytes 32768 | tf_op jit(solution)/shard_map/psum | solution.py:44
  229.3 5.1 subtract_convert_fusion.3
  243.1 6.0 convolution_convert_fusion.8
  270.0 9.9 fusion.124
  280.7 278.3 %reduce-scatter.12.cloned.1.call-done = f32[2048,256]{1,0:T(8,128)} async-done(((f32[2048,2048]{1,0:T(8,128)}), f32[2048,256]{1,0:T(8,128)}) %reduce-scatter.12.cloned.1.call-update) | async-done | bytes 2097168 | tf_op jit(solution)/shard_map/reduce_scatter | solution.py:40
  561.1 20.0 psum.71
  583.9 10.3 all-gather.24.cloned.1.call-done
  594.2 128.2 %all-gather.22.cloned.1.call-done = bf16[2048,2048]{1,0:T(8,128)(2,1)} async-done(((bf16[2048,256]{1,0:T(8,128)(2,1)}), bf16[2048,2048]{1,0:T(8,128)(2,1)}) %all-gather.22.cloned.1.call-update) | async-done | bytes 8388624 | tf_op jit(solution)/shard_map/all_gather | solution.py:36
  722.5 14.4 fusion.125
  736.9 19.9 all-gather.26.cloned.1.call-done
  756.8 16.9 multiply_convert_fusion.3
  773.8 19.1 all-gather.28.cloned.1.call-done
  792.8 15.1 fusion.126
  808.0 282.8 %reduce-scatter.14.cloned.1.call-done = f32[2048,256]{1,0:T(8,128)} async-done(((f32[2048,2048]{1,0:T(8,128)}), f32[2048,256]{1,0:T(8,128)}) %reduce-scatter.14.cloned.1.call-update) | async-done | bytes 2097168 | tf_op jit(solution)/shard_map/reduce_scatter | solution.py:40
  1092.8 20.1 psum.72
  1116.0 17.4 psum.73
  1136.5 124.1 %all-gather.30.cloned.1.call-done = bf16[2048,2048]{1,0:T(8,128)(2,1)} async-done(((bf16[2048,256]{1,0:T(8,128)(2,1)}), bf16[2048,2048]{1,0:T(8,128)(2,1)}) %all-gather.30.cloned.1.call-update) | async-done | bytes 8388624 | tf_op jit(solution)/shard_map/all_gather | solution.py:36
  1260.6 22.0 multiply_convert_fusion.1
  1282.6 14.0 fusion.127
  1296.6 17.9 convolution_add_fusion
  1314.6 281.0 %reduce-scatter.16.cloned.1.call-done = f32[2048,256]{1,0:T(8,128)} async-done(((f32[2048,2048]{1,0:T(8,128)}), f32[2048,256]{1,0:T(8,128)}) %reduce-scatter.16.cloned.1.call-update) | async-done | bytes 2097168 | tf_op jit(solution)/shard_map/reduce_scatter | solution.py:40
  1598.5 19.7 psum.74
  1618.3 5.3 subtract_convert_fusion.2
  1623.6 14.1 convolution_convert_fusion
  1637.8 14.2 convolution_convert_fusion.2
  1652.8 14.1 convolution_convert_fusion.1
  1667.3 79.0 %all-gather.32.cloned.1.call-done = bf16[2048,2048]{1,0:T(8,128)(2,1)} async-done(((bf16[2048,256]{1,0:T(8,128)(2,1)}), bf16[2048,2048]{1,0:T(8,128)(2,1)}) %all-gather.32.cloned.1.call-update) | async-done | bytes 8388624 | tf_op jit(solution)/shard_map/all_gather | solution.py:36
  1746.3 5.7 convolution_convert_fusion.7
  1757.7 4.6 multiply_reduce_fusion.1
  1775.4 4.0 multiply_reduce_fusion
  1793.2 4.7 pad_maximum_fusion
  1824.0 34.5 %psum.75 = f32[2,2048]{1,0:T(2,128)S(1)} all-reduce(f32[2,2048]{1,0:T(2,128)S(1)} %pad_maximum_fusion.8), channel_id=1, replica_groups=mesh['rows'=4,'cols'=8] {'cols'}, use_global_device_ids=true, to_apply=%region_28.29 | all-reduce | flops 4096 | bytes 32768 | tf_op jit(solution)/shard_map/psum | solution.py:44
  1861.1 6.8 fusion.45
  1871.4 6.9 fusion.44
  1878.4 6.8 convolution_convert_fusion.3
  1885.3 9.7 fusion.129
  1895.0 8.2 fusion.128
  1903.3 18.5 add_add_fusion
  1930.4 7.0 all-reduce.2
  1942.5 25.3 %reduce-scatter.20.cloned.1.call-done = bf16[512,256]{0,1:T(8,128)(2,1)} async-done(((bf16[2048,256]{0,1:T(8,128)(2,1)}), bf16[512,256]{0,1:T(8,128)(2,1)}) %reduce-scatter.20.cloned.1.call-update) | async-done | bytes 262160 | tf_op jit(solution)/shard_map/reduce_scatter | solution.py:284
  1969.7 25.7 %reduce-scatter.26.cloned.1.call-done = bf16[256,512]{1,0:T(8,128)(2,1)} async-done(((bf16[256,2048]{1,0:T(8,128)(2,1)}), bf16[256,512]{1,0:T(8,128)(2,1)}) %reduce-scatter.26.cloned.1.call-update) | async-done | bytes 262160 | tf_op jit(solution)/shard_map/reduce_scatter | solution.py:293
  1997.2 284.8 %reduce-scatter.18.cloned.1.call-done = f32[2048,256]{1,0:T(8,128)} async-done(((f32[2048,2048]{1,0:T(8,128)}), f32[2048,256]{1,0:T(8,128)}) %reduce-scatter.18.cloned.1.call-update) | async-done | bytes 2097168 | tf_op jit(solution)/shard_map/reduce_scatter | solution.py:40
  (346 shorter events, 151.0 us)
Async XLA Ops:
  7.2 21.8 all-gather.16.cloned.1.call-start
  7.9 148.6 %all-gather.12.cloned.1.call-start = ((), (), s32[]{:S(2)}) async-start(), calls=%async_computation.11 | async-start | bytes 9437184 | tf_op jit(solution)/shard_map/all_gather | solution.py:36
  8.7 164.4 %all-gather.18.cloned.1.call-start = ((), (), s32[]{:S(2)}) async-start(), calls=%async_computation.14 | async-start | bytes 1310720 | tf_op jit(solution)/shard_map/all_gather | solution.py:50
  9.4 233.7 %all-gather.14.cloned.1.call-start = ((), (), s32[]{:S(2)}) async-start(), calls=%async_computation.12 | async-start | bytes 1310720 | tf_op jit(solution)/shard_map/all_gather | solution.py:51
  10.0 260.0 %all-gather.20.cloned.1.call-start = ((), (), s32[]{:S(2)}) async-start(), calls=%async_computation.15 | async-start | bytes 1310720 | tf_op jit(solution)/shard_map/all_gather | solution.py:52
  10.6 548.4 %reduce-scatter.12.cloned.1.call-start = ((), (), s32[]{:S(2)}) async-start(), calls=%async_computation.16 | async-start | bytes 18874368 | tf_op jit(solution)/shard_map/reduce_scatter | solution.py:40
  16.0 233.1 %copy-start.39 = (pred[512,512]{0,1:T(8,128)(4,1)}, pred[512,512]{0,1:T(8,128)(4,1)S(1)}, u32[]{:S(2)}) copy-start(pred[512,512]{0,1:T(8,128)(4,1)S(1)} %fusion.90) | copy-start | bytes 786436
  20.3 246.0 %copy-start.5 = (pred[512,2048]{1,0:T(8,128)(4,1)}, pred[512,2048]{1,0:T(8,128)(4,1)S(1)}, u32[]{:S(2)}) copy-start(pred[512,2048]{1,0:T(8,128)(4,1)S(1)} %fusion.7) | copy-start | bytes 3145732
  162.6 55.4 %copy-start.24 = (f32[2048,256]{0,1:T(8,128)}, f32[2048,256]{0,1:T(8,128)S(1)}, u32[]{:S(2)}) copy-start(f32[2048,256]{0,1:T(8,128)S(1)} %get-tuple-element.184) | copy-start | bytes 6291460
  162.6 55.4 %copy-start.83 = (f32[256]{0:T(256)S(1)}, f32[256]{0:T(256)}, u32[]{:S(2)}) copy-start(f32[256]{0:T(256)} %param.43) | copy-start | bytes 3076
  234.5 27.3 %copy-start.7 = (bf16[1,2048,2,64]{3,1,2,0:T(8,128)(2,1)}, bf16[1,2048,2,64]{3,1,2,0:T(8,128)(2,1)S(1)}, u32[]{:S(2)}) copy-start(bf16[1,2048,2,64]{3,1,2,0:T(8,128)(2,1)S(1)} %get-tuple-element.152) | copy-start | bytes 1572868
  234.5 27.3 %copy-start.9 = (bf16[1,2048,2,64]{3,1,2,0:T(8,128)(2,1)}, bf16[1,2048,2,64]{3,1,2,0:T(8,128)(2,1)S(1)}, u32[]{:S(2)}) copy-start(bf16[1,2048,2,64]{3,1,2,0:T(8,128)(2,1)S(1)} %get-tuple-element.153) | copy-start | bytes 1572868
  239.2 14.3 copy-start.63
  249.1 17.3 copy-start.36
  269.9 9.9 copy-start.44
  279.8 301.3 %copy-start.31 = (bf16[2048,256]{1,0:T(8,128)(2,1)S(1)}, bf16[2048,256]{1,0:T(8,128)(2,1)}, u32[]{:S(2)}) copy-start(bf16[2048,256]{1,0:T(8,128)(2,1)} %param.34) | copy-start | bytes 3145732
  279.9 301.3 %copy-start.79 = (f32[256]{0:T(256)S(1)}, f32[256]{0:T(256)}, u32[]{:S(2)}) copy-start(f32[256]{0:T(256)} %param.45) | copy-start | bytes 3076
  279.9 314.4 %all-gather.24.cloned.1.call-start = ((), (), s32[]{:S(2)}) async-start(), calls=%async_computation.18 | async-start | bytes 5242880 | tf_op jit(solution)/shard_map/all_gather | solution.py:58
  280.6 441.9 %all-gather.22.cloned.1.call-start = ((), (), s32[]{:S(2)}) async-start(), calls=%async_computation.17 | async-start | bytes 9437184 | tf_op jit(solution)/shard_map/all_gather | solution.py:36
  559.0 22.1 copy-start.11
  582.6 174.3 %all-gather.26.cloned.1.call-start = ((), (), s32[]{:S(2)}) async-start(), calls=%async_computation.19 | async-start | bytes 5242880 | tf_op jit(solution)/shard_map/all_gather | solution.py:59
  583.3 209.5 %all-gather.28.cloned.1.call-start = ((), (), s32[]{:S(2)}) async-start(), calls=%async_computation.20 | async-start | bytes 5242880 | tf_op jit(solution)/shard_map/all_gather | solution.py:60
  583.9 507.0 %reduce-scatter.14.cloned.1.call-start = ((), (), s32[]{:S(2)}) async-start(), calls=%async_computation.21 | async-start | bytes 18874368 | tf_op jit(solution)/shard_map/reduce_scatter | solution.py:40
  808.0 305.0 %copy-start.17 = (bf16[2048,256]{1,0:T(8,128)(2,1)S(1)}, bf16[2048,256]{1,0:T(8,128)(2,1)}, u32[]{:S(2)}) copy-start(bf16[2048,256]{1,0:T(8,128)(2,1)} %param.47) | copy-start | bytes 3145732
  808.0 305.0 %copy-start.80 = (f32[256]{0:T(256)S(1)}, f32[256]{0:T(256)}, u32[]{:S(2)}) copy-start(f32[256]{0:T(256)} %param.46) | copy-start | bytes 3076
  808.0 452.6 %all-gather.30.cloned.1.call-start = ((), (), s32[]{:S(2)}) async-start(), calls=%async_computation.22 | async-start | bytes 9437184 | tf_op jit(solution)/shard_map/all_gather | solution.py:36
  1136.4 459.2 %reduce-scatter.16.cloned.1.call-start = ((), (), s32[]{:S(2)}) async-start(), calls=%async_computation.23 | async-start | bytes 18874368 | tf_op jit(solution)/shard_map/reduce_scatter | solution.py:40
  1260.6 22.0 copy-start.87
  1314.6 431.8 %all-gather.32.cloned.1.call-start = ((), (), s32[]{:S(2)}) async-start(), calls=%async_computation.24 | async-start | bytes 9437184 | tf_op jit(solution)/shard_map/all_gather | solution.py:36
  1623.6 298.3 %reduce-scatter.32.cloned.1.call-start = ((), (), s32[]{:S(2)}) async-start(), calls=%async_computation.32 | async-start | bytes 5242880 | tf_op jit(solution)/shard_map/reduce_scatter | solution.py:213
  1637.7 287.0 %reduce-scatter.28.cloned.1.call-start = ((), (), s32[]{:S(2)}) async-start(), calls=%async_computation.30 | async-start | bytes 5242880 | tf_op jit(solution)/shard_map/reduce_scatter | solution.py:207
  1652.1 275.5 %reduce-scatter.30.cloned.1.call-start = ((), (), s32[]{:S(2)}) async-start(), calls=%async_computation.31 | async-start | bytes 5242880 | tf_op jit(solution)/shard_map/reduce_scatter | solution.py:210
  1666.8 79.5 %copy-start.57 = (bf16[256,2048]{1,0:T(8,128)(2,1)S(1)}, bf16[256,2048]{1,0:T(8,128)(2,1)}, u32[]{:S(2)}) copy-start(bf16[256,2048]{1,0:T(8,128)(2,1)} %all-gather.20.cloned.1.call-done) | copy-start | bytes 3145732
  1666.9 85.2 %copy-start.37 = (bf16[2048,256]{0,1:T(8,128)(2,1)S(1)}, bf16[2048,256]{0,1:T(8,128)(2,1)}, u32[]{:S(2)}) copy-start(bf16[2048,256]{0,1:T(8,128)(2,1)} %copy-done.36) | copy-start | bytes 3145732
  1666.9 85.2 %copy-start.40 = (pred[512,512]{0,1:T(8,128)(4,1)S(1)}, pred[512,512]{0,1:T(8,128)(4,1)}, u32[]{:S(2)}) copy-start(pred[512,512]{0,1:T(8,128)(4,1)} %copy-done.39) | copy-start | bytes 786436
  1666.9 270.4 %reduce-scatter.24.cloned.1.call-start = ((), (), s32[]{:S(2)}) async-start(), calls=%async_computation.28 | async-start | bytes 1310720 | tf_op jit(solution)/shard_map/reduce_scatter | solution.py:290
  1757.7 9.6 slice-start.4
  1766.0 9.4 slice-start
  1800.9 10.6 slice-start.6
  1821.8 118.9 %reduce-scatter.22.cloned.1.call-start = ((), (), s32[]{:S(2)}) async-start(), calls=%async_computation.27 | async-start | bytes 1310720 | tf_op jit(solution)/shard_map/reduce_scatter | solution.py:287
  1867.9 99.9 %reduce-scatter.20.cloned.1.call-start = ((), (), s32[]{:S(2)}) async-start(), calls=%async_computation.26 | async-start | bytes 1310720 | tf_op jit(solution)/shard_map/reduce_scatter | solution.py:284
  1878.4 117.0 %reduce-scatter.26.cloned.1.call-start = ((), (), s32[]{:S(2)}) async-start(), calls=%async_computation.29 | async-start | bytes 1310720 | tf_op jit(solution)/shard_map/reduce_scatter | solution.py:293
  1885.2 9.8 copy-start.47
  1885.3 396.7 %reduce-scatter.18.cloned.1.call-start = ((), (), s32[]{:S(2)}) async-start(), calls=%async_computation.25 | async-start | bytes 18874368 | tf_op jit(solution)/shard_map/reduce_scatter | solution.py:40
  1885.3 9.7 copy-start.55
  1895.0 8.3 copy-start.56
  1930.3 351.7 %copy-start.18 = (bf16[2048,256]{1,0:T(8,128)(2,1)S(1)}, bf16[2048,256]{1,0:T(8,128)(2,1)}, u32[]{:S(2)}) copy-start(bf16[2048,256]{1,0:T(8,128)(2,1)} %param.47) | copy-start | bytes 3145732
  1930.3 351.7 %copy-start.23 = (f32[2048,256]{1,0:T(8,128)S(1)}, f32[2048,256]{1,0:T(8,128)}, u32[]{:S(2)}) copy-start(f32[2048,256]{1,0:T(8,128)} %reduce-scatter.16.cloned.1.call-done) | copy-start | bytes 6291460
  (73 other events, 224.9 us)
Sparse Core Ops, SparseCore 0:
  9.6 19.4 all-gather.15
  31.1 125.4 all-gather.11
  158.1 14.8 all-gather.17
  174.5 16.7 all-gather.13
  192.7 16.7 all-gather.19
  280.0 278.9 reduce-scatter.11
  560.6 33.5 all-gather.23
  597.0 125.3 all-gather.21
  724.1 32.6 all-gather.25
  758.3 34.4 all-gather.27
  808.1 282.7 reduce-scatter.13
  1136.5 124.0 all-gather.29
  1314.7 280.8 reduce-scatter.15
  1623.7 122.6 all-gather.31
  1748.9 42.6 reduce-scatter.31
  1794.0 44.4 reduce-scatter.27
  1841.1 44.4 reduce-scatter.29
  1888.0 24.8 reduce-scatter.23
  1915.6 25.0 reduce-scatter.21
  1943.0 24.7 reduce-scatter.19
  1970.5 24.8 reduce-scatter.25
  1999.2 282.7 reduce-scatter.17
where the time goes:
time: 2300 us; the launch traced here: 2290 us
  waiting for transfers between devices  1710 us (74%)
  matrix products  289 us (13%)
  blocking collectives  156 us (7%)
  other arithmetic  80.7 us (4%)
  local copies, waits for them, and re-layouts  36.2 us (2%)
    reduce_scatter x4, waiting for transfers between devices, reduce_features(): return lax.psum_scatter(values, 'cols', scatter_dimension=1, tiled=True)  1130 us
    all_gather x4, waiting for transfers between devices, spread_features(): return lax.all_gather(values, 'cols', axis=1, tiled=True)  459 us
    psum x6, blocking collectives, token_totals(): return lax.psum(stacked, 'cols')  149 us
  transfers between devices with their start and end apart: 22, of which 16 were waited for; matrix products, arithmetic and copies ran while one was open for 13% of the time, Pallas kernels for 0%

commit v1 on v0

v1 whole, which is shorter than its diff:
```python
import functools

import jax
import jax.numpy as jnp
from jax import lax
from jax.experimental import pallas as pl
from jax.experimental.pallas import tpu as pltpu
from jax.sharding import PartitionSpec as P

HEAD_DIM = 128
EPS = 1e-06
THETA = 500000.0
MASKED = -1e30
LOW = jnp.bfloat16
WIDE = jnp.float32
CHUNKS = 4
DOCUMENTS = 8
VMEM = 52 * 2**20


def rotation(length, width):
    halfway = width // 2
    rates = THETA ** (-2.0 * jnp.arange(halfway, dtype=WIDE) / width)
    angles = jnp.arange(length, dtype=WIDE)[:, None] * rates[None, :]
    cosine, sine_part = jnp.cos(angles), jnp.sin(angles)
    return (
        jnp.concatenate([cosine, cosine], axis=1),
        jnp.concatenate([-sine_part, sine_part], axis=1),
    )


def attend_kernel(first, block, lows, starts, query, key, value, out, log_total):
    index = pl.program_id(1)
    begin = (first + index) * block
    queries = query[...]
    start = starts[...]
    place = begin + lax.broadcasted_iota(jnp.int32, (1, block), 1)

    def body(step, carry):
        peak, total, held = carry
        rows = pl.ds(pl.multiple_of(step * block, block), block)
        scores = lax.dot_general(
            key[rows, :], queries, (((1,), (1,)), ((), ())), preferred_element_type=WIDE
        )
        key_place = step * block + lax.broadcasted_iota(jnp.int32, (block, 1), 0)
        scores = jnp.where((key_place >= start) & (key_place <= place), scores, MASKED)
        top = jnp.maximum(peak, jnp.max(scores, axis=0, keepdims=True))
        weights = jnp.exp(scores - top)
        fade = jnp.exp(peak - top)
        total = total * fade + jnp.sum(weights, axis=0, keepdims=True)
        held = held * fade + lax.dot_general(
            value[rows, :], weights.astype(LOW), (((0,), (0,)), ((), ())), preferred_element_type=WIDE
        )
        return (top, total, held)

    row = jnp.full((1, block), MASKED, WIDE)
    carry = (row, jnp.zeros((1, block), WIDE), jnp.zeros((HEAD_DIM, block), WIDE))
    peak, total, held = lax.fori_loop(lows[first + index], first + index + 1, body, carry)
    out[...] = (held / total).T.astype(LOW)
    log_total[0] = peak + jnp.log(total)


def attend(lows, starts, query, key, value, first, count, block):
    length, local = query.shape
    heads = local // HEAD_DIM
    rows = count * block
    own = pl.BlockSpec((block, HEAD_DIM), lambda h, i, _: (first + i, h))
    all_keys = pl.BlockSpec((length, HEAD_DIM), lambda h, i, _: (0, h))
    made = pl.BlockSpec((block, HEAD_DIM), lambda h, i, _: (i, h))
    return pl.pallas_call(
        functools.partial(attend_kernel, first, block),
        grid_spec=pltpu.PrefetchScalarGridSpec(
            num_scalar_prefetch=1,
            grid=(heads, count),
            in_specs=[pl.BlockSpec((1, block), lambda h, i, _: (0, first + i)), own, all_keys, all_keys],
            out_specs=[made, pl.BlockSpec((1, 1, block), lambda h, i, _: (h, 0, i))],
        ),
        out_shape=[
            jax.ShapeDtypeStruct((rows, local), LOW),
            jax.ShapeDtypeStruct((heads, 1, rows), WIDE),
        ],
        compiler_params=params(),
        cost_estimate=pl.CostEstimate(
            flops=8 * rows * 1024 * local, bytes_accessed=12 * length * local, transcendentals=0
        ),
    )(lows, starts, query, key, value)


def attend_back_kernel(
    block, lows, starts, query, key, value, log_total, out, grads, dquery, dkey, dvalue
):
    index = pl.program_id(1)
    begin = index * block
    queries, out_grads = query[...], grads[...]
    start = starts[...]
    place = begin + lax.broadcasted_iota(jnp.int32, (1, block), 1)
    lse = log_total[0]
    products = out_grads.astype(WIDE) * out[...].astype(WIDE)
    less = jnp.sum(products.T, axis=0, keepdims=True)

    @pl.when(index == 0)
    def _():
        dkey[...] = jnp.zeros_like(dkey)
        dvalue[...] = jnp.zeros_like(dvalue)

    def body(step, held):
        rows = pl.ds(pl.multiple_of(step * block, block), block)
        keys_here = key[rows, :]
        across = (((1,), (1,)), ((), ()))
        scores = lax.dot_general(keys_here, queries, across, preferred_element_type=WIDE)
        key_place = step * block + lax.broadcasted_iota(jnp.int32, (block, 1), 0)
        allowed = (key_place >= start) & (key_place <= place)
        weights = jnp.exp(jnp.where(allowed, scores - lse, MASKED))
        back = lax.dot_general(value[rows, :], out_grads, across, preferred_element_type=WIDE)
        score_back = (weights * (back - less)).astype(LOW)
        dvalue[rows, :] += jnp.dot(weights.astype(LOW), out_grads, preferred_element_type=WIDE)
        dkey[rows, :] += jnp.dot(score_back, queries, preferred_element_type=WIDE)
        return held + lax.dot_general(
            keys_here, score_back, (((0,), (0,)), ((), ())), preferred_element_type=WIDE
        )

    held = lax.fori_loop(lows[index], index + 1, body, jnp.zeros((HEAD_DIM, block), WIDE))
    dquery[...] = held.T


def attend_back(lows, starts, query, key, value, log_total, out, grads, block):
    length, local = query.shape
    heads = local // HEAD_DIM
    own = pl.BlockSpec((block, HEAD_DIM), lambda h, i, _: (i, h))
    full = pl.BlockSpec((length, HEAD_DIM), lambda h, i, _: (0, h))
    line = pl.BlockSpec((1, 1, block), lambda h, i, _: (h, 0, i))
    shape = jax.ShapeDtypeStruct((length, local), WIDE)
    return pl.pallas_call(
        functools.partial(attend_back_kernel, block),
        grid_spec=pltpu.PrefetchScalarGridSpec(
            num_scalar_prefetch=1,
            grid=(heads, length // block),
            in_specs=[
                pl.BlockSpec((1, block), lambda h, i, _: (0, i)),
                own,
                full,
                full,
                line,
                own,
                own,
            ],
            out_specs=[own, full, full],
        ),
        out_shape=[shape, shape, shape],
        compiler_params=params(),
        cost_estimate=pl.CostEstimate(
            flops=20 * length * 1024 * local, bytes_accessed=20 * length * local, transcendentals=0
        ),
    )(lows, starts, query, key, value, log_total, out, grads)


def norm_back(cot_hat, raw, scale_rows, gain, total, width):
    return scale_rows * (cot_hat * gain) - raw * scale_rows**3 * (total[:, None] / width)


class Layout:
    def __init__(self, rows, cols):
        self.rows, self.cols = rows, cols
        self.half = cols // 2
        self.per = cols // rows

    def name(self, row, col):
        core, x = row & 1, row >> 1
        high, low = col // self.half, col % self.half
        return (x * 2 + high, core * self.half + low)

    def place(self, group, rank):
        x, high = group >> 1, group & 1
        core, low = rank // self.half, rank % self.half
        return (x * 2 + core) * self.cols + high * self.half + low

    def pairs(self, target):
        out = []
        for row in range(self.rows):
            for col in range(self.cols):
                out.append((row * self.cols + col, target(row, col)))
        return out

    def across_ranks(self, mask):
        def target(row, col):
            group, rank = self.name(row, col)
            return self.place(group, rank ^ mask)

        return self.pairs(target)

    def across_groups(self, mask):
        def target(row, col):
            group, rank = self.name(row, col)
            return self.place(group ^ mask, rank)

        return self.pairs(target)

    def exchange(self, flip):
        def target(row, col):
            core, x = row & 1, row >> 1
            high, low = col // self.half, col % self.half
            return (x * 2 + high) * self.cols + (core ^ flip) * self.half + low

        return self.pairs(target)

    def exchange_back(self, flip):
        return [(b, a) for a, b in self.exchange(flip)]


def send(values, pairs):
    return lax.ppermute(values, ("rows", "cols"), pairs)


class Chain:
    def __init__(self):
        self.last = None

    def send(self, values, pairs):
        if self.last is not None:
            values, self.last = lax.optimization_barrier((values, self.last))
        self.last = send(values, pairs)
        return self.last


def pick(values, places):
    if len(places) == 1:
        return values[places[0]][None]
    gap = places[1] - places[0]
    if places == list(range(places[0], places[-1] + 1, gap)):
        return values[places[0] : places[-1] + 1 : gap]
    return jnp.stack([values[p] for p in places])


def after(values, *others):
    return lax.optimization_barrier((values, *others))[0]


def params():
    return pltpu.CompilerParams(vmem_limit_bytes=VMEM)


def whole(shape):
    zeros = (0,) * len(shape)
    return pl.BlockSpec(shape, lambda *_: zeros, pipeline_mode=pl.Buffered(1))


def gather_pieces(ids, pieces, names, wide, per):
    rank, group = ids[0], ids[1]
    width = pieces[0].shape[-1]
    shift = per.bit_length() - 1
    for piece, numbers in zip(pieces, names, strict=True):
        for place, index in enumerate(numbers):
            block = jnp.bitwise_xor(rank, index)
            shard = jnp.bitwise_xor(lax.shift_right_logical(block, shift), group)
            inside = jnp.bitwise_and(block, per - 1)
            columns = pl.ds(pl.multiple_of(inside * width, width), width)
            wide[shard, :, columns] = piece[place]


def dot_rows(wide, shards, turned):
    dims = (((1,), (1,)), ((), ())) if turned else (((1,), (0,)), ((), ()))
    total = None
    for index, shard in enumerate(shards):
        part = lax.dot_general(wide[index], shard, dims, preferred_element_type=WIDE)
        total = part if total is None else total + part
    return total


def rows_kernel(names, count, shards, per, turned, epilogue, extra, merged, ids, *refs):
    pieces, refs = refs[: len(names)], refs[len(names) :]
    stacks, refs = refs[:shards], refs[shards:]
    extras, outs = refs[:extra], refs[extra + merged :]
    wide = outs[-1]
    gather_pieces(ids, pieces, names, wide, per)
    results = [dot_rows(wide, [stack[n] for stack in stacks], turned) for n in range(count)]
    epilogue(results, extras, outs[:-1])


def matmul_rows(ids, pieces, names, stacks, per, turned, epilogue, extras, out_types, into, block):
    rows, width = pieces[0].shape[1:]
    chunk, chunks, earlier = into
    shards = len(stacks)
    count = stacks[0].shape[0]
    block = min(block, rows)
    wide_width = per * width
    first = chunk * (rows // block)

    def tall(columns, merge=False):
        offset = first if merge else 0
        return pl.BlockSpec((block, columns), lambda i, _: (i + offset, 0))

    in_specs = [pl.BlockSpec((p.shape[0], block, width), lambda i, _: (0, i, 0)) for p in pieces]
    in_specs += [whole(stack.shape) for stack in stacks]
    in_specs += [tall(extra.shape[1]) for extra in extras]
    out_specs = [tall(columns, merge) for columns, _, merge in out_types]
    out_specs.append(pl.BlockSpec((shards, block, wide_width), lambda i, _: (0, i + first, 0)))
    out_shape = [
        jax.ShapeDtypeStruct((rows * chunks if merge else rows, columns), kind)
        for columns, kind, merge in out_types
    ]
    out_shape.append(jax.ShapeDtypeStruct((shards, rows * chunks, wide_width), LOW))
    merged = [i for i, kind in enumerate(out_types) if kind[2]] + [len(out_types)]
    handed = [] if earlier is None else [earlier[i] for i in merged]
    in_specs += [pl.BlockSpec(memory_space=pl.ANY) for _ in handed]
    operands = [ids, *pieces, *stacks, *extras]
    aliases = {len(operands) + n: i for n, i in enumerate(merged)} if handed else {}
    body = functools.partial(
        rows_kernel, names, count, shards, per, turned, epilogue, len(extras), len(handed)
    )
    size = sum(a.size * a.dtype.itemsize for a in operands)
    size += sum(columns * rows * jnp.dtype(kind).itemsize for columns, kind, _ in out_types)
    flops = 2 * rows * stacks[0].size * shards
    return pl.pallas_call(
        body,
        grid_spec=pltpu.PrefetchScalarGridSpec(
            num_scalar_prefetch=1,
            grid=(rows // block,),
            in_specs=in_specs,
            out_specs=out_specs,
        ),
        out_shape=out_shape,
        input_output_aliases=aliases,
        compiler_params=params(),
        cost_estimate=pl.CostEstimate(flops=flops, bytes_accessed=size, transcendentals=0),
    )(*operands, *handed)


def columns_kernel(count, shards, per, turned, ids, *refs):
    lefts, stacks = refs[:count], refs[count : count + shards]
    keep, give, held = refs[count + shards :]
    rank, group = ids[0], ids[1]
    half, _, width = keep.shape
    shift = per.bit_length() - 1
    dims = (((1,), (1,)), ((), ())) if turned else (((1,), (0,)), ((), ()))
    for index, stack in enumerate(stacks):
        total = None
        for number, left in enumerate(lefts):
            part = lax.dot_general(left[...], stack[number], dims, preferred_element_type=WIDE)
            total = part if total is None else total + part
        total = total.astype(LOW)
        base = lax.shift_left(jnp.bitwise_xor(group, index), shift)
        for inside in range(per):
            piece = jnp.bitwise_xor(base + inside, rank)
            held[piece] = total[:, inside * width : (inside + 1) * width]
    keep[...] = held[:half]
    give[...] = held[half:]


def matmul_columns(ids, lefts, offset, rows, stacks, per, ranks, turned, block):
    block = min(block, rows)
    shards = len(stacks)
    width = stacks[0].shape[1 if turned else 2] // per
    first = offset // block
    in_specs = [
        pl.BlockSpec((block, left.shape[1]), lambda i, _: (i + first, 0)) for left in lefts
    ]
    in_specs += [whole(stack.shape) for stack in stacks]
    part = pl.BlockSpec((ranks // 2, block, width), lambda i, _: (0, i, 0))
    shape = jax.ShapeDtypeStruct((ranks // 2, rows, width), LOW)
    size = sum(rows * left.shape[1] * 2 for left in lefts) + 4 * shape.size
    size += sum(stack.size * 2 for stack in stacks)
    flops = 2 * rows * stacks[0].size * shards
    return pl.pallas_call(
        functools.partial(columns_kernel, len(lefts), shards, per, turned),
        grid_spec=pltpu.PrefetchScalarGridSpec(
            num_scalar_prefetch=1,
            grid=(rows // block,),
            in_specs=in_specs,
            out_specs=[part, part],
            scratch_shapes=[pltpu.VMEM((ranks, block, width), LOW)],
        ),
        out_shape=[shape, shape],
        compiler_params=params(),
        cost_estimate=pl.CostEstimate(flops=flops, bytes_accessed=size, transcendentals=0),
    )(ids, *lefts, *stacks)


def tall_kernel(counts, half, wide_left, wide, *refs):
    talls, (keep, give) = refs[: sum(counts)], refs[sum(counts) :]
    results = []
    for count in counts:
        total, offset = None, 0
        for tall in talls[:count]:
            rows = tall.shape[0]
            sides = (wide[0, offset : offset + rows, :], tall[...])
            left, right = sides if wide_left else sides[::-1]
            dims = (((0,), (0,)), ((), ()))
            part = lax.dot_general(left, right, dims, preferred_element_type=WIDE)
            total = part if total is None else total + part
            offset += rows
        talls = talls[count:]
        results.append(total.astype(LOW))

    @pl.when(pl.program_id(0) < half)
    def _():
        for number, result in enumerate(results):
            give[0, number] = result

    @pl.when(pl.program_id(0) >= half)
    def _():
        for number, result in enumerate(results):
            keep[0, number] = result


def matmul_tall(wide, groups, wide_left, block):
    shards, length, features = wide.shape
    columns = groups[0][0].shape[1]
    half = shards // 2
    count = len(groups)
    talls = [tall for group in groups for tall in group]

    def order(i):
        return lax.rem(i + half, shards)

    if wide_left:
        block = min(block, features)
        steps = features // block
        in_specs = [pl.BlockSpec((1, length, block), lambda i, j: (order(i), 0, j))]
        in_specs += [whole(tall.shape) for tall in talls]
        tile = (1, count, block, columns)
        full = (half, count, features, columns)
    else:
        block = min(block, columns)
        steps = columns // block
        in_specs = [pl.BlockSpec((1, length, features), lambda i, j: (order(i), 0, 0))]
        in_specs += [pl.BlockSpec((tall.shape[0], block), lambda i, j: (0, j)) for tall in talls]
        tile = (1, count, block, features)
        full = (half, count, columns, features)

    def give_place(i, j):
        ahead = i < half
        return (jnp.where(ahead, i, half - 1), 0, jnp.where(ahead, j, steps - 1), 0)

    def keep_place(i, j):
        ahead = i < half
        return (jnp.where(ahead, 0, i - half), 0, jnp.where(ahead, 0, j), 0)

    shape = jax.ShapeDtypeStruct(full, LOW)
    size = wide.size * 2 + sum(tall.size * 2 for tall in talls) + 4 * shape.size
    return pl.pallas_call(
        functools.partial(tall_kernel, [len(g) for g in groups], half, wide_left),
        grid=(shards, steps),
        in_specs=in_specs,
        out_specs=[pl.BlockSpec(tile, keep_place), pl.BlockSpec(tile, give_place)],
        out_shape=[shape, shape],
        compiler_params=params(),
        cost_estimate=pl.CostEstimate(
            flops=2 * wide.size * columns * count, bytes_accessed=size, transcendentals=0
        ),
    )(wide, *talls)


def prepare_kernel(scale, query, key, scales, gains, cosine, sine_part, query_low, key_low):
    heads = query.shape[1] // HEAD_DIM
    columns = scales[...].T
    for source, target, number, factor in ((query, query_low, 0, scale), (key, key_low, 1, 1.0)):
        normed = source[...] * columns[:, number : number + 1] * gains[number : number + 1, :]
        for head in range(heads):
            part = normed[:, head * HEAD_DIM : (head + 1) * HEAD_DIM]
            spun = part * cosine[...] + pltpu.roll(part, HEAD_DIM // 2, 1) * sine_part[...]
            target[:, head * HEAD_DIM : (head + 1) * HEAD_DIM] = (spun * factor).astype(LOW)


def prepare(query, key, scales, gains, cosine, sine_part, scale, block):
    length, local = query.shape
    tall = pl.BlockSpec((block, local), lambda i: (i, 0))
    table = pl.BlockSpec((block, HEAD_DIM), lambda i: (i, 0))
    shape = jax.ShapeDtypeStruct((length, local), LOW)
    return pl.pallas_call(
        functools.partial(prepare_kernel, scale),
        grid=(length // block,),
        in_specs=[
            tall,
            tall,
            pl.BlockSpec((8, block), lambda i: (0, i)),
            whole(gains.shape),
            table,
            table,
        ],
        out_specs=[tall, tall],
        out_shape=[shape, shape],
        compiler_params=params(),
        cost_estimate=pl.CostEstimate(
            flops=20 * query.size, bytes_accessed=12 * query.size, transcendentals=0
        ),
    )(query, key, scales, gains, cosine, sine_part)


def unturn_kernel(
    scale, query, key, query_grad, key_grad, scales, gains, cosine, sine_part, *outs
):
    query_hat, key_hat, sums, gain_sums = outs
    heads = query.shape[1] // HEAD_DIM
    columns = scales[...].T
    lines, gain_rows = [], []
    for raw, grad, target, number, factor in (
        (query, query_grad, query_hat, 0, scale),
        (key, key_grad, key_hat, 1, 1.0),
    ):
        for head in range(heads):
            part = slice(head * HEAD_DIM, (head + 1) * HEAD_DIM)
            back = grad[:, part] * factor
            target[:, part] = back * cosine[...] - pltpu.roll(back, HEAD_DIM // 2, 1) * sine_part[...]
        product = target[...] * raw[...]
        gain_rows.append(
            jnp.sum(product * columns[:, number : number + 1], axis=0, keepdims=True)
        )
        weighted = product * gains[number : number + 1, :]
        lines.append(jnp.sum(weighted, axis=1, keepdims=True))
    spread = jnp.concatenate(lines + [jnp.zeros((query.shape[0], 6), WIDE)], axis=1)
    sums[...] = spread.T

    @pl.when(pl.program_id(0) == 0)
    def _():
        gain_sums[...] = jnp.zeros_like(gain_sums)

    for number, line in enumerate(gain_rows):
        gain_sums[number : number + 1, :] += line


def unturn(query, key, query_grad, key_grad, scales, gains, cosine, sine_part, scale, block):
    length, local = query.shape
    tall = pl.BlockSpec((block, local), lambda i: (i, 0))
    table = pl.BlockSpec((block, HEAD_DIM), lambda i: (i, 0))
    line = pl.BlockSpec((8, block), lambda i: (0, i))
    shape = jax.ShapeDtypeStruct((length, local), WIDE)
    return pl.pallas_call(
        functools.partial(unturn_kernel, scale),
        grid=(length // block,),
        in_specs=[tall, tall, tall, tall, line, whole(gains.shape), table, table],
        out_specs=[tall, tall, line, pl.BlockSpec((8, local), lambda i: (0, 0))],
        out_shape=[
            shape,
            shape,
            jax.ShapeDtypeStruct((8, length), WIDE),
            jax.ShapeDtypeStruct((8, local), WIDE),
        ],
        compiler_params=params(),
        cost_estimate=pl.CostEstimate(
            flops=20 * query.size, bytes_accessed=24 * query.size, transcendentals=0
        ),
    )(query, key, query_grad, key_grad, scales, gains, cosine, sine_part)


def query_key_value(results, _, outs):
    query, key, value = results
    outs[0][...] = query
    outs[1][...] = key
    outs[2][...] = value.astype(LOW)


def gated(results, _, outs):
    gate, upward = results
    outs[0][...] = (gate * jax.nn.sigmoid(gate) * upward).astype(LOW)
    outs[1][...] = gate.astype(LOW)
    outs[2][...] = upward.astype(LOW)


def gated_back(results, extras, outs):
    mixed_back = results[0]
    gate = extras[0][...].astype(WIDE)
    upward = extras[1][...].astype(WIDE)
    gate_sig = jax.nn.sigmoid(gate)
    outs[0][...] = (mixed_back * upward * gate_sig * (1.0 + gate * (1.0 - gate_sig))).astype(LOW)
    outs[1][...] = (mixed_back * gate * gate_sig).astype(LOW)


def just_low(results, _, outs):
    outs[0][...] = results[0].astype(LOW)


def per_device(
    layout,
    tokens,
    segment_ids,
    w_query,
    w_key,
    w_value,
    w_out,
    w_gate,
    w_up,
    w_down,
    q_gain,
    k_gain,
    attn_gain,
    ffn_gain,
    out_grad,
):
    seq_len = segment_ids.shape[1]
    rows, local = tokens.shape
    ranks, groups, per = layout.cols, layout.rows, layout.per
    model = local * ranks
    hidden_units = w_gate.shape[1]
    scale = HEAD_DIM ** (-0.5)
    chunks = CHUNKS
    step = rows // chunks
    cuts = [(c * step, (c + 1) * step) for c in range(chunks)]
    row, col = lax.axis_index("rows"), lax.axis_index("cols")
    group = (row // 2) * 2 + col // layout.half
    rank = (row % 2) * layout.half + col % layout.half
    ids = jnp.stack([rank, group]).astype(jnp.int32)
    rank_bits = [1 << i for i in range(ranks.bit_length() - 1)]
    group_bits = [1 << i for i in range(1, groups.bit_length() - 1)]
    cores = rank_bits[-1]

    def links(index):
        return rank_bits[:-1] if index % 2 else rank_bits[:-1][::-1]

    def piece_names(index):
        found = [(0,)]
        for mask in [*links(index), cores]:
            found.append(tuple(j ^ mask for names in found for j in names))
        return found

    far, side = Chain(), Chain()

    def spread(piece, index):
        pieces = [piece[None]]
        for mask in [*links(index), cores]:
            whole_part = pieces[0] if len(pieces) == 1 else jnp.concatenate(pieces)
            pieces.append(send(whole_part, layout.across_ranks(mask)))
        return pieces

    def totals(stacked):
        for mask in rank_bits:
            stacked = stacked + send(stacked, layout.across_ranks(mask))
        return stacked

    def reduce(keep, give, index):
        arrived = send(give, layout.across_ranks(cores))
        names = list(range(cores))
        for mask in links(index + 1):
            total = (keep.astype(WIDE) + arrived.astype(WIDE)).astype(LOW)
            stay = [n for n, name in enumerate(names) if not name & mask]
            leave = [names.index(names[n] ^ mask) for n in stay]
            keep, give = pick(total, stay), pick(total, leave)
            names = [names[n] for n in stay]
            arrived = send(give, layout.across_ranks(mask))
        return keep[0].astype(WIDE) + arrived[0].astype(WIDE)

    def whole_weight(stack):
        found = [far.send(stack, layout.exchange(0)), far.send(stack, layout.exchange(1))]
        for mask in group_bits:
            found += [side.send(v, layout.across_groups(mask)) for v in found]
        return found

    def owners_sum(keep, give):
        for mask in group_bits[::-1]:
            arrived = side.send(give, layout.across_groups(mask))
            total = (keep.astype(WIDE) + arrived.astype(WIDE)).astype(LOW)
            size = total.shape[0] // 2
            keep, give = total[:size], total[size:]
        mine = far.send(keep[0], layout.exchange_back(0))
        other = far.send(give[0], layout.exchange_back(1))
        count = mine.shape[0]
        return [mine[n].astype(WIDE) + other[n].astype(WIDE) for n in range(count)]

    tokens = send(tokens, layout.exchange(0))
    full_qkv = whole_weight(jnp.stack([w_query, w_key, w_value]))
    gains = send(jnp.stack([q_gain, k_gain, attn_gain, ffn_gain]), layout.exchange(0))
    attn_gain, ffn_gain = gains[2], gains[3]
    segment_ids = send(segment_ids, layout.exchange(0))
    full_out = whole_weight(w_out[None])
    full_gated = whole_weight(jnp.stack([w_gate, w_up]))
    full_down = whole_weight(w_down[None])
    out_grad = far.send(out_grad, layout.exchange(0))
    cosine, sine_part = rotation(seq_len, HEAD_DIM)

    made = None
    for index, (low, high) in enumerate(cuts):
        made = matmul_rows(
            ids,
            spread(tokens[low:high], index),
            piece_names(index),
            full_qkv,
            per,
            False,
            query_key_value,
            [],
            [(local, WIDE, True), (local, WIDE, True), (local, LOW, True)],
            (index, chunks, made),
            256,
        )
    query_raw, key_raw, value_low, token_wide = made
    qk_stats = totals(
        jnp.stack([jnp.sum(query_raw * query_raw, axis=1), jnp.sum(key_raw * key_raw, axis=1)])
    )
    scales = jnp.pad(lax.rsqrt(qk_stats / model + EPS), ((0, 6), (0, 0)))
    block = min(512, seq_len)
    query_low, key_low = prepare(
        query_raw, key_raw, scales, gains, cosine, sine_part, scale, block
    )
    names = jnp.arange(DOCUMENTS, dtype=jnp.int32)[:, None]
    before = jnp.sum((segment_ids < names).astype(jnp.int32), axis=1, keepdims=True)
    starts = jnp.sum(jnp.where(segment_ids == names, before, 0), axis=0, keepdims=True)
    lows = starts[0, ::block] // block
    per_chunk = step // block
    columns = functools.partial(matmul_columns, ids, per=per, ranks=ranks, block=256)
    attn_parts, log_totals, out_sums = [], [], []
    for index in range(chunks):
        if index:
            query_low = after(query_low, out_sums[-1])
        out, log_total = attend(
            lows, starts, query_low, key_low, value_low, index * per_chunk, per_chunk, block
        )
        out_sums.append(columns([out], 0, step, full_out, turned=False))
        attn_parts.append(out)
        log_totals.append(log_total)

    def mean_scale(stats):
        return lax.rsqrt(stats / model + EPS)[:, None]

    hidden_made, ffn_made, attn_made = None, None, None
    mixes, gate_backs, up_backs, hidden_cots, layer_outs = [], [], [], [], []
    gain_attn, gain_ffn = 0.0, 0.0
    for index, (low, high) in enumerate(cuts):
        attn_sum = reduce(*out_sums[index], index)
        attn_scale = mean_scale(totals(jnp.sum(attn_sum * attn_sum, axis=1)[None])[0])
        hidden = tokens[low:high].astype(WIDE) + attn_sum * attn_scale * attn_gain
        pieces = spread(hidden.astype(LOW), index)
        if index:
            pieces = after(pieces, forward_last)
        hidden_made = matmul_rows(
            ids,
            pieces,
            piece_names(index),
            full_gated,
            per,
            False,
            gated,
            [],
            [(hidden_units, LOW, False)] * 3,
            (index, chunks, hidden_made),
            256,
        )
        mixed, gate, upward = hidden_made[:3]
        forward_last = columns([mixed], 0, step, full_down, turned=False)
        ffn_sum = reduce(*forward_last, index)
        out_cot = out_grad[low:high].astype(WIDE)
        stats = totals(
            jnp.stack(
                [
                    jnp.sum(ffn_sum * ffn_sum, axis=1),
                    jnp.sum(out_cot * ffn_gain * ffn_sum, axis=1),
                ]
            )
        )
        ffn_scale = mean_scale(stats[0])
        layer_outs.append((hidden + ffn_sum * ffn_scale * ffn_gain).astype(LOW))
        gain_ffn = gain_ffn + jnp.sum(out_cot * ffn_sum * ffn_scale, axis=0)
        ffn_back = norm_back(out_cot, ffn_sum, ffn_scale, ffn_gain, stats[1], model).astype(LOW)
        pieces = spread(ffn_back, index)
        if index:
            pieces = after(pieces, backward_last)
        ffn_made = matmul_rows(
            ids,
            pieces,
            piece_names(index),
            full_down,
            per,
            True,
            gated_back,
            [gate, upward],
            [(hidden_units, LOW, False)] * 2,
            (index, chunks, ffn_made),
            256,
        )
        gate_back, up_back = ffn_made[:2]
        backward_last = columns([gate_back, up_back], 0, step, full_gated, turned=True)
        hidden_cot = out_cot + reduce(*backward_last, index)
        attn_total = totals(jnp.sum(hidden_cot * attn_gain * attn_sum, axis=1)[None])[0]
        gain_attn = gain_attn + jnp.sum(hidden_cot * attn_sum * attn_scale, axis=0)
        attn_back = norm_back(
            hidden_cot, attn_sum, attn_scale, attn_gain, attn_total, model
        ).astype(LOW)
        attn_made = matmul_rows(
            ids,
            spread(attn_back, index),
            piece_names(index),
            full_out,
            per,
            True,
            just_low,
            [],
            [(local, LOW, True)],
            (index, chunks, attn_made),
            256,
        )
        mixes.append(mixed)
        gate_backs.append(gate_back)
        up_backs.append(up_back)
        hidden_cots.append(hidden_cot)

    layer_out = far.send(jnp.concatenate(layer_outs), layout.exchange_back(0))
    grad_down = owners_sum(*matmul_tall(ffn_made[-1], [mixes], False, 512))[0]
    grad_gate, grad_up = owners_sum(
        *matmul_tall(hidden_made[-1], [gate_backs, up_backs], True, 256)
    )
    out_back, attn_wide = attn_made
    grad_out = owners_sum(*matmul_tall(attn_wide, [attn_parts], False, 256))[0]

    query_grad, key_grad, value_grad = attend_back(
        lows,
        starts,
        query_low,
        key_low,
        value_low,
        jnp.concatenate(log_totals, axis=2),
        jnp.concatenate(attn_parts),
        out_back,
        block,
    )
    value_back = value_grad.astype(LOW)
    query_hat, key_hat, sums, gain_sums = unturn(
        query_raw,
        key_raw,
        query_grad,
        key_grad,
        scales,
        gains,
        cosine,
        sine_part,
        scale,
        block,
    )
    qk_totals = totals(sums[:2])
    query_back = norm_back(
        query_hat, query_raw, scales[0][:, None], gains[0], qk_totals[0], model
    ).astype(LOW)
    key_back = norm_back(
        key_hat, key_raw, scales[1][:, None], gains[1], qk_totals[1], model
    ).astype(LOW)

    input_grads = []
    for index, (low, high) in enumerate(cuts):
        total = columns([query_back, key_back, value_back], low, step, full_qkv, turned=True)
        total = reduce(*total, index)
        total = (hidden_cots[index] + total).astype(LOW)
        input_grads.append(send(total, layout.exchange_back(0)))
    input_grad = jnp.concatenate(input_grads)
    grad_query, grad_key, grad_value = owners_sum(
        *matmul_tall(token_wide, [[query_back], [key_back], [value_back]], True, 512)
    )

    gains = jnp.concatenate([gain_sums[:2], gain_attn[None], gain_ffn[None]])
    for mask in [1, *group_bits]:
        gains = gains + send(gains, layout.across_groups(mask))
    gains = send(gains, layout.exchange_back(0))
    return (
        layer_out,
        input_grad,
        grad_query,
        grad_key,
        grad_value,
        grad_out,
        grad_gate,
        grad_up,
        grad_down,
        gains[0],
        gains[1],
        gains[2],
        gains[3],
    )


def solution(mesh):
    layout = Layout(mesh.shape["rows"], mesh.shape["cols"])
    both, turned, lone = P("rows", "cols"), P("cols", "rows"), P("cols")
    in_specs = (both, P("rows", None), both, both, both, turned, both, both, turned)
    in_specs += (lone, lone, lone, lone, both)
    out_specs = (both, both, both, both, both, turned, both, both, turned)
    out_specs += (lone, lone, lone, lone)
    return jax.shard_map(
        functools.partial(per_device, layout),
        mesh=mesh,
        in_specs=in_specs,
        out_specs=out_specs,
        check_vma=False,
    )
```

time: 2300 us -> 1070 us (0.47)
  waiting for transfers between devices: 1710 us -> 364 us
  Pallas kernels: 0 us -> 324 us
  matrix products: 289 us -> 0 us
  starting transfers between devices: 1.54 us -> 270 us
  blocking collectives: 156 us -> 0 us
    reduce_scatter x11 -> x0, waiting for transfers between devices: 1180 us -> none  [the longest x4 1130 us: reduce_features(): return lax.psum_scatter(values, 'cols', scatter_dimension=1, tiled=True)]
    all_gather x11 -> x0, waiting for transfers between devices: 527 us -> none  [the longest x4 459 us: spread_features(): return lax.all_gather(values, 'cols', axis=1, tiled=True)]
    ppermute x0 -> x178, waiting for transfers between devices: none -> 364 us  [send(): return lax.ppermute(values, ('rows', 'cols'), pairs)]
    pallas_call x0 -> x43, Pallas kernels: none -> 324 us  [the longest x16 110 us: matmul_rows(): pl.pallas_call(body, grid_spec=pltpu.PrefetchScalarGridSpec(num_scalar_pr...]
    dot_general x45 -> x0, matrix products: 289 us -> none  [the longest x1 22 us: per_device(): jnp.einsum('td,fd->tf', ffn_back_wide, back_down, preferred_element_type=...]
    ppermute x0 -> x178, starting transfers between devices: none -> 270 us  [send(): return lax.ppermute(values, ('rows', 'cols'), pairs)]
    psum x7 -> x0, blocking collectives: 156 us -> none  [the longest x6 149 us: token_totals(): return lax.psum(stacked, 'cols')]
  transfers between devices with their start and end apart: 22 -> 178, of which waited for: 16 -> 59; matrix products, arithmetic and copies ran while one was open for 13% -> 8% of each run, Pallas kernels for 0% -> 29%
where the time goes in v1:
time: 1070 us; the launch traced here: 1060 us
  waiting for transfers between devices  364 us (34%)
  Pallas kernels  324 us (30%)
  starting transfers between devices  270 us (25%)
  other arithmetic  76.1 us (7%)
  local copies, waits for them, and re-layouts  20.2 us (2%)
    ppermute x178, waiting for transfers between devices, send(): return lax.ppermute(values, ('rows', 'cols'), pairs)  364 us
    ppermute x178, starting transfers between devices, send(): return lax.ppermute(values, ('rows', 'cols'), pairs)  270 us
    pallas_call x16, Pallas kernels, matmul_rows(): pl.pallas_call(body, grid_spec=pltpu.PrefetchScalarGridSpec(num_scalar_pr...  110 us
    pallas_call x16, Pallas kernels, matmul_columns(): pl.pallas_call(functools.partial(columns_kernel, len(lefts), shards, per,...  98.9 us
    pallas_call x4, Pallas kernels, matmul_tall(): pl.pallas_call(functools.partial(tall_kernel, [len(g) for g in groups], h...  59.4 us
    pallas_call x1, Pallas kernels, attend_back(): pl.pallas_call(functools.partial(attend_back_kernel, block), grid_spec=pl...  21.8 us
  transfers between devices with their start and end apart: 178, of which 59 were waited for; matrix products, arithmetic and copies ran while one was open for 8% of the time, Pallas kernels for 29%

profile of v1, /device:TPU:0, one launch (start us, length us, event | category | flops | bytes accessed | tf_op | source)
XLA Modules:
  0.0 1057.9 jit_solution(4798978653303403902)
XLA Ops:
  14.7 35.2 %collective-permute-start.6 = (bf16[3,512,256]{2,1,0:T(8,128)(2,1)S(1)}, bf16[3,512,256]{2,1,0:T(8,128)(2,1)S(1)}, u32[]{:S(2)}, u32[]{:S(2)}) collective-permute-start(bf16[3,512,256]{2,1,0:T(8,128)(2,1)S(1)} %pad_maximum_fusion.22), channel_id=1, source_target_pairs={{0,4},{1,5},{2,6},{3,7},{4,12},{5,13},{6,14},{7,15},{8,0},{9,1},{1... | collective-permute-start | bytes 2359304 | tf_op jit(solution)/shard_map/ppermute | solution.py:211
  63.5 8.4 collective-permute-done.16.refs_2_
  90.7 7.4 collective-permute-done.8.refs_7_.refs_6_
  130.8 12.3 %collective-permute-start.23 = (bf16[1,256,512]{2,1,0:T(8,128)(2,1)S(1)}, bf16[1,256,512]{2,1,0:T(8,128)(2,1)S(1)}, u32[]{:S(2)}, u32[]{:S(2)}) collective-permute-start(bf16[1,256,512]{2,1,0:T(8,128)(2,1)S(1)} %bitcast.535), channel_id=1, source_target_pairs={{0,4},{1,5},{2,6},{3,7},{4,12},{5,13},{6,14},{7,15},{8,0},{9,1},{1... | collective-permute-start | bytes 786440 | tf_op jit(solution)/shard_map/ppermute | solution.py:211
  175.4 6.6 shard_map.250
  197.5 7.5 collective-permute-start.36
  210.1 9.9 collective-permute-done.51
  222.5 24.5 %collective-permute-done.81 = bf16[2,512,256]{2,1,0:T(8,128)(2,1)S(1)} collective-permute-done((bf16[2,512,256]{2,1,0:T(8,128)(2,1)S(1)}, bf16[2,512,256]{2,1,0:T(8,128)(2,1)S(1)}, u32[]{:S(2)}, u32[]{:S(2)}) %collective-permute-start.81) | collective-permute-done | bytes 524320 | tf_op jit(solution)/shard_map/ppermute | solution.py:211
  250.5 8.5 collective-permute-done.67
  274.2 8.1 collective-permute-done.32.refs_1_
  283.6 16.1 %collective-permute-start.40 = (bf16[1,1024,512]{2,1,0:T(8,128)(2,1)S(1)}, bf16[1,1024,512]{2,1,0:T(8,128)(2,1)}, u32[]{:S(2)}, u32[]{:S(2)}) collective-permute-start(bf16[1,1024,512]{2,1,0:T(8,128)(2,1)S(1)} %bitcast.533), channel_id=1, source_target_pairs={{0,4},{1,5},{2,6},{3,7},{4,12},{5,13},{6,14},{7,15},{8,0},{9,1},{1... | collective-permute-start | bytes 3145736 | tf_op jit(solution)/shard_map/ppermute | solution.py:211
  315.1 14.1 %collective-permute-done.71.refs_1_ = bf16[1,512,256]{2,1,0:T(8,128)(2,1)S(1)} collective-permute-done((bf16[1,512,256]{2,1,0:T(8,128)(2,1)S(1)}, bf16[1,512,256]{2,1,0:T(8,128)(2,1)S(1)}, u32[]{:S(2)}, u32[]{:S(2)}) %collective-permute-start.71) | collective-permute-done | bytes 262176 | tf_op jit(solution)/shard_map/ppermute | solution.py:211
  331.3 9.1 collective-permute-done.57.refs_2_
  340.6 7.9 collective-permute-done.87.refs_2_
  351.2 10.5 shard_map.244
  362.7 6.5 shard_map.245
  369.2 10.4 shard_map.248
  379.6 6.5 shard_map.249
  386.0 10.4 shard_map.252
  402.9 10.4 shard_map.256
  413.3 6.5 shard_map.257
  428.5 16.8 %collective-permute-done.90 = bf16[2,512,256]{2,1,0:T(8,128)(2,1)S(1)} collective-permute-done((bf16[2,512,256]{2,1,0:T(8,128)(2,1)S(1)}, bf16[2,512,256]{2,1,0:T(8,128)(2,1)S(1)}, u32[]{:S(2)}, u32[]{:S(2)}) %collective-permute-start.90) | collective-permute-done | bytes 524320 | tf_op jit(solution)/shard_map/ppermute | solution.py:211
  450.1 8.9 collective-permute-done.60
  496.5 10.3 collective-permute-done.97.refs_2_
  514.9 9.0 collective-permute-done.103.refs_2_
  527.6 7.8 shard_map.258
  535.3 10.2 shard_map.259
  546.4 7.7 shard_map.260
  554.1 10.1 shard_map.261
  564.4 7.7 shard_map.262
  572.1 10.5 shard_map.263
  583.7 7.7 shard_map.264
  591.3 10.3 shard_map.265
  606.5 9.5 collective-permute-start.95
  622.9 19.6 %collective-permute-done.130 = bf16[2,512,256]{2,1,0:T(8,128)(2,1)S(1)} collective-permute-done((bf16[2,512,256]{2,1,0:T(8,128)(2,1)S(1)}, bf16[2,512,256]{2,1,0:T(8,128)(2,1)S(1)}, u32[]{:S(2)}, u32[]{:S(2)}) %collective-permute-start.130) | collective-permute-done | bytes 524320 | tf_op jit(solution)/shard_map/ppermute | solution.py:211
  671.3 16.5 %shard_map.279 = (bf16[2,1,1024,512]{3,2,1,0:T(8,128)(2,1)}, bf16[2,1,1024,512]{3,2,1,0:T(8,128)(2,1)}) custom-call(bf16[4,2048,512]{2,1,0:T(8,128)(2,1)} %get-tuple-element.323.wide, bf16[512,1024]{1,0:T(8,128)(2,1)S(1)} %copy-done.13, bf16[512,1024]{1,0:T(8,128)(2,1)} %get-tuple-element.224.refs_0_.refs_1_, ...), custom_call_target="tpu_custom_call" | custom-call | flops 8589934592 | bytes 16777216 | tf_op jit(solution)/shard_map/pallas_call | solution.py:440
  711.0 25.2 %collective-permute-done.163 = bf16[2,1,1024,512]{3,2,1,0:T(8,128)(2,1)} collective-permute-done((bf16[2,1,1024,512]{3,2,1,0:T(8,128)(2,1)}, bf16[2,1,1024,512]{3,2,1,0:T(8,128)(2,1)}, u32[]{:S(2)}, u32[]{:S(2)}) %collective-permute-start.163) | collective-permute-done | bytes 2097184 | tf_op jit(solution)/shard_map/ppermute | solution.py:211
  738.0 24.9 %shard_map.278 = (bf16[2,2,512,1024]{3,2,1,0:T(8,128)(2,1)}, bf16[2,2,512,1024]{3,2,1,0:T(8,128)(2,1)}) custom-call(bf16[4,2048,512]{2,1,0:T(8,128)(2,1)} %get-tuple-element.321.wide, bf16[512,1024]{1,0:T(8,128)(2,1)S(1)} %copy-done.12, bf16[512,1024]{1,0:T(8,128)(2,1)} %get-tuple-element.269.refs_0_.refs_1_, ...), custom_call_target="tpu_custom_call" | custom-call | flops 17179869184 | bytes 25165824 | tf_op jit(solution)/shard_map/pallas_call | solution.py:440
  789.6 21.8 %shard_map.270 = (f32[2048,256]{1,0:T(8,128)}, f32[2048,256]{1,0:T(8,128)}, f32[2048,256]{1,0:T(8,128)}) custom-call(s32[4]{0:T(128)S(1)} %and_select_fusion.lows, s32[1,2048]{1,0:T(1,128)S(1)} %bitcast.402, bf16[2048,256]{1,0:T(8,128)(2,1)S(1)} %get-tuple-element.239.query, bf16[2048,256]{1,0:T(8,128)(2,1)} %get-tuple-element.194.key, ...), custom_call_target="tpu_custom_call" | custom-call | flops 10737418240 | bytes 10485760 | tf_op jit(solution)/shard_map/pallas_call | solution.py:133
  811.5 7.6 shard_map.271
  825.5 29.7 %collective-permute-done.176 = f32[4,256]{1,0:T(4,128)S(1)} collective-permute-done((f32[4,256]{1,0:T(4,128)S(1)}, f32[4,256]{1,0:T(4,128)S(1)}, u32[]{:S(2)}, u32[]{:S(2)}) %collective-permute-start.176) | collective-permute-done | bytes 4128 | tf_op jit(solution)/shard_map/ppermute | solution.py:211
  856.3 6.7 shard_map.277
  906.6 11.3 %shard_map.276 = (bf16[2,3,512,256]{3,2,1,0:T(8,128)(2,1)}, bf16[2,3,512,256]{3,2,1,0:T(8,128)(2,1)}) custom-call(bf16[4,2048,512]{2,1,0:T(8,128)(2,1)} %get-tuple-element.316.wide, bf16[2048,256]{1,0:T(8,128)(2,1)S(1)} %copy-done.2, bf16[2048,256]{1,0:T(8,128)(2,1)} %get-tuple-element.423.refs_1_, bf16[2048,256]{1,0:T(8,128)(2,1)} %convert_element_type.729.refs_2_), custom_call_target="tpu_custom_call" | custom-call | flops 6442450944 | bytes 14680064 | tf_op jit(solution)/shard_map/pallas_call | solution.py:440
  936.2 20.4 %collective-permute-done.152 = bf16[2,512,256]{2,1,0:T(8,128)(2,1)S(1)} collective-permute-done((bf16[2,512,256]{2,1,0:T(8,128)(2,1)S(1)}, bf16[2,512,256]{2,1,0:T(8,128)(2,1)S(1)}, u32[]{:S(2)}, u32[]{:S(2)}) %collective-permute-start.152) | collective-permute-done | bytes 524320 | tf_op jit(solution)/shard_map/ppermute | solution.py:211
  957.2 10.6 collective-permute-done.160
  978.4 10.0 collective-permute-start.172
  1000.9 24.8 %collective-permute-start.174 = (bf16[3,512,256]{2,1,0:T(8,128)(2,1)S(1)}, bf16[3,512,256]{2,1,0:T(8,128)(2,1)S(1)}, u32[]{:S(2)}, u32[]{:S(2)}) collective-permute-start(bf16[3,512,256]{2,1,0:T(8,128)(2,1)S(1)} %get-tuple-element.339), channel_id=1, source_target_pairs={{4,0},{5,1},{6,2},{7,3},{12,4},{13,5},{14,6},{15,7},{0,8},{1,9},{2... | collective-permute-start | bytes 2359304 | tf_op jit(solution)/shard_map/ppermute | solution.py:211
  1030.6 23.4 %collective-permute-done.174 = bf16[3,512,256]{2,1,0:T(8,128)(2,1)S(1)} collective-permute-done((bf16[3,512,256]{2,1,0:T(8,128)(2,1)S(1)}, bf16[3,512,256]{2,1,0:T(8,128)(2,1)S(1)}, u32[]{:S(2)}, u32[]{:S(2)}) %collective-permute-start.174) | collective-permute-done | bytes 786464 | tf_op jit(solution)/shard_map/ppermute | solution.py:211
  (833 shorter events, 438.4 us)
Async XLA Ops:
  4.6 46.9 %collective-permute-start.15 = (bf16[1,512,256]{2,1,0:T(8,128)(2,1)S(1)}, bf16[1,512,256]{2,1,0:T(8,128)(2,1)S(1)}, u32[]{:S(2)}, u32[]{:S(2)}) collective-permute-start(bf16[1,512,256]{2,1,0:T(8,128)(2,1)S(1)} %get-tuple-element.394.refs_0_), channel_id=1, source_target_pairs={{0,2},{1,3},{2,0},{3,1},{4,6},{5,7},{6,4},{7,5},{8,10},{9,11},{10,... | collective-permute-start | bytes 786440 | tf_op jit(solution)/shard_map/ppermute | solution.py:211
  7.7 44.3 %collective-permute-start.12 = (bf16[1,512,256]{2,1,0:T(8,128)(2,1)S(1)}, bf16[1,512,256]{2,1,0:T(8,128)(2,1)S(1)}, u32[]{:S(2)}, u32[]{:S(2)}) collective-permute-start(bf16[1,512,256]{2,1,0:T(8,128)(2,1)S(1)} %get-tuple-element.395.refs_0_), channel_id=1, source_target_pairs={{0,1},{1,0},{2,3},{3,2},{4,5},{5,4},{6,7},{7,6},{8,9},{9,8},{10,11... | collective-permute-start | bytes 786440 | tf_op jit(solution)/shard_map/ppermute | solution.py:211
  9.2 44.5 %collective-permute-start.9 = (bf16[1,512,256]{2,1,0:T(8,128)(2,1)S(1)}, bf16[1,512,256]{2,1,0:T(8,128)(2,1)S(1)}, u32[]{:S(2)}, u32[]{:S(2)}) collective-permute-start(bf16[1,512,256]{2,1,0:T(8,128)(2,1)S(1)} %get-tuple-element.396.refs_0_), channel_id=1, source_target_pairs={{0,2},{1,3},{2,0},{3,1},{4,6},{5,7},{6,4},{7,5},{8,10},{9,11},{10,... | collective-permute-start | bytes 786440 | tf_op jit(solution)/shard_map/ppermute | solution.py:211
  14.7 63.2 %collective-permute-start.6 = (bf16[3,512,256]{2,1,0:T(8,128)(2,1)S(1)}, bf16[3,512,256]{2,1,0:T(8,128)(2,1)S(1)}, u32[]{:S(2)}, u32[]{:S(2)}) collective-permute-start(bf16[3,512,256]{2,1,0:T(8,128)(2,1)S(1)} %pad_maximum_fusion.22), channel_id=1, source_target_pairs={{0,4},{1,5},{2,6},{3,7},{4,12},{5,13},{6,14},{7,15},{8,0},{9,1},{1... | collective-permute-start | bytes 2359304 | tf_op jit(solution)/shard_map/ppermute | solution.py:211
  87.9 29.7 %collective-permute-start.4 = (bf16[4,512,256]{2,1,0:T(8,128)(2,1)S(1)}, bf16[4,512,256]{2,1,0:T(8,128)(2,1)S(1)}, u32[]{:S(2)}, u32[]{:S(2)}) collective-permute-start(bf16[4,512,256]{2,1,0:T(8,128)(2,1)S(1)} %pad_maximum_fusion.1), channel_id=1, source_target_pairs={{0,8},{1,9},{2,10},{3,11},{4,12},{5,13},{6,14},{7,15},{8,0},{9,1},... | collective-permute-start | bytes 3145736 | tf_op jit(solution)/shard_map/ppermute | solution.py:211
  98.1 55.1 %collective-permute-start.21 = (f32[4,256]{1,0:T(4,128)S(1)}, f32[4,256]{1,0:T(4,128)S(1)}, u32[]{:S(2)}, u32[]{:S(2)}) collective-permute-start(f32[4,256]{1,0:T(4,128)S(1)} %pad_maximum_fusion.41), channel_id=1, source_target_pairs={{0,0},{1,1},{2,2},{3,3},{4,8},{5,9},{6,10},{7,11},{8,4},{9,5},{10,... | collective-permute-start | bytes 12296 | tf_op jit(solution)/shard_map/ppermute | solution.py:211
  98.8 29.0 %collective-permute-start.1 = (s32[1,2048]{1,0:T(1,128)S(1)}, s32[1,2048]{1,0:T(1,128)S(1)}, u32[]{:S(2)}, u32[]{:S(2)}) collective-permute-start(s32[1,2048]{1,0:T(1,128)S(1)} %copy-done.130), channel_id=1, source_target_pairs={{0,0},{1,1},{2,2},{3,3},{4,8},{5,9},{6,10},{7,11},{8,4},{9,5},{10,... | collective-permute-start | bytes 24584 | tf_op jit(solution)/shard_map/ppermute | solution.py:211
  147.1 48.8 %collective-permute-start.35 = (bf16[2,512,1024]{2,1,0:T(8,128)(2,1)}, bf16[2,512,1024]{2,1,0:T(8,128)(2,1)S(1)}, u32[]{:S(2)}, u32[]{:S(2)}) collective-permute-start(bf16[2,512,1024]{2,1,0:T(8,128)(2,1)} %pad_maximum_fusion), channel_id=1, source_target_pairs={{0,0},{1,1},{2,2},{3,3},{4,8},{5,9},{6,10},{7,11},{8,4},{9,5},{10,... | collective-permute-start | bytes 6291464 | tf_op jit(solution)/shard_map/ppermute | solution.py:211
  195.9 63.7 %collective-permute-start.37 = (bf16[2,512,1024]{2,1,0:T(8,128)(2,1)S(1)}, bf16[2,512,1024]{2,1,0:T(8,128)(2,1)S(1)}, u32[]{:S(2)}, u32[]{:S(2)}) collective-permute-start(bf16[2,512,1024]{2,1,0:T(8,128)(2,1)S(1)} %collective-permute-done.35.refs_4_.refs_2_), channel_id=1, source_target_pairs={{0,16},{1,17},{2,18},{3,19},{4,20},{5,21},{6,22},{7,23},{8,24},{9,... | collective-permute-start | bytes 6291464 | tf_op jit(solution)/shard_map/ppermute | solution.py:211
  197.5 63.8 %collective-permute-start.36 = (bf16[2,512,1024]{2,1,0:T(8,128)(2,1)S(1)}, bf16[2,512,1024]{2,1,0:T(8,128)(2,1)S(1)}, u32[]{:S(2)}, u32[]{:S(2)}) collective-permute-start(bf16[2,512,1024]{2,1,0:T(8,128)(2,1)S(1)} %copy-done.84), channel_id=1, source_target_pairs={{0,4},{1,5},{2,6},{3,7},{4,12},{5,13},{6,14},{7,15},{8,0},{9,1},{1... | collective-permute-start | bytes 6291464 | tf_op jit(solution)/shard_map/ppermute | solution.py:211
  207.4 39.6 %collective-permute-start.81 = (bf16[2,512,256]{2,1,0:T(8,128)(2,1)S(1)}, bf16[2,512,256]{2,1,0:T(8,128)(2,1)S(1)}, u32[]{:S(2)}, u32[]{:S(2)}) collective-permute-start(bf16[2,512,256]{2,1,0:T(8,128)(2,1)S(1)} %slice.487), channel_id=1, source_target_pairs={{0,2},{1,3},{2,0},{3,1},{4,6},{5,7},{6,4},{7,5},{8,10},{9,11},{10,... | collective-permute-start | bytes 1572872 | tf_op jit(solution)/shard_map/ppermute | solution.py:211
  220.0 29.7 %collective-permute-start.27 = (bf16[2,512,256]{2,1,0:T(8,128)(2,1)S(1)}, bf16[2,512,256]{2,1,0:T(8,128)(2,1)S(1)}, u32[]{:S(2)}, u32[]{:S(2)}) collective-permute-start(bf16[2,512,256]{2,1,0:T(8,128)(2,1)S(1)} %slice.351), channel_id=1, source_target_pairs={{0,1},{1,0},{2,3},{3,2},{4,5},{5,4},{6,7},{7,6},{8,9},{9,8},{10,11... | collective-permute-start | bytes 1572872 | tf_op jit(solution)/shard_map/ppermute | solution.py:211
  220.5 29.7 %collective-permute-start.52 = (bf16[1,512,256]{2,1,0:T(8,128)(2,1)S(1)}, bf16[1,512,256]{2,1,0:T(8,128)(2,1)S(1)}, u32[]{:S(2)}, u32[]{:S(2)}) collective-permute-start(bf16[1,512,256]{2,1,0:T(8,128)(2,1)S(1)} %slice.473), channel_id=1, source_target_pairs={{0,1},{1,0},{2,3},{3,2},{4,5},{5,4},{6,7},{7,6},{8,9},{9,8},{10,11... | collective-permute-start | bytes 786440 | tf_op jit(solution)/shard_map/ppermute | solution.py:211
  261.3 41.0 %collective-permute-start.38 = (bf16[2,512,1024]{2,1,0:T(8,128)(2,1)S(1)}, bf16[2,512,1024]{2,1,0:T(8,128)(2,1)S(1)}, u32[]{:S(2)}, u32[]{:S(2)}) collective-permute-start(bf16[2,512,1024]{2,1,0:T(8,128)(2,1)S(1)} %collective-permute-done.36.refs_5_.refs_3_), channel_id=1, source_target_pairs={{0,16},{1,17},{2,18},{3,19},{4,20},{5,21},{6,22},{7,23},{8,24},{9,... | collective-permute-start | bytes 6291464 | tf_op jit(solution)/shard_map/ppermute | solution.py:211
  282.4 29.9 %collective-permute-start.33 = (bf16[2,512,256]{2,1,0:T(8,128)(2,1)S(1)}, bf16[2,512,256]{2,1,0:T(8,128)(2,1)S(1)}, u32[]{:S(2)}, u32[]{:S(2)}) collective-permute-start(bf16[2,512,256]{2,1,0:T(8,128)(2,1)S(1)} %pad_maximum_fusion.27), channel_id=1, source_target_pairs={{0,1},{1,0},{2,3},{3,2},{4,5},{5,4},{6,7},{7,6},{8,9},{9,8},{10,11... | collective-permute-start | bytes 1572872 | tf_op jit(solution)/shard_map/ppermute | solution.py:211
  283.6 45.6 %collective-permute-start.40 = (bf16[1,1024,512]{2,1,0:T(8,128)(2,1)S(1)}, bf16[1,1024,512]{2,1,0:T(8,128)(2,1)}, u32[]{:S(2)}, u32[]{:S(2)}) collective-permute-start(bf16[1,1024,512]{2,1,0:T(8,128)(2,1)S(1)} %bitcast.533), channel_id=1, source_target_pairs={{0,4},{1,5},{2,6},{3,7},{4,12},{5,13},{6,14},{7,15},{8,0},{9,1},{1... | collective-permute-start | bytes 3145736 | tf_op jit(solution)/shard_map/ppermute | solution.py:211
  315.0 36.2 %collective-permute-start.34 = (bf16[4,512,256]{2,1,0:T(8,128)(2,1)S(1)}, bf16[4,512,256]{2,1,0:T(8,128)(2,1)}, u32[]{:S(2)}, u32[]{:S(2)}) collective-permute-start(bf16[4,512,256]{2,1,0:T(8,128)(2,1)S(1)} %pad_maximum_fusion.7), channel_id=1, source_target_pairs={{0,8},{1,9},{2,10},{3,11},{4,12},{5,13},{6,14},{7,15},{8,0},{9,1},... | collective-permute-start | bytes 3145736 | tf_op jit(solution)/shard_map/ppermute | solution.py:211
  330.3 31.4 %collective-permute-start.42 = (bf16[1,1024,512]{2,1,0:T(8,128)(2,1)}, bf16[1,1024,512]{2,1,0:T(8,128)(2,1)S(1)}, u32[]{:S(2)}, u32[]{:S(2)}) collective-permute-start(bf16[1,1024,512]{2,1,0:T(8,128)(2,1)} %collective-permute-done.40.refs_2_.refs_5_), channel_id=1, source_target_pairs={{0,16},{1,17},{2,18},{3,19},{4,20},{5,21},{6,22},{7,23},{8,24},{9,... | collective-permute-start | bytes 3145736 | tf_op jit(solution)/shard_map/ppermute | solution.py:211
  349.6 53.3 %collective-permute-start.88 = (bf16[4,512,256]{2,1,0:T(8,128)(2,1)}, bf16[4,512,256]{2,1,0:T(8,128)(2,1)}, u32[]{:S(2)}, u32[]{:S(2)}) collective-permute-start(bf16[4,512,256]{2,1,0:T(8,128)(2,1)} %pad_maximum_fusion.10), channel_id=1, source_target_pairs={{0,8},{1,9},{2,10},{3,11},{4,12},{5,13},{6,14},{7,15},{8,0},{9,1},... | collective-permute-start | bytes 3145736 | tf_op jit(solution)/shard_map/ppermute | solution.py:211
  350.7 35.3 %collective-permute-start.73 = (bf16[4,512,256]{2,1,0:T(8,128)(2,1)}, bf16[4,512,256]{2,1,0:T(8,128)(2,1)}, u32[]{:S(2)}, u32[]{:S(2)}) collective-permute-start(bf16[4,512,256]{2,1,0:T(8,128)(2,1)} %pad_maximum_fusion.9), channel_id=1, source_target_pairs={{0,8},{1,9},{2,10},{3,11},{4,12},{5,13},{6,14},{7,15},{8,0},{9,1},... | collective-permute-start | bytes 3145736 | tf_op jit(solution)/shard_map/ppermute | solution.py:211
  421.9 38.4 %collective-permute-start.46 = (bf16[2048,256]{1,0:T(8,128)(2,1)S(1)}, bf16[2048,256]{1,0:T(8,128)(2,1)S(1)}, u32[]{:S(2)}, u32[]{:S(2)}) collective-permute-start(bf16[2048,256]{1,0:T(8,128)(2,1)S(1)} %copy-done.126), channel_id=1, source_target_pairs={{0,0},{1,1},{2,2},{3,3},{4,8},{5,9},{6,10},{7,11},{8,4},{9,5},{10,... | collective-permute-start | bytes 3145736 | tf_op jit(solution)/shard_map/ppermute | solution.py:211
  427.5 31.5 %collective-permute-start.60 = (bf16[2,512,256]{2,1,0:T(8,128)(2,1)S(1)}, bf16[2,512,256]{2,1,0:T(8,128)(2,1)S(1)}, u32[]{:S(2)}, u32[]{:S(2)}) collective-permute-start(bf16[2,512,256]{2,1,0:T(8,128)(2,1)S(1)} %slice.475), channel_id=1, source_target_pairs={{0,2},{1,3},{2,0},{3,1},{4,6},{5,7},{6,4},{7,5},{8,10},{9,11},{10,... | collective-permute-start | bytes 1572872 | tf_op jit(solution)/shard_map/ppermute | solution.py:211
  514.8 30.6 %collective-permute-start.110 = (bf16[4,512,256]{2,1,0:T(8,128)(2,1)}, bf16[4,512,256]{2,1,0:T(8,128)(2,1)S(1)}, u32[]{:S(2)}, u32[]{:S(2)}) collective-permute-start(bf16[4,512,256]{2,1,0:T(8,128)(2,1)} %pad_maximum_fusion.16), channel_id=1, source_target_pairs={{0,8},{1,9},{2,10},{3,11},{4,12},{5,13},{6,14},{7,15},{8,0},{9,1},... | collective-permute-start | bytes 3145736 | tf_op jit(solution)/shard_map/ppermute | solution.py:211
  525.0 57.7 %collective-permute-start.104 = (bf16[4,512,256]{2,1,0:T(8,128)(2,1)}, bf16[4,512,256]{2,1,0:T(8,128)(2,1)S(1)}, u32[]{:S(2)}, u32[]{:S(2)}) collective-permute-start(bf16[4,512,256]{2,1,0:T(8,128)(2,1)} %pad_maximum_fusion.14), channel_id=1, source_target_pairs={{0,8},{1,9},{2,10},{3,11},{4,12},{5,13},{6,14},{7,15},{8,0},{9,1},... | collective-permute-start | bytes 3145736 | tf_op jit(solution)/shard_map/ppermute | solution.py:211
  526.2 38.2 %collective-permute-start.107 = (bf16[4,512,256]{2,1,0:T(8,128)(2,1)}, bf16[4,512,256]{2,1,0:T(8,128)(2,1)}, u32[]{:S(2)}, u32[]{:S(2)}) collective-permute-start(bf16[4,512,256]{2,1,0:T(8,128)(2,1)} %pad_maximum_fusion.15), channel_id=1, source_target_pairs={{0,8},{1,9},{2,10},{3,11},{4,12},{5,13},{6,14},{7,15},{8,0},{9,1},... | collective-permute-start | bytes 3145736 | tf_op jit(solution)/shard_map/ppermute | solution.py:211
  564.2 51.7 %collective-permute-start.129 = (bf16[4,512,256]{2,1,0:T(8,128)(2,1)}, bf16[4,512,256]{2,1,0:T(8,128)(2,1)}, u32[]{:S(2)}, u32[]{:S(2)}) collective-permute-start(bf16[4,512,256]{2,1,0:T(8,128)(2,1)} %get-tuple-element.272), channel_id=1, source_target_pairs={{0,8},{1,9},{2,10},{3,11},{4,12},{5,13},{6,14},{7,15},{8,0},{9,1},... | collective-permute-start | bytes 3145736 | tf_op jit(solution)/shard_map/ppermute | solution.py:211
  606.5 160.9 %collective-permute-start.95 = (bf16[2048,256]{1,0:T(8,128)(2,1)}, bf16[2048,256]{1,0:T(8,128)(2,1)}, u32[]{:S(2)}, u32[]{:S(2)}) collective-permute-start(bf16[2048,256]{1,0:T(8,128)(2,1)} %pad_maximum_fusion.11), channel_id=1, source_target_pairs={{0,0},{1,1},{2,2},{3,3},{8,4},{9,5},{10,6},{11,7},{4,8},{5,9},{6,1... | collective-permute-start | bytes 3145736 | tf_op jit(solution)/shard_map/ppermute | solution.py:211
  619.6 29.4 %collective-permute-start.112 = (bf16[2,512,256]{2,1,0:T(8,128)(2,1)S(1)}, bf16[2,512,256]{2,1,0:T(8,128)(2,1)S(1)}, u32[]{:S(2)}, u32[]{:S(2)}) collective-permute-start(bf16[2,512,256]{2,1,0:T(8,128)(2,1)S(1)} %slice.504), channel_id=1, source_target_pairs={{0,2},{1,3},{2,0},{3,1},{4,6},{5,7},{6,4},{7,5},{8,10},{9,11},{10,... | collective-permute-start | bytes 1572872 | tf_op jit(solution)/shard_map/ppermute | solution.py:211
  620.4 30.4 %collective-permute-start.100 = (bf16[2,512,256]{2,1,0:T(8,128)(2,1)S(1)}, bf16[2,512,256]{2,1,0:T(8,128)(2,1)S(1)}, u32[]{:S(2)}, u32[]{:S(2)}) collective-permute-start(bf16[2,512,256]{2,1,0:T(8,128)(2,1)S(1)} %slice.394), channel_id=1, source_target_pairs={{0,1},{1,0},{2,3},{3,2},{4,5},{5,4},{6,7},{7,6},{8,9},{9,8},{10,11... | collective-permute-start | bytes 1572872 | tf_op jit(solution)/shard_map/ppermute | solution.py:211
  621.8 29.3 %collective-permute-start.121 = (bf16[2,512,256]{2,1,0:T(8,128)(2,1)S(1)}, bf16[2,512,256]{2,1,0:T(8,128)(2,1)S(1)}, u32[]{:S(2)}, u32[]{:S(2)}) collective-permute-start(bf16[2,512,256]{2,1,0:T(8,128)(2,1)S(1)} %slice.406), channel_id=1, source_target_pairs={{0,1},{1,0},{2,3},{3,2},{4,5},{5,4},{6,7},{7,6},{8,9},{9,8},{10,11... | collective-permute-start | bytes 1572872 | tf_op jit(solution)/shard_map/ppermute | solution.py:211
  687.8 48.4 %collective-permute-start.163 = (bf16[2,1,1024,512]{3,2,1,0:T(8,128)(2,1)}, bf16[2,1,1024,512]{3,2,1,0:T(8,128)(2,1)}, u32[]{:S(2)}, u32[]{:S(2)}) collective-permute-start(bf16[2,1,1024,512]{3,2,1,0:T(8,128)(2,1)} %get-tuple-element.325), channel_id=1, source_target_pairs={{0,16},{1,17},{2,18},{3,19},{4,20},{5,21},{6,22},{7,23},{8,24},{9,... | collective-permute-start | bytes 6291464 | tf_op jit(solution)/shard_map/ppermute | solution.py:211
  701.8 61.1 %collective-permute-start.142 = (bf16[2,512,256]{2,1,0:T(8,128)(2,1)}, bf16[2,512,256]{2,1,0:T(8,128)(2,1)S(1)}, u32[]{:S(2)}, u32[]{:S(2)}) collective-permute-start(bf16[2,512,256]{2,1,0:T(8,128)(2,1)} %pad_maximum_fusion.38), channel_id=1, source_target_pairs={{0,1},{1,0},{2,3},{3,2},{4,5},{5,4},{6,7},{7,6},{8,9},{9,8},{10,11... | collective-permute-start | bytes 1572872 | tf_op jit(solution)/shard_map/ppermute | solution.py:211
  705.0 58.4 %collective-permute-start.136 = (bf16[2,512,256]{2,1,0:T(8,128)(2,1)}, bf16[2,512,256]{2,1,0:T(8,128)(2,1)S(1)}, u32[]{:S(2)}, u32[]{:S(2)}) collective-permute-start(bf16[2,512,256]{2,1,0:T(8,128)(2,1)} %pad_maximum_fusion.37), channel_id=1, source_target_pairs={{0,2},{1,3},{2,0},{3,1},{4,6},{5,7},{6,4},{7,5},{8,10},{9,11},{10,... | collective-permute-start | bytes 1572872 | tf_op jit(solution)/shard_map/ppermute | solution.py:211
  709.2 55.4 %collective-permute-start.127 = (bf16[2,512,256]{2,1,0:T(8,128)(2,1)}, bf16[2,512,256]{2,1,0:T(8,128)(2,1)S(1)}, u32[]{:S(2)}, u32[]{:S(2)}) collective-permute-start(bf16[2,512,256]{2,1,0:T(8,128)(2,1)} %pad_maximum_fusion.36), channel_id=1, source_target_pairs={{0,1},{1,0},{2,3},{3,2},{4,5},{5,4},{6,7},{7,6},{8,9},{9,8},{10,11... | collective-permute-start | bytes 1572872 | tf_op jit(solution)/shard_map/ppermute | solution.py:211
  736.2 30.0 %collective-permute-start.118 = (bf16[2,512,256]{2,1,0:T(8,128)(2,1)}, bf16[2,512,256]{2,1,0:T(8,128)(2,1)S(1)}, u32[]{:S(2)}, u32[]{:S(2)}) collective-permute-start(bf16[2,512,256]{2,1,0:T(8,128)(2,1)} %pad_maximum_fusion.35), channel_id=1, source_target_pairs={{0,2},{1,3},{2,0},{3,1},{4,6},{5,7},{6,4},{7,5},{8,10},{9,11},{10,... | collective-permute-start | bytes 1572872 | tf_op jit(solution)/shard_map/ppermute | solution.py:211
  762.9 106.1 %collective-permute-start.164 = (bf16[2,2,512,1024]{3,2,1,0:T(8,128)(2,1)}, bf16[2,2,512,1024]{3,2,1,0:T(8,128)(2,1)}, u32[]{:S(2)}, u32[]{:S(2)}) collective-permute-start(bf16[2,2,512,1024]{3,2,1,0:T(8,128)(2,1)} %get-tuple-element.326), channel_id=1, source_target_pairs={{0,16},{1,17},{2,18},{3,19},{4,20},{5,21},{6,22},{7,23},{8,24},{9,... | collective-permute-start | bytes 12582920 | tf_op jit(solution)/shard_map/ppermute | solution.py:211
  771.6 53.9 %collective-permute-start.167 = (bf16[1,1024,512]{2,1,0:T(8,128)(2,1)}, bf16[1,1024,512]{2,1,0:T(8,128)(2,1)S(1)}, u32[]{:S(2)}, u32[]{:S(2)}) collective-permute-start(bf16[1,1024,512]{2,1,0:T(8,128)(2,1)} %get-tuple-element.332), channel_id=1, source_target_pairs={{0,0},{1,1},{2,2},{3,3},{8,4},{9,5},{10,6},{11,7},{4,8},{5,9},{6,1... | collective-permute-start | bytes 3145736 | tf_op jit(solution)/shard_map/ppermute | solution.py:211
  821.7 34.2 %collective-permute-start.144 = (f32[2,2048]{1,0:T(2,128)S(1)}, f32[2,2048]{1,0:T(2,128)S(1)}, u32[]{:S(2)}, u32[]{:S(2)}) collective-permute-start(f32[2,2048]{1,0:T(2,128)S(1)} %slice.414), channel_id=1, source_target_pairs={{0,1},{1,0},{2,3},{3,2},{4,5},{5,4},{6,7},{7,6},{8,9},{9,8},{10,11... | collective-permute-start | bytes 49160 | tf_op jit(solution)/shard_map/ppermute | solution.py:211
  823.7 31.6 %collective-permute-start.176 = (f32[4,256]{1,0:T(4,128)S(1)}, f32[4,256]{1,0:T(4,128)S(1)}, u32[]{:S(2)}, u32[]{:S(2)}) collective-permute-start(f32[4,256]{1,0:T(4,128)S(1)} %fusion.115), channel_id=1, source_target_pairs={{0,16},{1,17},{2,18},{3,19},{4,20},{5,21},{6,22},{7,23},{8,24},{9,... | collective-permute-start | bytes 12296 | tf_op jit(solution)/shard_map/ppermute | solution.py:211
  825.5 51.8 %collective-permute-start.168 = (bf16[1,1024,512]{2,1,0:T(8,128)(2,1)S(1)}, bf16[1,1024,512]{2,1,0:T(8,128)(2,1)S(1)}, u32[]{:S(2)}, u32[]{:S(2)}) collective-permute-start(bf16[1,1024,512]{2,1,0:T(8,128)(2,1)S(1)} %copy-done.115), channel_id=1, source_target_pairs={{4,0},{5,1},{6,2},{7,3},{12,4},{13,5},{14,6},{15,7},{0,8},{1,9},{2... | collective-permute-start | bytes 3145736 | tf_op jit(solution)/shard_map/ppermute | solution.py:211
  878.3 43.3 %collective-permute-start.169 = (bf16[2,512,1024]{2,1,0:T(8,128)(2,1)}, bf16[2,512,1024]{2,1,0:T(8,128)(2,1)S(1)}, u32[]{:S(2)}, u32[]{:S(2)}) collective-permute-start(bf16[2,512,1024]{2,1,0:T(8,128)(2,1)} %get-tuple-element.334), channel_id=1, source_target_pairs={{0,0},{1,1},{2,2},{3,3},{8,4},{9,5},{10,6},{11,7},{4,8},{5,9},{6,1... | collective-permute-start | bytes 6291464 | tf_op jit(solution)/shard_map/ppermute | solution.py:211
  920.5 36.1 %collective-permute-start.152 = (bf16[2,512,256]{2,1,0:T(8,128)(2,1)S(1)}, bf16[2,512,256]{2,1,0:T(8,128)(2,1)S(1)}, u32[]{:S(2)}, u32[]{:S(2)}) collective-permute-start(bf16[2,512,256]{2,1,0:T(8,128)(2,1)S(1)} %slice.521), channel_id=1, source_target_pairs={{0,2},{1,3},{2,0},{3,1},{4,6},{5,7},{6,4},{7,5},{8,10},{9,11},{10,... | collective-permute-start | bytes 1572872 | tf_op jit(solution)/shard_map/ppermute | solution.py:211
  921.7 46.1 %collective-permute-start.160 = (bf16[2,512,256]{2,1,0:T(8,128)(2,1)S(1)}, bf16[2,512,256]{2,1,0:T(8,128)(2,1)S(1)}, u32[]{:S(2)}, u32[]{:S(2)}) collective-permute-start(bf16[2,512,256]{2,1,0:T(8,128)(2,1)S(1)} %slice.527), channel_id=1, source_target_pairs={{0,2},{1,3},{2,0},{3,1},{4,6},{5,7},{6,4},{7,5},{8,10},{9,11},{10,... | collective-permute-start | bytes 1572872 | tf_op jit(solution)/shard_map/ppermute | solution.py:211
  923.6 53.6 %collective-permute-start.170 = (bf16[2,512,1024]{2,1,0:T(8,128)(2,1)S(1)}, bf16[2,512,1024]{2,1,0:T(8,128)(2,1)S(1)}, u32[]{:S(2)}, u32[]{:S(2)}) collective-permute-start(bf16[2,512,1024]{2,1,0:T(8,128)(2,1)S(1)} %copy-done.90), channel_id=1, source_target_pairs={{4,0},{5,1},{6,2},{7,3},{12,4},{13,5},{14,6},{15,7},{0,8},{1,9},{2... | collective-permute-start | bytes 6291464 | tf_op jit(solution)/shard_map/ppermute | solution.py:211
  934.8 33.6 %collective-permute-start.156 = (bf16[2,512,256]{2,1,0:T(8,128)(2,1)S(1)}, bf16[2,512,256]{2,1,0:T(8,128)(2,1)S(1)}, u32[]{:S(2)}, u32[]{:S(2)}) collective-permute-start(bf16[2,512,256]{2,1,0:T(8,128)(2,1)S(1)} %slice.428), channel_id=1, source_target_pairs={{0,1},{1,0},{2,3},{3,2},{4,5},{5,4},{6,7},{7,6},{8,9},{9,8},{10,11... | collective-permute-start | bytes 1572872 | tf_op jit(solution)/shard_map/ppermute | solution.py:211
  935.3 41.8 %collective-permute-start.166 = (bf16[2,3,512,256]{3,2,1,0:T(8,128)(2,1)S(1)}, bf16[2,3,512,256]{3,2,1,0:T(8,128)(2,1)S(1)}, u32[]{:S(2)}, u32[]{:S(2)}) collective-permute-start(bf16[2,3,512,256]{3,2,1,0:T(8,128)(2,1)S(1)} %copy-done.124), channel_id=1, source_target_pairs={{0,16},{1,17},{2,18},{3,19},{4,20},{5,21},{6,22},{7,23},{8,24},{9,... | collective-permute-start | bytes 4718600 | tf_op jit(solution)/shard_map/ppermute | solution.py:211
  995.8 29.9 %collective-permute-start.154 = (bf16[512,256]{1,0:T(8,128)(2,1)S(1)}, bf16[512,256]{1,0:T(8,128)(2,1)S(1)}, u32[]{:S(2)}, u32[]{:S(2)}) collective-permute-start(bf16[512,256]{1,0:T(8,128)(2,1)S(1)} %fusion.32), channel_id=1, source_target_pairs={{0,0},{1,1},{2,2},{3,3},{8,4},{9,5},{10,6},{11,7},{4,8},{5,9},{6,1... | collective-permute-start | bytes 786440 | tf_op jit(solution)/shard_map/ppermute | solution.py:211
  1000.9 53.1 %collective-permute-start.174 = (bf16[3,512,256]{2,1,0:T(8,128)(2,1)S(1)}, bf16[3,512,256]{2,1,0:T(8,128)(2,1)S(1)}, u32[]{:S(2)}, u32[]{:S(2)}) collective-permute-start(bf16[3,512,256]{2,1,0:T(8,128)(2,1)S(1)} %get-tuple-element.339), channel_id=1, source_target_pairs={{4,0},{5,1},{6,2},{7,3},{12,4},{13,5},{14,6},{15,7},{0,8},{1,9},{2... | collective-permute-start | bytes 2359304 | tf_op jit(solution)/shard_map/ppermute | solution.py:211
  (261 other events, 3787.0 us)

commit v2 on v1

--- a/solution.py
+++ b/solution.py
@@ -837,12 +837,13 @@
         total = reduce(*total, index)
         total = (hidden_cots[index] + total).astype(LOW)
         input_grads.append(send(total, layout.exchange_back(0)))
-    input_grad = jnp.concatenate(input_grads)
     grad_query, grad_key, grad_value = owners_sum(
         *matmul_tall(token_wide, [[query_back], [key_back], [value_back]], True, 512)
     )
 
     gains = jnp.concatenate([gain_sums[:2], gain_attn[None], gain_ffn[None]])
+    gains, input_grads[0] = lax.optimization_barrier((gains, input_grads[0]))
+    input_grad = jnp.concatenate(input_grads)
     for mask in [1, *group_bits]:
         gains = gains + send(gains, layout.across_groups(mask))
     gains = send(gains, layout.exchange_back(0))

time: 1070 us -> 1060 us (level)
  waiting for transfers between devices: 364 us -> 328 us
  starting transfers between devices: 270 us -> 303 us
    ppermute x178, waiting for transfers between devices: 364 us -> 328 us  [send(): return lax.ppermute(values, ('rows', 'cols'), pairs)]
    ppermute x178, starting transfers between devices: 270 us -> 303 us  [send(): return lax.ppermute(values, ('rows', 'cols'), pairs)]
  transfers between devices with their start and end apart: 178 -> 178, of which waited for: 59 -> 60; matrix products, arithmetic and copies ran while one was open for 8% -> 8% of each run, Pallas kernels for 29% -> 29%
where the time goes in v2:
time: 1060 us; the launch traced here: 1050 us
  waiting for transfers between devices  328 us (31%)
  Pallas kernels  318 us (30%)
  starting transfers between devices  303 us (29%)
  other arithmetic  77.2 us (7%)
  local copies, waits for them, and re-layouts  17.2 us (2%)
    ppermute x178, waiting for transfers between devices, send(): return lax.ppermute(values, ('rows', 'cols'), pairs)  328 us
    ppermute x178, starting transfers between devices, send(): return lax.ppermute(values, ('rows', 'cols'), pairs)  303 us
    pallas_call x16, Pallas kernels, matmul_rows(): pl.pallas_call(body, grid_spec=pltpu.PrefetchScalarGridSpec(num_scalar_pr...  110 us
    pallas_call x16, Pallas kernels, matmul_columns(): pl.pallas_call(functools.partial(columns_kernel, len(lefts), shards, per,...  99.3 us
    pallas_call x4, Pallas kernels, matmul_tall(): pl.pallas_call(functools.partial(tall_kernel, [len(g) for g in groups], h...  59.4 us
  transfers between devices with their start and end apart: 178, of which 60 were waited for; matrix products, arithmetic and copies ran while one was open for 8% of the time, Pallas kernels for 29%

profile of v2, /device:TPU:0, one launch (start us, length us, event | category | flops | bytes accessed | tf_op | source)
XLA Modules:
  0.0 1046.7 jit_solution(14249530911081662469)
XLA Ops:
  14.7 35.2 %collective-permute-start.6 = (bf16[3,512,256]{2,1,0:T(8,128)(2,1)S(1)}, bf16[3,512,256]{2,1,0:T(8,128)(2,1)S(1)}, u32[]{:S(2)}, u32[]{:S(2)}) collective-permute-start(bf16[3,512,256]{2,1,0:T(8,128)(2,1)S(1)} %pad_maximum_fusion.22), channel_id=1, source_target_pairs={{0,4},{1,5},{2,6},{3,7},{4,12},{5,13},{6,14},{7,15},{8,0},{9,1},{1... | collective-permute-start | bytes 2359304 | tf_op jit(solution)/shard_map/ppermute | solution.py:211
  63.5 8.4 collective-permute-done.16.refs_2_
  90.7 7.5 collective-permute-done.8.refs_7_.refs_6_
  130.8 12.3 %collective-permute-start.23 = (bf16[1,256,512]{2,1,0:T(8,128)(2,1)S(1)}, bf16[1,256,512]{2,1,0:T(8,128)(2,1)S(1)}, u32[]{:S(2)}, u32[]{:S(2)}) collective-permute-start(bf16[1,256,512]{2,1,0:T(8,128)(2,1)S(1)} %bitcast.533), channel_id=1, source_target_pairs={{0,4},{1,5},{2,6},{3,7},{4,12},{5,13},{6,14},{7,15},{8,0},{9,1},{1... | collective-permute-start | bytes 786440 | tf_op jit(solution)/shard_map/ppermute | solution.py:211
  194.7 10.3 collective-permute-start.36
  210.1 7.1 collective-permute-done.51
  221.7 23.8 %collective-permute-done.81 = bf16[2,512,256]{2,1,0:T(8,128)(2,1)S(1)} collective-permute-done((bf16[2,512,256]{2,1,0:T(8,128)(2,1)S(1)}, bf16[2,512,256]{2,1,0:T(8,128)(2,1)S(1)}, u32[]{:S(2)}, u32[]{:S(2)}) %collective-permute-start.81) | collective-permute-done | bytes 524320 | tf_op jit(solution)/shard_map/ppermute | solution.py:211
  249.0 8.7 collective-permute-done.67
  274.3 8.1 collective-permute-done.32.refs_1_
  283.5 16.1 %collective-permute-start.40 = (bf16[1,1024,512]{2,1,0:T(8,128)(2,1)S(1)}, bf16[1,1024,512]{2,1,0:T(8,128)(2,1)}, u32[]{:S(2)}, u32[]{:S(2)}) collective-permute-start(bf16[1,1024,512]{2,1,0:T(8,128)(2,1)S(1)} %bitcast.531), channel_id=1, source_target_pairs={{0,4},{1,5},{2,6},{3,7},{4,12},{5,13},{6,14},{7,15},{8,0},{9,1},{1... | collective-permute-start | bytes 3145736 | tf_op jit(solution)/shard_map/ppermute | solution.py:211
  314.0 15.1 %collective-permute-done.71.refs_1_ = bf16[1,512,256]{2,1,0:T(8,128)(2,1)S(1)} collective-permute-done((bf16[1,512,256]{2,1,0:T(8,128)(2,1)S(1)}, bf16[1,512,256]{2,1,0:T(8,128)(2,1)S(1)}, u32[]{:S(2)}, u32[]{:S(2)}) %collective-permute-start.71) | collective-permute-done | bytes 262176 | tf_op jit(solution)/shard_map/ppermute | solution.py:211
  330.3 10.0 collective-permute-done.57.refs_2_
  340.5 6.6 collective-permute-done.87.refs_2_
  349.8 10.4 shard_map.244
  367.7 10.4 shard_map.248
  384.6 10.4 shard_map.252
  401.5 10.4 shard_map.256
  411.9 6.5 shard_map.257
  427.2 19.2 %collective-permute-done.90 = bf16[2,512,256]{2,1,0:T(8,128)(2,1)S(1)} collective-permute-done((bf16[2,512,256]{2,1,0:T(8,128)(2,1)S(1)}, bf16[2,512,256]{2,1,0:T(8,128)(2,1)S(1)}, u32[]{:S(2)}, u32[]{:S(2)}) %collective-permute-start.90) | collective-permute-done | bytes 524320 | tf_op jit(solution)/shard_map/ppermute | solution.py:211
  451.1 7.0 collective-permute-done.60
  495.9 10.3 collective-permute-done.106.refs_2_
  514.5 9.0 collective-permute-done.97.refs_2_
  527.2 7.7 shard_map.258
  534.9 10.1 shard_map.259
  546.0 7.7 shard_map.260
  553.7 10.1 shard_map.261
  563.9 7.7 shard_map.262
  571.6 10.4 shard_map.263
  582.9 7.7 shard_map.264
  590.6 10.2 shard_map.265
  608.7 9.5 collective-permute-done.127
  619.4 9.2 collective-permute-done.109
  653.7 16.7 %shard_map.279 = (bf16[2,1,1024,512]{3,2,1,0:T(8,128)(2,1)}, bf16[2,1,1024,512]{3,2,1,0:T(8,128)(2,1)}) custom-call(bf16[4,2048,512]{2,1,0:T(8,128)(2,1)} %get-tuple-element.327.wide, bf16[512,1024]{1,0:T(8,128)(2,1)S(1)} %copy-done.13, bf16[512,1024]{1,0:T(8,128)(2,1)} %get-tuple-element.226.refs_0_.refs_1_, ...), custom_call_target="tpu_custom_call" | custom-call | flops 8589934592 | bytes 16777216 | tf_op jit(solution)/shard_map/pallas_call | solution.py:440
  694.1 9.4 collective-permute-done.142.refs_2_
  703.5 9.5 collective-permute-start.95
  719.1 24.9 %shard_map.278 = (bf16[2,2,512,1024]{3,2,1,0:T(8,128)(2,1)}, bf16[2,2,512,1024]{3,2,1,0:T(8,128)(2,1)}) custom-call(bf16[4,2048,512]{2,1,0:T(8,128)(2,1)} %get-tuple-element.325.wide, bf16[512,1024]{1,0:T(8,128)(2,1)S(1)} %copy-done.12, bf16[512,1024]{1,0:T(8,128)(2,1)} %get-tuple-element.271.refs_0_.refs_1_, ...), custom_call_target="tpu_custom_call" | custom-call | flops 17179869184 | bytes 25165824 | tf_op jit(solution)/shard_map/pallas_call | solution.py:440
  767.4 18.0 %shard_map.270 = (f32[2048,256]{1,0:T(8,128)}, f32[2048,256]{1,0:T(8,128)}, f32[2048,256]{1,0:T(8,128)}) custom-call(s32[4]{0:T(128)S(1)} %and_select_fusion.lows, s32[1,2048]{1,0:T(1,128)S(1)} %bitcast.402, bf16[2048,256]{1,0:T(8,128)(2,1)S(1)} %get-tuple-element.241.query, bf16[2048,256]{1,0:T(8,128)(2,1)} %get-tuple-element.196.key, ...), custom_call_target="tpu_custom_call" | custom-call | flops 10737418240 | bytes 10485760 | tf_op jit(solution)/shard_map/pallas_call | solution.py:133
  785.5 7.6 shard_map.271
  803.1 6.5 shard_map.277
  828.2 9.3 collective-permute-done.164
  863.4 11.2 %shard_map.276 = (bf16[2,3,512,256]{3,2,1,0:T(8,128)(2,1)}, bf16[2,3,512,256]{3,2,1,0:T(8,128)(2,1)}) custom-call(bf16[4,2048,512]{2,1,0:T(8,128)(2,1)} %get-tuple-element.320.wide, bf16[2048,256]{1,0:T(8,128)(2,1)S(1)} %copy-done.2, bf16[2048,256]{1,0:T(8,128)(2,1)} %get-tuple-element.427.refs_1_, bf16[2048,256]{1,0:T(8,128)(2,1)} %convert_element_type.729.refs_2_), custom_call_target="tpu_custom_call" | custom-call | flops 6442450944 | bytes 14680064 | tf_op jit(solution)/shard_map/pallas_call | solution.py:440
  883.7 26.4 %collective-permute-done.152 = bf16[2,512,256]{2,1,0:T(8,128)(2,1)S(1)} collective-permute-done((bf16[2,512,256]{2,1,0:T(8,128)(2,1)S(1)}, bf16[2,512,256]{2,1,0:T(8,128)(2,1)S(1)}, u32[]{:S(2)}, u32[]{:S(2)}) %collective-permute-start.152) | collective-permute-done | bytes 524320 | tf_op jit(solution)/shard_map/ppermute | solution.py:211
  910.3 11.0 %collective-permute-done.160 = bf16[2,512,256]{2,1,0:T(8,128)(2,1)S(1)} collective-permute-done((bf16[2,512,256]{2,1,0:T(8,128)(2,1)S(1)}, bf16[2,512,256]{2,1,0:T(8,128)(2,1)S(1)}, u32[]{:S(2)}, u32[]{:S(2)}) %collective-permute-start.160) | collective-permute-done | bytes 524320 | tf_op jit(solution)/shard_map/ppermute | solution.py:211
  941.4 28.7 %collective-permute-start.175 = (f32[4,256]{1,0:T(4,128)S(1)}, f32[4,256]{1,0:T(4,128)S(1)}, u32[]{:S(2)}, u32[]{:S(2)}) collective-permute-start(f32[4,256]{1,0:T(4,128)S(1)} %pad_maximum_fusion.46), channel_id=1, source_target_pairs={{0,4},{1,5},{2,6},{3,7},{4,0},{5,1},{6,2},{7,3},{8,12},{9,13},{10,... | collective-permute-start | bytes 12296 | tf_op jit(solution)/shard_map/ppermute | solution.py:211
  971.5 10.5 %collective-permute-start.172 = (bf16[1,256,512]{2,1,0:T(8,128)(2,1)S(1)}, bf16[1,256,512]{2,1,0:T(8,128)(2,1)S(1)}, u32[]{:S(2)}, u32[]{:S(2)}) collective-permute-start(bf16[1,256,512]{2,1,0:T(8,128)(2,1)S(1)} %get-tuple-element.341), channel_id=1, source_target_pairs={{4,0},{5,1},{6,2},{7,3},{12,4},{13,5},{14,6},{15,7},{0,8},{1,9},{2... | collective-permute-start | bytes 786440 | tf_op jit(solution)/shard_map/ppermute | solution.py:211
  982.1 6.8 collective-permute-done.172
  997.3 27.5 %collective-permute-start.174 = (bf16[3,512,256]{2,1,0:T(8,128)(2,1)S(1)}, bf16[3,512,256]{2,1,0:T(8,128)(2,1)S(1)}, u32[]{:S(2)}, u32[]{:S(2)}) collective-permute-start(bf16[3,512,256]{2,1,0:T(8,128)(2,1)S(1)} %get-tuple-element.343), channel_id=1, source_target_pairs={{4,0},{5,1},{6,2},{7,3},{12,4},{13,5},{14,6},{15,7},{0,8},{1,9},{2... | collective-permute-start | bytes 2359304 | tf_op jit(solution)/shard_map/ppermute | solution.py:211
  1029.2 13.8 %collective-permute-done.174 = bf16[3,512,256]{2,1,0:T(8,128)(2,1)S(1)} collective-permute-done((bf16[3,512,256]{2,1,0:T(8,128)(2,1)S(1)}, bf16[3,512,256]{2,1,0:T(8,128)(2,1)S(1)}, u32[]{:S(2)}, u32[]{:S(2)}) %collective-permute-start.174) | collective-permute-done | bytes 786464 | tf_op jit(solution)/shard_map/ppermute | solution.py:211
  (837 shorter events, 452.0 us)
Async XLA Ops:
  4.6 46.9 %collective-permute-start.15 = (bf16[1,512,256]{2,1,0:T(8,128)(2,1)S(1)}, bf16[1,512,256]{2,1,0:T(8,128)(2,1)S(1)}, u32[]{:S(2)}, u32[]{:S(2)}) collective-permute-start(bf16[1,512,256]{2,1,0:T(8,128)(2,1)S(1)} %get-tuple-element.398.refs_0_), channel_id=1, source_target_pairs={{0,2},{1,3},{2,0},{3,1},{4,6},{5,7},{6,4},{7,5},{8,10},{9,11},{10,... | collective-permute-start | bytes 786440 | tf_op jit(solution)/shard_map/ppermute | solution.py:211
  7.6 44.3 %collective-permute-start.12 = (bf16[1,512,256]{2,1,0:T(8,128)(2,1)S(1)}, bf16[1,512,256]{2,1,0:T(8,128)(2,1)S(1)}, u32[]{:S(2)}, u32[]{:S(2)}) collective-permute-start(bf16[1,512,256]{2,1,0:T(8,128)(2,1)S(1)} %get-tuple-element.399.refs_0_), channel_id=1, source_target_pairs={{0,1},{1,0},{2,3},{3,2},{4,5},{5,4},{6,7},{7,6},{8,9},{9,8},{10,11... | collective-permute-start | bytes 786440 | tf_op jit(solution)/shard_map/ppermute | solution.py:211
  9.2 44.5 %collective-permute-start.9 = (bf16[1,512,256]{2,1,0:T(8,128)(2,1)S(1)}, bf16[1,512,256]{2,1,0:T(8,128)(2,1)S(1)}, u32[]{:S(2)}, u32[]{:S(2)}) collective-permute-start(bf16[1,512,256]{2,1,0:T(8,128)(2,1)S(1)} %get-tuple-element.400.refs_0_), channel_id=1, source_target_pairs={{0,2},{1,3},{2,0},{3,1},{4,6},{5,7},{6,4},{7,5},{8,10},{9,11},{10,... | collective-permute-start | bytes 786440 | tf_op jit(solution)/shard_map/ppermute | solution.py:211
  14.7 63.2 %collective-permute-start.6 = (bf16[3,512,256]{2,1,0:T(8,128)(2,1)S(1)}, bf16[3,512,256]{2,1,0:T(8,128)(2,1)S(1)}, u32[]{:S(2)}, u32[]{:S(2)}) collective-permute-start(bf16[3,512,256]{2,1,0:T(8,128)(2,1)S(1)} %pad_maximum_fusion.22), channel_id=1, source_target_pairs={{0,4},{1,5},{2,6},{3,7},{4,12},{5,13},{6,14},{7,15},{8,0},{9,1},{1... | collective-permute-start | bytes 2359304 | tf_op jit(solution)/shard_map/ppermute | solution.py:211
  87.9 29.6 %collective-permute-start.4 = (bf16[4,512,256]{2,1,0:T(8,128)(2,1)S(1)}, bf16[4,512,256]{2,1,0:T(8,128)(2,1)S(1)}, u32[]{:S(2)}, u32[]{:S(2)}) collective-permute-start(bf16[4,512,256]{2,1,0:T(8,128)(2,1)S(1)} %pad_maximum_fusion.1), channel_id=1, source_target_pairs={{0,8},{1,9},{2,10},{3,11},{4,12},{5,13},{6,14},{7,15},{8,0},{9,1},... | collective-permute-start | bytes 3145736 | tf_op jit(solution)/shard_map/ppermute | solution.py:211
  98.1 55.1 %collective-permute-start.21 = (f32[4,256]{1,0:T(4,128)S(1)}, f32[4,256]{1,0:T(4,128)S(1)}, u32[]{:S(2)}, u32[]{:S(2)}) collective-permute-start(f32[4,256]{1,0:T(4,128)S(1)} %pad_maximum_fusion.41), channel_id=1, source_target_pairs={{0,0},{1,1},{2,2},{3,3},{4,8},{5,9},{6,10},{7,11},{8,4},{9,5},{10,... | collective-permute-start | bytes 12296 | tf_op jit(solution)/shard_map/ppermute | solution.py:211
  98.8 29.0 %collective-permute-start.1 = (s32[1,2048]{1,0:T(1,128)S(1)}, s32[1,2048]{1,0:T(1,128)S(1)}, u32[]{:S(2)}, u32[]{:S(2)}) collective-permute-start(s32[1,2048]{1,0:T(1,128)S(1)} %copy-done.132), channel_id=1, source_target_pairs={{0,0},{1,1},{2,2},{3,3},{4,8},{5,9},{6,10},{7,11},{8,4},{9,5},{10,... | collective-permute-start | bytes 24584 | tf_op jit(solution)/shard_map/ppermute | solution.py:211
  147.0 46.0 %collective-permute-start.35 = (bf16[2,512,1024]{2,1,0:T(8,128)(2,1)}, bf16[2,512,1024]{2,1,0:T(8,128)(2,1)S(1)}, u32[]{:S(2)}, u32[]{:S(2)}) collective-permute-start(bf16[2,512,1024]{2,1,0:T(8,128)(2,1)} %pad_maximum_fusion), channel_id=1, source_target_pairs={{0,0},{1,1},{2,2},{3,3},{4,8},{5,9},{6,10},{7,11},{8,4},{9,5},{10,... | collective-permute-start | bytes 6291464 | tf_op jit(solution)/shard_map/ppermute | solution.py:211
  193.0 65.3 %collective-permute-start.37 = (bf16[2,512,1024]{2,1,0:T(8,128)(2,1)S(1)}, bf16[2,512,1024]{2,1,0:T(8,128)(2,1)S(1)}, u32[]{:S(2)}, u32[]{:S(2)}) collective-permute-start(bf16[2,512,1024]{2,1,0:T(8,128)(2,1)S(1)} %collective-permute-done.35.refs_4_.refs_2_), channel_id=1, source_target_pairs={{0,16},{1,17},{2,18},{3,19},{4,20},{5,21},{6,22},{7,23},{8,24},{9,... | collective-permute-start | bytes 6291464 | tf_op jit(solution)/shard_map/ppermute | solution.py:211
  194.7 65.3 %collective-permute-start.36 = (bf16[2,512,1024]{2,1,0:T(8,128)(2,1)S(1)}, bf16[2,512,1024]{2,1,0:T(8,128)(2,1)S(1)}, u32[]{:S(2)}, u32[]{:S(2)}) collective-permute-start(bf16[2,512,1024]{2,1,0:T(8,128)(2,1)S(1)} %copy-done.93), channel_id=1, source_target_pairs={{0,4},{1,5},{2,6},{3,7},{4,12},{5,13},{6,14},{7,15},{8,0},{9,1},{1... | collective-permute-start | bytes 6291464 | tf_op jit(solution)/shard_map/ppermute | solution.py:211
  207.4 38.1 %collective-permute-start.81 = (bf16[2,512,256]{2,1,0:T(8,128)(2,1)S(1)}, bf16[2,512,256]{2,1,0:T(8,128)(2,1)S(1)}, u32[]{:S(2)}, u32[]{:S(2)}) collective-permute-start(bf16[2,512,256]{2,1,0:T(8,128)(2,1)S(1)} %slice.487), channel_id=1, source_target_pairs={{0,2},{1,3},{2,0},{3,1},{4,6},{5,7},{6,4},{7,5},{8,10},{9,11},{10,... | collective-permute-start | bytes 1572872 | tf_op jit(solution)/shard_map/ppermute | solution.py:211
  217.2 31.0 %collective-permute-start.27 = (bf16[2,512,256]{2,1,0:T(8,128)(2,1)S(1)}, bf16[2,512,256]{2,1,0:T(8,128)(2,1)S(1)}, u32[]{:S(2)}, u32[]{:S(2)}) collective-permute-start(bf16[2,512,256]{2,1,0:T(8,128)(2,1)S(1)} %slice.351), channel_id=1, source_target_pairs={{0,1},{1,0},{2,3},{3,2},{4,5},{5,4},{6,7},{7,6},{8,9},{9,8},{10,11... | collective-permute-start | bytes 1572872 | tf_op jit(solution)/shard_map/ppermute | solution.py:211
  260.1 44.3 %collective-permute-start.38 = (bf16[2,512,1024]{2,1,0:T(8,128)(2,1)S(1)}, bf16[2,512,1024]{2,1,0:T(8,128)(2,1)S(1)}, u32[]{:S(2)}, u32[]{:S(2)}) collective-permute-start(bf16[2,512,1024]{2,1,0:T(8,128)(2,1)S(1)} %collective-permute-done.36.refs_5_.refs_3_), channel_id=1, source_target_pairs={{0,16},{1,17},{2,18},{3,19},{4,20},{5,21},{6,22},{7,23},{8,24},{9,... | collective-permute-start | bytes 6291464 | tf_op jit(solution)/shard_map/ppermute | solution.py:211
  282.5 29.6 %collective-permute-start.33 = (bf16[2,512,256]{2,1,0:T(8,128)(2,1)S(1)}, bf16[2,512,256]{2,1,0:T(8,128)(2,1)S(1)}, u32[]{:S(2)}, u32[]{:S(2)}) collective-permute-start(bf16[2,512,256]{2,1,0:T(8,128)(2,1)S(1)} %pad_maximum_fusion.27), channel_id=1, source_target_pairs={{0,1},{1,0},{2,3},{3,2},{4,5},{5,4},{6,7},{7,6},{8,9},{9,8},{10,11... | collective-permute-start | bytes 1572872 | tf_op jit(solution)/shard_map/ppermute | solution.py:211
  283.5 45.6 %collective-permute-start.40 = (bf16[1,1024,512]{2,1,0:T(8,128)(2,1)S(1)}, bf16[1,1024,512]{2,1,0:T(8,128)(2,1)}, u32[]{:S(2)}, u32[]{:S(2)}) collective-permute-start(bf16[1,1024,512]{2,1,0:T(8,128)(2,1)S(1)} %bitcast.531), channel_id=1, source_target_pairs={{0,4},{1,5},{2,6},{3,7},{4,12},{5,13},{6,14},{7,15},{8,0},{9,1},{1... | collective-permute-start | bytes 3145736 | tf_op jit(solution)/shard_map/ppermute | solution.py:211
  313.9 35.9 %collective-permute-start.34 = (bf16[4,512,256]{2,1,0:T(8,128)(2,1)S(1)}, bf16[4,512,256]{2,1,0:T(8,128)(2,1)}, u32[]{:S(2)}, u32[]{:S(2)}) collective-permute-start(bf16[4,512,256]{2,1,0:T(8,128)(2,1)S(1)} %pad_maximum_fusion.7), channel_id=1, source_target_pairs={{0,8},{1,9},{2,10},{3,11},{4,12},{5,13},{6,14},{7,15},{8,0},{9,1},... | collective-permute-start | bytes 3145736 | tf_op jit(solution)/shard_map/ppermute | solution.py:211
  330.3 30.0 %collective-permute-start.42 = (bf16[1,1024,512]{2,1,0:T(8,128)(2,1)}, bf16[1,1024,512]{2,1,0:T(8,128)(2,1)S(1)}, u32[]{:S(2)}, u32[]{:S(2)}) collective-permute-start(bf16[1,1024,512]{2,1,0:T(8,128)(2,1)} %collective-permute-done.40.refs_2_.refs_5_), channel_id=1, source_target_pairs={{0,16},{1,17},{2,18},{3,19},{4,20},{5,21},{6,22},{7,23},{8,24},{9,... | collective-permute-start | bytes 3145736 | tf_op jit(solution)/shard_map/ppermute | solution.py:211
  348.2 53.3 %collective-permute-start.88 = (bf16[4,512,256]{2,1,0:T(8,128)(2,1)}, bf16[4,512,256]{2,1,0:T(8,128)(2,1)}, u32[]{:S(2)}, u32[]{:S(2)}) collective-permute-start(bf16[4,512,256]{2,1,0:T(8,128)(2,1)} %pad_maximum_fusion.10), channel_id=1, source_target_pairs={{0,8},{1,9},{2,10},{3,11},{4,12},{5,13},{6,14},{7,15},{8,0},{9,1},... | collective-permute-start | bytes 3145736 | tf_op jit(solution)/shard_map/ppermute | solution.py:211
  349.3 35.3 %collective-permute-start.73 = (bf16[4,512,256]{2,1,0:T(8,128)(2,1)}, bf16[4,512,256]{2,1,0:T(8,128)(2,1)}, u32[]{:S(2)}, u32[]{:S(2)}) collective-permute-start(bf16[4,512,256]{2,1,0:T(8,128)(2,1)} %pad_maximum_fusion.9), channel_id=1, source_target_pairs={{0,8},{1,9},{2,10},{3,11},{4,12},{5,13},{6,14},{7,15},{8,0},{9,1},... | collective-permute-start | bytes 3145736 | tf_op jit(solution)/shard_map/ppermute | solution.py:211
  419.4 41.5 %collective-permute-start.46 = (bf16[2048,256]{1,0:T(8,128)(2,1)}, bf16[2048,256]{1,0:T(8,128)(2,1)S(1)}, u32[]{:S(2)}, u32[]{:S(2)}) collective-permute-start(bf16[2048,256]{1,0:T(8,128)(2,1)} %param.27), channel_id=1, source_target_pairs={{0,0},{1,1},{2,2},{3,3},{4,8},{5,9},{6,10},{7,11},{8,4},{9,5},{10,... | collective-permute-start | bytes 3145736 | tf_op jit(solution)/shard_map/ppermute | solution.py:211
  426.1 31.9 %collective-permute-start.60 = (bf16[2,512,256]{2,1,0:T(8,128)(2,1)S(1)}, bf16[2,512,256]{2,1,0:T(8,128)(2,1)S(1)}, u32[]{:S(2)}, u32[]{:S(2)}) collective-permute-start(bf16[2,512,256]{2,1,0:T(8,128)(2,1)S(1)} %slice.475), channel_id=1, source_target_pairs={{0,2},{1,3},{2,0},{3,1},{4,6},{5,7},{6,4},{7,5},{8,10},{9,11},{10,... | collective-permute-start | bytes 1572872 | tf_op jit(solution)/shard_map/ppermute | solution.py:211
  514.5 30.5 %collective-permute-start.104 = (bf16[4,512,256]{2,1,0:T(8,128)(2,1)}, bf16[4,512,256]{2,1,0:T(8,128)(2,1)S(1)}, u32[]{:S(2)}, u32[]{:S(2)}) collective-permute-start(bf16[4,512,256]{2,1,0:T(8,128)(2,1)} %pad_maximum_fusion.15), channel_id=1, source_target_pairs={{0,8},{1,9},{2,10},{3,11},{4,12},{5,13},{6,14},{7,15},{8,0},{9,1},... | collective-permute-start | bytes 3145736 | tf_op jit(solution)/shard_map/ppermute | solution.py:211
  524.6 57.4 %collective-permute-start.98 = (bf16[4,512,256]{2,1,0:T(8,128)(2,1)}, bf16[4,512,256]{2,1,0:T(8,128)(2,1)S(1)}, u32[]{:S(2)}, u32[]{:S(2)}) collective-permute-start(bf16[4,512,256]{2,1,0:T(8,128)(2,1)} %pad_maximum_fusion.13), channel_id=1, source_target_pairs={{0,8},{1,9},{2,10},{3,11},{4,12},{5,13},{6,14},{7,15},{8,0},{9,1},... | collective-permute-start | bytes 3145736 | tf_op jit(solution)/shard_map/ppermute | solution.py:211
  525.7 38.2 %collective-permute-start.101 = (bf16[4,512,256]{2,1,0:T(8,128)(2,1)}, bf16[4,512,256]{2,1,0:T(8,128)(2,1)}, u32[]{:S(2)}, u32[]{:S(2)}) collective-permute-start(bf16[4,512,256]{2,1,0:T(8,128)(2,1)} %pad_maximum_fusion.14), channel_id=1, source_target_pairs={{0,8},{1,9},{2,10},{3,11},{4,12},{5,13},{6,14},{7,15},{8,0},{9,1},... | collective-permute-start | bytes 3145736 | tf_op jit(solution)/shard_map/ppermute | solution.py:211
  563.9 37.9 %collective-permute-start.126 = (bf16[4,512,256]{2,1,0:T(8,128)(2,1)}, bf16[4,512,256]{2,1,0:T(8,128)(2,1)}, u32[]{:S(2)}, u32[]{:S(2)}) collective-permute-start(bf16[4,512,256]{2,1,0:T(8,128)(2,1)} %get-tuple-element.274), channel_id=1, source_target_pairs={{0,8},{1,9},{2,10},{3,11},{4,12},{5,13},{6,14},{7,15},{8,0},{9,1},... | collective-permute-start | bytes 3145736 | tf_op jit(solution)/shard_map/ppermute | solution.py:211
  670.4 48.7 %collective-permute-start.163 = (bf16[2,1,1024,512]{3,2,1,0:T(8,128)(2,1)}, bf16[2,1,1024,512]{3,2,1,0:T(8,128)(2,1)}, u32[]{:S(2)}, u32[]{:S(2)}) collective-permute-start(bf16[2,1,1024,512]{3,2,1,0:T(8,128)(2,1)} %get-tuple-element.329), channel_id=1, source_target_pairs={{0,16},{1,17},{2,18},{3,19},{4,20},{5,21},{6,22},{7,23},{8,24},{9,... | collective-permute-start | bytes 6291464 | tf_op jit(solution)/shard_map/ppermute | solution.py:211
  703.5 40.6 %collective-permute-start.95 = (bf16[2048,256]{1,0:T(8,128)(2,1)}, bf16[2048,256]{1,0:T(8,128)(2,1)}, u32[]{:S(2)}, u32[]{:S(2)}) collective-permute-start(bf16[2048,256]{1,0:T(8,128)(2,1)} %pad_maximum_fusion.11), channel_id=1, source_target_pairs={{0,0},{1,1},{2,2},{3,3},{8,4},{9,5},{10,6},{11,7},{4,8},{5,9},{6,1... | collective-permute-start | bytes 3145736 | tf_op jit(solution)/shard_map/ppermute | solution.py:211
  714.1 36.1 %collective-permute-start.143 = (bf16[4,512,256]{2,1,0:T(8,128)(2,1)}, bf16[4,512,256]{2,1,0:T(8,128)(2,1)}, u32[]{:S(2)}, u32[]{:S(2)}) collective-permute-start(bf16[4,512,256]{2,1,0:T(8,128)(2,1)} %pad_maximum_fusion.20), channel_id=1, source_target_pairs={{0,8},{1,9},{2,10},{3,11},{4,12},{5,13},{6,14},{7,15},{8,0},{9,1},... | collective-permute-start | bytes 3145736 | tf_op jit(solution)/shard_map/ppermute | solution.py:211
  715.2 40.8 %collective-permute-start.134 = (bf16[4,512,256]{2,1,0:T(8,128)(2,1)}, bf16[4,512,256]{2,1,0:T(8,128)(2,1)}, u32[]{:S(2)}, u32[]{:S(2)}) collective-permute-start(bf16[4,512,256]{2,1,0:T(8,128)(2,1)} %pad_maximum_fusion.19), channel_id=1, source_target_pairs={{0,8},{1,9},{2,10},{3,11},{4,12},{5,13},{6,14},{7,15},{8,0},{9,1},... | collective-permute-start | bytes 3145736 | tf_op jit(solution)/shard_map/ppermute | solution.py:211
  716.8 43.0 %collective-permute-start.125 = (bf16[4,512,256]{2,1,0:T(8,128)(2,1)}, bf16[4,512,256]{2,1,0:T(8,128)(2,1)}, u32[]{:S(2)}, u32[]{:S(2)}) collective-permute-start(bf16[4,512,256]{2,1,0:T(8,128)(2,1)} %pad_maximum_fusion.18), channel_id=1, source_target_pairs={{0,8},{1,9},{2,10},{3,11},{4,12},{5,13},{6,14},{7,15},{8,0},{9,1},... | collective-permute-start | bytes 3145736 | tf_op jit(solution)/shard_map/ppermute | solution.py:211
  719.1 44.6 %collective-permute-start.116 = (bf16[4,512,256]{2,1,0:T(8,128)(2,1)}, bf16[4,512,256]{2,1,0:T(8,128)(2,1)}, u32[]{:S(2)}, u32[]{:S(2)}) collective-permute-start(bf16[4,512,256]{2,1,0:T(8,128)(2,1)} %pad_maximum_fusion.17), channel_id=1, source_target_pairs={{0,8},{1,9},{2,10},{3,11},{4,12},{5,13},{6,14},{7,15},{8,0},{9,1},... | collective-permute-start | bytes 3145736 | tf_op jit(solution)/shard_map/ppermute | solution.py:211
  744.1 93.4 %collective-permute-start.164 = (bf16[2,2,512,1024]{3,2,1,0:T(8,128)(2,1)}, bf16[2,2,512,1024]{3,2,1,0:T(8,128)(2,1)}, u32[]{:S(2)}, u32[]{:S(2)}) collective-permute-start(bf16[2,2,512,1024]{3,2,1,0:T(8,128)(2,1)} %get-tuple-element.330), channel_id=1, source_target_pairs={{0,16},{1,17},{2,18},{3,19},{4,20},{5,21},{6,22},{7,23},{8,24},{9,... | collective-permute-start | bytes 12582920 | tf_op jit(solution)/shard_map/ppermute | solution.py:211
  750.1 48.2 %collective-permute-start.167 = (bf16[1,1024,512]{2,1,0:T(8,128)(2,1)}, bf16[1,1024,512]{2,1,0:T(8,128)(2,1)S(1)}, u32[]{:S(2)}, u32[]{:S(2)}) collective-permute-start(bf16[1,1024,512]{2,1,0:T(8,128)(2,1)} %get-tuple-element.336), channel_id=1, source_target_pairs={{0,0},{1,1},{2,2},{3,3},{8,4},{9,5},{10,6},{11,7},{4,8},{5,9},{6,1... | collective-permute-start | bytes 3145736 | tf_op jit(solution)/shard_map/ppermute | solution.py:211
  798.3 47.1 %collective-permute-start.168 = (bf16[1,1024,512]{2,1,0:T(8,128)(2,1)}, bf16[1,1024,512]{2,1,0:T(8,128)(2,1)S(1)}, u32[]{:S(2)}, u32[]{:S(2)}) collective-permute-start(bf16[1,1024,512]{2,1,0:T(8,128)(2,1)} %get-tuple-element.337), channel_id=1, source_target_pairs={{4,0},{5,1},{6,2},{7,3},{12,4},{13,5},{14,6},{15,7},{0,8},{1,9},{2... | collective-permute-start | bytes 3145736 | tf_op jit(solution)/shard_map/ppermute | solution.py:211
  822.2 52.4 %collective-permute-start.151 = (bf16[4,512,256]{2,1,0:T(8,128)(2,1)}, bf16[4,512,256]{2,1,0:T(8,128)(2,1)S(1)}, u32[]{:S(2)}, u32[]{:S(2)}) collective-permute-start(bf16[4,512,256]{2,1,0:T(8,128)(2,1)} %get-tuple-element.315), channel_id=1, source_target_pairs={{0,8},{1,9},{2,10},{3,11},{4,12},{5,13},{6,14},{7,15},{8,0},{9,1},... | collective-permute-start | bytes 3145736 | tf_op jit(solution)/shard_map/ppermute | solution.py:211
  827.7 48.5 %collective-permute-start.159 = (bf16[4,512,256]{2,1,0:T(8,128)(2,1)}, bf16[4,512,256]{2,1,0:T(8,128)(2,1)S(1)}, u32[]{:S(2)}, u32[]{:S(2)}) collective-permute-start(bf16[4,512,256]{2,1,0:T(8,128)(2,1)} %get-tuple-element.319), channel_id=1, source_target_pairs={{0,8},{1,9},{2,10},{3,11},{4,12},{5,13},{6,14},{7,15},{8,0},{9,1},... | collective-permute-start | bytes 3145736 | tf_op jit(solution)/shard_map/ppermute | solution.py:211
  845.5 37.5 %collective-permute-start.169 = (bf16[2,512,1024]{2,1,0:T(8,128)(2,1)}, bf16[2,512,1024]{2,1,0:T(8,128)(2,1)S(1)}, u32[]{:S(2)}, u32[]{:S(2)}) collective-permute-start(bf16[2,512,1024]{2,1,0:T(8,128)(2,1)} %get-tuple-element.338), channel_id=1, source_target_pairs={{0,0},{1,1},{2,2},{3,3},{8,4},{9,5},{10,6},{11,7},{4,8},{5,9},{6,1... | collective-permute-start | bytes 6291464 | tf_op jit(solution)/shard_map/ppermute | solution.py:211
  875.0 35.1 %collective-permute-start.152 = (bf16[2,512,256]{2,1,0:T(8,128)(2,1)S(1)}, bf16[2,512,256]{2,1,0:T(8,128)(2,1)S(1)}, u32[]{:S(2)}, u32[]{:S(2)}) collective-permute-start(bf16[2,512,256]{2,1,0:T(8,128)(2,1)S(1)} %slice.521), channel_id=1, source_target_pairs={{0,2},{1,3},{2,0},{3,1},{4,6},{5,7},{6,4},{7,5},{8,10},{9,11},{10,... | collective-permute-start | bytes 1572872 | tf_op jit(solution)/shard_map/ppermute | solution.py:211
  876.5 44.8 %collective-permute-start.160 = (bf16[2,512,256]{2,1,0:T(8,128)(2,1)S(1)}, bf16[2,512,256]{2,1,0:T(8,128)(2,1)S(1)}, u32[]{:S(2)}, u32[]{:S(2)}) collective-permute-start(bf16[2,512,256]{2,1,0:T(8,128)(2,1)S(1)} %slice.527), channel_id=1, source_target_pairs={{0,2},{1,3},{2,0},{3,1},{4,6},{5,7},{6,4},{7,5},{8,10},{9,11},{10,... | collective-permute-start | bytes 1572872 | tf_op jit(solution)/shard_map/ppermute | solution.py:211
  879.1 44.5 %collective-permute-start.148 = (bf16[2,512,256]{2,1,0:T(8,128)(2,1)S(1)}, bf16[2,512,256]{2,1,0:T(8,128)(2,1)S(1)}, u32[]{:S(2)}, u32[]{:S(2)}) collective-permute-start(bf16[2,512,256]{2,1,0:T(8,128)(2,1)S(1)} %slice.421), channel_id=1, source_target_pairs={{0,1},{1,0},{2,3},{3,2},{4,5},{5,4},{6,7},{7,6},{8,9},{9,8},{10,11... | collective-permute-start | bytes 1572872 | tf_op jit(solution)/shard_map/ppermute | solution.py:211
  881.5 59.0 %collective-permute-start.156 = (bf16[2,512,256]{2,1,0:T(8,128)(2,1)S(1)}, bf16[2,512,256]{2,1,0:T(8,128)(2,1)S(1)}, u32[]{:S(2)}, u32[]{:S(2)}) collective-permute-start(bf16[2,512,256]{2,1,0:T(8,128)(2,1)S(1)} %slice.429), channel_id=1, source_target_pairs={{0,1},{1,0},{2,3},{3,2},{4,5},{5,4},{6,7},{7,6},{8,9},{9,8},{10,11... | collective-permute-start | bytes 1572872 | tf_op jit(solution)/shard_map/ppermute | solution.py:211
  883.0 39.1 %collective-permute-start.165 = (bf16[2,1,256,512]{3,2,1,0:T(8,128)(2,1)S(1)}, bf16[2,1,256,512]{3,2,1,0:T(8,128)(2,1)S(1)}, u32[]{:S(2)}, u32[]{:S(2)}) collective-permute-start(bf16[2,1,256,512]{3,2,1,0:T(8,128)(2,1)S(1)} %copy-done.130), channel_id=1, source_target_pairs={{0,16},{1,17},{2,18},{3,19},{4,20},{5,21},{6,22},{7,23},{8,24},{9,... | collective-permute-start | bytes 1572872 | tf_op jit(solution)/shard_map/ppermute | solution.py:211
  910.0 60.3 %collective-permute-start.170 = (bf16[2,512,1024]{2,1,0:T(8,128)(2,1)S(1)}, bf16[2,512,1024]{2,1,0:T(8,128)(2,1)S(1)}, u32[]{:S(2)}, u32[]{:S(2)}) collective-permute-start(bf16[2,512,1024]{2,1,0:T(8,128)(2,1)S(1)} %copy-done.97), channel_id=1, source_target_pairs={{4,0},{5,1},{6,2},{7,3},{12,4},{13,5},{14,6},{15,7},{0,8},{1,9},{2... | collective-permute-start | bytes 6291464 | tf_op jit(solution)/shard_map/ppermute | solution.py:211
  923.6 47.4 %collective-permute-start.166 = (bf16[2,3,512,256]{3,2,1,0:T(8,128)(2,1)S(1)}, bf16[2,3,512,256]{3,2,1,0:T(8,128)(2,1)S(1)}, u32[]{:S(2)}, u32[]{:S(2)}) collective-permute-start(bf16[2,3,512,256]{3,2,1,0:T(8,128)(2,1)S(1)} %copy-done.128), channel_id=1, source_target_pairs={{0,16},{1,17},{2,18},{3,19},{4,20},{5,21},{6,22},{7,23},{8,24},{9,... | collective-permute-start | bytes 4718600 | tf_op jit(solution)/shard_map/ppermute | solution.py:211
  940.7 48.9 %collective-permute-start.157 = (bf16[1,512,256]{2,1,0:T(8,128)(2,1)S(1)}, bf16[1,512,256]{2,1,0:T(8,128)(2,1)S(1)}, u32[]{:S(2)}, u32[]{:S(2)}) collective-permute-start(bf16[1,512,256]{2,1,0:T(8,128)(2,1)S(1)} %slice.525), channel_id=1, source_target_pairs={{0,2},{1,3},{2,0},{3,1},{4,6},{5,7},{6,4},{7,5},{8,10},{9,11},{10,... | collective-permute-start | bytes 786440 | tf_op jit(solution)/shard_map/ppermute | solution.py:211
  941.4 50.5 %collective-permute-start.175 = (f32[4,256]{1,0:T(4,128)S(1)}, f32[4,256]{1,0:T(4,128)S(1)}, u32[]{:S(2)}, u32[]{:S(2)}) collective-permute-start(f32[4,256]{1,0:T(4,128)S(1)} %pad_maximum_fusion.46), channel_id=1, source_target_pairs={{0,4},{1,5},{2,6},{3,7},{4,0},{5,1},{6,2},{7,3},{8,12},{9,13},{10,... | collective-permute-start | bytes 12296 | tf_op jit(solution)/shard_map/ppermute | solution.py:211
  995.6 29.3 %collective-permute-start.177 = (f32[4,256]{1,0:T(4,128)S(1)}, f32[4,256]{1,0:T(4,128)S(1)}, u32[]{:S(2)}, u32[]{:S(2)}) collective-permute-start(f32[4,256]{1,0:T(4,128)S(1)} %add.771), channel_id=1, source_target_pairs={{0,0},{1,1},{2,2},{3,3},{8,4},{9,5},{10,6},{11,7},{4,8},{5,9},{6,1... | collective-permute-start | bytes 12296 | tf_op jit(solution)/shard_map/ppermute | solution.py:211
  997.3 45.7 %collective-permute-start.174 = (bf16[3,512,256]{2,1,0:T(8,128)(2,1)S(1)}, bf16[3,512,256]{2,1,0:T(8,128)(2,1)S(1)}, u32[]{:S(2)}, u32[]{:S(2)}) collective-permute-start(bf16[3,512,256]{2,1,0:T(8,128)(2,1)S(1)} %get-tuple-element.343), channel_id=1, source_target_pairs={{4,0},{5,1},{6,2},{7,3},{12,4},{13,5},{14,6},{15,7},{0,8},{1,9},{2... | collective-permute-start | bytes 2359304 | tf_op jit(solution)/shard_map/ppermute | solution.py:211
  (263 other events, 3842.9 us)

commit v3 on v2

--- a/solution.py
+++ b/solution.py
@@ -792,9 +792,9 @@
         hidden_cots.append(hidden_cot)
 
     layer_out = far.send(jnp.concatenate(layer_outs), layout.exchange_back(0))
-    grad_down = owners_sum(*matmul_tall(ffn_made[-1], [mixes], False, 512))[0]
+    grad_down = owners_sum(*matmul_tall(ffn_made[-1], [mixes], False, 1024))[0]
     grad_gate, grad_up = owners_sum(
-        *matmul_tall(hidden_made[-1], [gate_backs, up_backs], True, 256)
+        *matmul_tall(hidden_made[-1], [gate_backs, up_backs], True, 512)
     )
     out_back, attn_wide = attn_made
     grad_out = owners_sum(*matmul_tall(attn_wide, [attn_parts], False, 256))[0]

time: 1060 us -> 1050 us (level)
  starting transfers between devices: 303 us -> 287 us
    ppermute x178, starting transfers between devices: 303 us -> 287 us  [send(): return lax.ppermute(values, ('rows', 'cols'), pairs)]
  transfers between devices with their start and end apart: 178 -> 178, of which waited for: 60 -> 62; matrix products, arithmetic and copies ran while one was open for 8% -> 8% of each run, Pallas kernels for 29% -> 29%
where the time goes in v3:
time: 1050 us; the launch traced here: 1040 us
  waiting for transfers between devices  337 us (32%)
  Pallas kernels  322 us (31%)
  starting transfers between devices  287 us (27%)
  other arithmetic  77.2 us (7%)
  local copies, waits for them, and re-layouts  17.2 us (2%)
    ppermute x178, waiting for transfers between devices, send(): return lax.ppermute(values, ('rows', 'cols'), pairs)  337 us
    ppermute x178, starting transfers between devices, send(): return lax.ppermute(values, ('rows', 'cols'), pairs)  287 us
    pallas_call x16, Pallas kernels, matmul_rows(): pl.pallas_call(body, grid_spec=pltpu.PrefetchScalarGridSpec(num_scalar_pr...  110 us
    pallas_call x16, Pallas kernels, matmul_columns(): pl.pallas_call(functools.partial(columns_kernel, len(lefts), shards, per,...  99.5 us
    pallas_call x4, Pallas kernels, matmul_tall(): pl.pallas_call(functools.partial(tall_kernel, [len(g) for g in groups], h...  56.7 us
    pallas_call x1, Pallas kernels, attend_back(): pl.pallas_call(functools.partial(attend_back_kernel, block), grid_spec=pl...  21.8 us
  transfers between devices with their start and end apart: 178, of which 62 were waited for; matrix products, arithmetic and copies ran while one was open for 8% of the time, Pallas kernels for 29%

profile of v3, /device:TPU:0, one launch (start us, length us, event | category | flops | bytes accessed | tf_op | source)
XLA Modules:
  0.0 1043.8 jit_solution(16530372019001226900)
XLA Ops:
  14.7 35.2 %collective-permute-start.6 = (bf16[3,512,256]{2,1,0:T(8,128)(2,1)S(1)}, bf16[3,512,256]{2,1,0:T(8,128)(2,1)S(1)}, u32[]{:S(2)}, u32[]{:S(2)}) collective-permute-start(bf16[3,512,256]{2,1,0:T(8,128)(2,1)S(1)} %pad_maximum_fusion.22), channel_id=1, source_target_pairs={{0,4},{1,5},{2,6},{3,7},{4,12},{5,13},{6,14},{7,15},{8,0},{9,1},{1... | collective-permute-start | bytes 2359304 | tf_op jit(solution)/shard_map/ppermute | solution.py:211
  63.5 8.4 collective-permute-done.16.refs_2_
  90.7 7.5 collective-permute-done.8.refs_7_.refs_6_
  130.8 12.3 %collective-permute-start.23 = (bf16[1,256,512]{2,1,0:T(8,128)(2,1)S(1)}, bf16[1,256,512]{2,1,0:T(8,128)(2,1)S(1)}, u32[]{:S(2)}, u32[]{:S(2)}) collective-permute-start(bf16[1,256,512]{2,1,0:T(8,128)(2,1)S(1)} %bitcast.533), channel_id=1, source_target_pairs={{0,4},{1,5},{2,6},{3,7},{4,12},{5,13},{6,14},{7,15},{8,0},{9,1},{1... | collective-permute-start | bytes 786440 | tf_op jit(solution)/shard_map/ppermute | solution.py:211
  183.3 6.6 shard_map.254
  197.7 7.4 collective-permute-start.36
  210.1 7.1 collective-permute-done.51
  221.7 25.4 %collective-permute-done.81 = bf16[2,512,256]{2,1,0:T(8,128)(2,1)S(1)} collective-permute-done((bf16[2,512,256]{2,1,0:T(8,128)(2,1)S(1)}, bf16[2,512,256]{2,1,0:T(8,128)(2,1)S(1)}, u32[]{:S(2)}, u32[]{:S(2)}) %collective-permute-start.81) | collective-permute-done | bytes 524320 | tf_op jit(solution)/shard_map/ppermute | solution.py:211
  250.6 7.2 collective-permute-done.67
  272.8 7.8 collective-permute-done.32.refs_1_
  281.7 16.6 %collective-permute-start.40 = (bf16[1,1024,512]{2,1,0:T(8,128)(2,1)S(1)}, bf16[1,1024,512]{2,1,0:T(8,128)(2,1)}, u32[]{:S(2)}, u32[]{:S(2)}) collective-permute-start(bf16[1,1024,512]{2,1,0:T(8,128)(2,1)S(1)} %bitcast.531), channel_id=1, source_target_pairs={{0,4},{1,5},{2,6},{3,7},{4,12},{5,13},{6,14},{7,15},{8,0},{9,1},{1... | collective-permute-start | bytes 3145736 | tf_op jit(solution)/shard_map/ppermute | solution.py:211
  317.2 11.0 %collective-permute-done.71.refs_1_ = bf16[1,512,256]{2,1,0:T(8,128)(2,1)S(1)} collective-permute-done((bf16[1,512,256]{2,1,0:T(8,128)(2,1)S(1)}, bf16[1,512,256]{2,1,0:T(8,128)(2,1)S(1)}, u32[]{:S(2)}, u32[]{:S(2)}) %collective-permute-start.71) | collective-permute-done | bytes 262176 | tf_op jit(solution)/shard_map/ppermute | solution.py:211
  330.5 9.0 collective-permute-done.57.refs_2_
  339.7 10.6 %collective-permute-done.87.refs_2_ = bf16[2,512,256]{2,1,0:T(8,128)(2,1)S(1)} collective-permute-done((bf16[2,512,256]{2,1,0:T(8,128)(2,1)S(1)}, bf16[2,512,256]{2,1,0:T(8,128)(2,1)S(1)}, u32[]{:S(2)}, u32[]{:S(2)}) %collective-permute-start.87) | collective-permute-done | bytes 524320 | tf_op jit(solution)/shard_map/ppermute | solution.py:211
  353.0 10.4 shard_map.244
  370.8 10.4 shard_map.248
  387.8 10.4 shard_map.252
  404.6 10.4 %shard_map.256 = (bf16[512,1024]{1,0:T(8,128)(2,1)}, bf16[512,1024]{1,0:T(8,128)(2,1)}, bf16[512,1024]{1,0:T(8,128)(2,1)}, bf16[4,2048,512]{2,1,0:T(8,128)(2,1)}) custom-call(s32[2]{0:T(128)S(1)} %pad_add_fusion.ids, bf16[1,512,256]{2,1,0:T(8,128)(2,1)S(1)} %get-tuple-element.245.refs_0_, ...), custom_call_target="tpu_custom_call", output_to_operand_aliasing={{3}: (9, {})} | custom-call | flops 4294967296 | bytes 13631496 | tf_op jit(solution)/shard_map/pallas_call | solution.py:313
  430.3 20.7 %collective-permute-done.90 = bf16[2,512,256]{2,1,0:T(8,128)(2,1)S(1)} collective-permute-done((bf16[2,512,256]{2,1,0:T(8,128)(2,1)S(1)}, bf16[2,512,256]{2,1,0:T(8,128)(2,1)S(1)}, u32[]{:S(2)}, u32[]{:S(2)}) %collective-permute-start.90) | collective-permute-done | bytes 524320 | tf_op jit(solution)/shard_map/ppermute | solution.py:211
  454.6 7.7 collective-permute-done.60
  499.0 10.3 collective-permute-done.106.refs_2_
  517.1 9.2 collective-permute-done.97.refs_2_
  530.0 7.7 shard_map.258
  537.7 10.1 shard_map.259
  548.8 7.7 shard_map.260
  556.5 10.1 shard_map.261
  566.8 7.7 shard_map.262
  574.5 10.6 %shard_map.263 = (bf16[4,512,256]{2,1,0:T(8,128)(2,1)S(1)}, bf16[4,512,256]{2,1,0:T(8,128)(2,1)}) custom-call(s32[2]{0:T(128)S(1)} %pad_add_fusion.ids, bf16[512,1024]{1,0:T(8,128)(2,1)} %get-tuple-element.282.refs_0_.refs_2_, bf16[512,1024]{1,0:T(8,128)(2,1)} %get-tuple-element.283.refs_1_.refs_6_, bf16[2,512,1024]{2,1,0:T(8,128)(2,1)} %copy-done.20, ...), custom_call_target="tpu_custom_call" | custom-call | flops 4294967296 | bytes 12582912 | tf_op jit(solution)/shard_map/pallas_call | solution.py:363
  586.1 7.7 shard_map.264
  593.7 10.2 shard_map.265
  611.7 9.4 collective-permute-done.127
  622.1 9.5 collective-permute-done.109
  657.0 14.1 %shard_map.279 = (bf16[2,1,1024,512]{3,2,1,0:T(8,128)(2,1)}, bf16[2,1,1024,512]{3,2,1,0:T(8,128)(2,1)}) custom-call(bf16[4,2048,512]{2,1,0:T(8,128)(2,1)} %get-tuple-element.327.wide, bf16[512,1024]{1,0:T(8,128)(2,1)S(1)} %copy-done.13, bf16[512,1024]{1,0:T(8,128)(2,1)} %get-tuple-element.226.refs_0_.refs_1_, ...), custom_call_target="tpu_custom_call" | custom-call | flops 8589934592 | bytes 16777216 | tf_op jit(solution)/shard_map/pallas_call | solution.py:440
  693.0 9.4 collective-permute-done.142.refs_2_
  702.4 9.5 collective-permute-start.95
  719.5 24.8 %shard_map.278 = (bf16[2,2,512,1024]{3,2,1,0:T(8,128)(2,1)}, bf16[2,2,512,1024]{3,2,1,0:T(8,128)(2,1)}) custom-call(bf16[4,2048,512]{2,1,0:T(8,128)(2,1)} %get-tuple-element.325.wide, bf16[512,1024]{1,0:T(8,128)(2,1)S(1)} %copy-done.12, bf16[512,1024]{1,0:T(8,128)(2,1)} %get-tuple-element.271.refs_0_.refs_1_, ...), custom_call_target="tpu_custom_call" | custom-call | flops 17179869184 | bytes 25165824 | tf_op jit(solution)/shard_map/pallas_call | solution.py:440
  766.3 21.8 %shard_map.270 = (f32[2048,256]{1,0:T(8,128)}, f32[2048,256]{1,0:T(8,128)}, f32[2048,256]{1,0:T(8,128)}) custom-call(s32[4]{0:T(128)S(1)} %and_select_fusion.lows, s32[1,2048]{1,0:T(1,128)S(1)} %bitcast.402, bf16[2048,256]{1,0:T(8,128)(2,1)S(1)} %get-tuple-element.241.query, bf16[2048,256]{1,0:T(8,128)(2,1)} %get-tuple-element.196.key, ...), custom_call_target="tpu_custom_call" | custom-call | flops 10737418240 | bytes 10485760 | tf_op jit(solution)/shard_map/pallas_call | solution.py:133
  788.2 7.6 shard_map.271
  803.5 6.5 shard_map.277
  828.6 9.1 collective-permute-done.164
  859.7 11.2 %shard_map.276 = (bf16[2,3,512,256]{3,2,1,0:T(8,128)(2,1)}, bf16[2,3,512,256]{3,2,1,0:T(8,128)(2,1)}) custom-call(bf16[4,2048,512]{2,1,0:T(8,128)(2,1)} %get-tuple-element.320.wide, bf16[2048,256]{1,0:T(8,128)(2,1)S(1)} %copy-done.2, bf16[2048,256]{1,0:T(8,128)(2,1)} %get-tuple-element.427.refs_1_, bf16[2048,256]{1,0:T(8,128)(2,1)} %convert_element_type.729.refs_2_), custom_call_target="tpu_custom_call" | custom-call | flops 6442450944 | bytes 14680064 | tf_op jit(solution)/shard_map/pallas_call | solution.py:440
  879.8 27.9 %collective-permute-done.152 = bf16[2,512,256]{2,1,0:T(8,128)(2,1)S(1)} collective-permute-done((bf16[2,512,256]{2,1,0:T(8,128)(2,1)S(1)}, bf16[2,512,256]{2,1,0:T(8,128)(2,1)S(1)}, u32[]{:S(2)}, u32[]{:S(2)}) %collective-permute-start.152) | collective-permute-done | bytes 524320 | tf_op jit(solution)/shard_map/ppermute | solution.py:211
  908.0 10.2 collective-permute-done.160
  938.3 28.8 %collective-permute-start.175 = (f32[4,256]{1,0:T(4,128)S(1)}, f32[4,256]{1,0:T(4,128)S(1)}, u32[]{:S(2)}, u32[]{:S(2)}) collective-permute-start(f32[4,256]{1,0:T(4,128)S(1)} %pad_maximum_fusion.46), channel_id=1, source_target_pairs={{0,4},{1,5},{2,6},{3,7},{4,0},{5,1},{6,2},{7,3},{8,12},{9,13},{10,... | collective-permute-start | bytes 12296 | tf_op jit(solution)/shard_map/ppermute | solution.py:211
  968.5 10.5 %collective-permute-start.172 = (bf16[1,256,512]{2,1,0:T(8,128)(2,1)S(1)}, bf16[1,256,512]{2,1,0:T(8,128)(2,1)S(1)}, u32[]{:S(2)}, u32[]{:S(2)}) collective-permute-start(bf16[1,256,512]{2,1,0:T(8,128)(2,1)S(1)} %get-tuple-element.341), channel_id=1, source_target_pairs={{4,0},{5,1},{6,2},{7,3},{12,4},{13,5},{14,6},{15,7},{0,8},{1,9},{2... | collective-permute-start | bytes 786440 | tf_op jit(solution)/shard_map/ppermute | solution.py:211
  979.1 6.8 collective-permute-done.172
  994.3 27.5 %collective-permute-start.174 = (bf16[3,512,256]{2,1,0:T(8,128)(2,1)S(1)}, bf16[3,512,256]{2,1,0:T(8,128)(2,1)S(1)}, u32[]{:S(2)}, u32[]{:S(2)}) collective-permute-start(bf16[3,512,256]{2,1,0:T(8,128)(2,1)S(1)} %get-tuple-element.343), channel_id=1, source_target_pairs={{4,0},{5,1},{6,2},{7,3},{12,4},{13,5},{14,6},{15,7},{0,8},{1,9},{2... | collective-permute-start | bytes 2359304 | tf_op jit(solution)/shard_map/ppermute | solution.py:211
  1026.2 13.8 %collective-permute-done.174 = bf16[3,512,256]{2,1,0:T(8,128)(2,1)S(1)} collective-permute-done((bf16[3,512,256]{2,1,0:T(8,128)(2,1)S(1)}, bf16[3,512,256]{2,1,0:T(8,128)(2,1)S(1)}, u32[]{:S(2)}, u32[]{:S(2)}) %collective-permute-start.174) | collective-permute-done | bytes 786464 | tf_op jit(solution)/shard_map/ppermute | solution.py:211
  (837 shorter events, 448.1 us)
Async XLA Ops:
  4.6 46.9 %collective-permute-start.15 = (bf16[1,512,256]{2,1,0:T(8,128)(2,1)S(1)}, bf16[1,512,256]{2,1,0:T(8,128)(2,1)S(1)}, u32[]{:S(2)}, u32[]{:S(2)}) collective-permute-start(bf16[1,512,256]{2,1,0:T(8,128)(2,1)S(1)} %get-tuple-element.398.refs_0_), channel_id=1, source_target_pairs={{0,2},{1,3},{2,0},{3,1},{4,6},{5,7},{6,4},{7,5},{8,10},{9,11},{10,... | collective-permute-start | bytes 786440 | tf_op jit(solution)/shard_map/ppermute | solution.py:211
  7.6 44.3 %collective-permute-start.12 = (bf16[1,512,256]{2,1,0:T(8,128)(2,1)S(1)}, bf16[1,512,256]{2,1,0:T(8,128)(2,1)S(1)}, u32[]{:S(2)}, u32[]{:S(2)}) collective-permute-start(bf16[1,512,256]{2,1,0:T(8,128)(2,1)S(1)} %get-tuple-element.399.refs_0_), channel_id=1, source_target_pairs={{0,1},{1,0},{2,3},{3,2},{4,5},{5,4},{6,7},{7,6},{8,9},{9,8},{10,11... | collective-permute-start | bytes 786440 | tf_op jit(solution)/shard_map/ppermute | solution.py:211
  9.2 44.5 %collective-permute-start.9 = (bf16[1,512,256]{2,1,0:T(8,128)(2,1)S(1)}, bf16[1,512,256]{2,1,0:T(8,128)(2,1)S(1)}, u32[]{:S(2)}, u32[]{:S(2)}) collective-permute-start(bf16[1,512,256]{2,1,0:T(8,128)(2,1)S(1)} %get-tuple-element.400.refs_0_), channel_id=1, source_target_pairs={{0,2},{1,3},{2,0},{3,1},{4,6},{5,7},{6,4},{7,5},{8,10},{9,11},{10,... | collective-permute-start | bytes 786440 | tf_op jit(solution)/shard_map/ppermute | solution.py:211
  14.7 63.2 %collective-permute-start.6 = (bf16[3,512,256]{2,1,0:T(8,128)(2,1)S(1)}, bf16[3,512,256]{2,1,0:T(8,128)(2,1)S(1)}, u32[]{:S(2)}, u32[]{:S(2)}) collective-permute-start(bf16[3,512,256]{2,1,0:T(8,128)(2,1)S(1)} %pad_maximum_fusion.22), channel_id=1, source_target_pairs={{0,4},{1,5},{2,6},{3,7},{4,12},{5,13},{6,14},{7,15},{8,0},{9,1},{1... | collective-permute-start | bytes 2359304 | tf_op jit(solution)/shard_map/ppermute | solution.py:211
  87.9 29.6 %collective-permute-start.4 = (bf16[4,512,256]{2,1,0:T(8,128)(2,1)S(1)}, bf16[4,512,256]{2,1,0:T(8,128)(2,1)S(1)}, u32[]{:S(2)}, u32[]{:S(2)}) collective-permute-start(bf16[4,512,256]{2,1,0:T(8,128)(2,1)S(1)} %pad_maximum_fusion.1), channel_id=1, source_target_pairs={{0,8},{1,9},{2,10},{3,11},{4,12},{5,13},{6,14},{7,15},{8,0},{9,1},... | collective-permute-start | bytes 3145736 | tf_op jit(solution)/shard_map/ppermute | solution.py:211
  98.1 55.1 %collective-permute-start.21 = (f32[4,256]{1,0:T(4,128)S(1)}, f32[4,256]{1,0:T(4,128)S(1)}, u32[]{:S(2)}, u32[]{:S(2)}) collective-permute-start(f32[4,256]{1,0:T(4,128)S(1)} %pad_maximum_fusion.41), channel_id=1, source_target_pairs={{0,0},{1,1},{2,2},{3,3},{4,8},{5,9},{6,10},{7,11},{8,4},{9,5},{10,... | collective-permute-start | bytes 12296 | tf_op jit(solution)/shard_map/ppermute | solution.py:211
  147.0 48.9 %collective-permute-start.35 = (bf16[2,512,1024]{2,1,0:T(8,128)(2,1)}, bf16[2,512,1024]{2,1,0:T(8,128)(2,1)S(1)}, u32[]{:S(2)}, u32[]{:S(2)}) collective-permute-start(bf16[2,512,1024]{2,1,0:T(8,128)(2,1)} %pad_maximum_fusion), channel_id=1, source_target_pairs={{0,0},{1,1},{2,2},{3,3},{4,8},{5,9},{6,10},{7,11},{8,4},{9,5},{10,... | collective-permute-start | bytes 6291464 | tf_op jit(solution)/shard_map/ppermute | solution.py:211
  196.0 62.3 %collective-permute-start.37 = (bf16[2,512,1024]{2,1,0:T(8,128)(2,1)S(1)}, bf16[2,512,1024]{2,1,0:T(8,128)(2,1)S(1)}, u32[]{:S(2)}, u32[]{:S(2)}) collective-permute-start(bf16[2,512,1024]{2,1,0:T(8,128)(2,1)S(1)} %collective-permute-done.35.refs_4_.refs_2_), channel_id=1, source_target_pairs={{0,16},{1,17},{2,18},{3,19},{4,20},{5,21},{6,22},{7,23},{8,24},{9,... | collective-permute-start | bytes 6291464 | tf_op jit(solution)/shard_map/ppermute | solution.py:211
  197.7 62.4 %collective-permute-start.36 = (bf16[2,512,1024]{2,1,0:T(8,128)(2,1)S(1)}, bf16[2,512,1024]{2,1,0:T(8,128)(2,1)S(1)}, u32[]{:S(2)}, u32[]{:S(2)}) collective-permute-start(bf16[2,512,1024]{2,1,0:T(8,128)(2,1)S(1)} %copy-done.93), channel_id=1, source_target_pairs={{0,4},{1,5},{2,6},{3,7},{4,12},{5,13},{6,14},{7,15},{8,0},{9,1},{1... | collective-permute-start | bytes 6291464 | tf_op jit(solution)/shard_map/ppermute | solution.py:211
  207.4 39.7 %collective-permute-start.81 = (bf16[2,512,256]{2,1,0:T(8,128)(2,1)S(1)}, bf16[2,512,256]{2,1,0:T(8,128)(2,1)S(1)}, u32[]{:S(2)}, u32[]{:S(2)}) collective-permute-start(bf16[2,512,256]{2,1,0:T(8,128)(2,1)S(1)} %slice.487), channel_id=1, source_target_pairs={{0,2},{1,3},{2,0},{3,1},{4,6},{5,7},{6,4},{7,5},{8,10},{9,11},{10,... | collective-permute-start | bytes 1572872 | tf_op jit(solution)/shard_map/ppermute | solution.py:211
  217.2 32.6 %collective-permute-start.27 = (bf16[2,512,256]{2,1,0:T(8,128)(2,1)S(1)}, bf16[2,512,256]{2,1,0:T(8,128)(2,1)S(1)}, u32[]{:S(2)}, u32[]{:S(2)}) collective-permute-start(bf16[2,512,256]{2,1,0:T(8,128)(2,1)S(1)} %slice.351), channel_id=1, source_target_pairs={{0,1},{1,0},{2,3},{3,2},{4,5},{5,4},{6,7},{7,6},{8,9},{9,8},{10,11... | collective-permute-start | bytes 1572872 | tf_op jit(solution)/shard_map/ppermute | solution.py:211
  260.1 44.5 %collective-permute-start.38 = (bf16[2,512,1024]{2,1,0:T(8,128)(2,1)S(1)}, bf16[2,512,1024]{2,1,0:T(8,128)(2,1)S(1)}, u32[]{:S(2)}, u32[]{:S(2)}) collective-permute-start(bf16[2,512,1024]{2,1,0:T(8,128)(2,1)S(1)} %collective-permute-done.36.refs_5_.refs_3_), channel_id=1, source_target_pairs={{0,16},{1,17},{2,18},{3,19},{4,20},{5,21},{6,22},{7,23},{8,24},{9,... | collective-permute-start | bytes 6291464 | tf_op jit(solution)/shard_map/ppermute | solution.py:211
  280.7 33.7 %collective-permute-start.33 = (bf16[2,512,256]{2,1,0:T(8,128)(2,1)S(1)}, bf16[2,512,256]{2,1,0:T(8,128)(2,1)S(1)}, u32[]{:S(2)}, u32[]{:S(2)}) collective-permute-start(bf16[2,512,256]{2,1,0:T(8,128)(2,1)S(1)} %pad_maximum_fusion.27), channel_id=1, source_target_pairs={{0,1},{1,0},{2,3},{3,2},{4,5},{5,4},{6,7},{7,6},{8,9},{9,8},{10,11... | collective-permute-start | bytes 1572872 | tf_op jit(solution)/shard_map/ppermute | solution.py:211
  281.7 46.6 %collective-permute-start.40 = (bf16[1,1024,512]{2,1,0:T(8,128)(2,1)S(1)}, bf16[1,1024,512]{2,1,0:T(8,128)(2,1)}, u32[]{:S(2)}, u32[]{:S(2)}) collective-permute-start(bf16[1,1024,512]{2,1,0:T(8,128)(2,1)S(1)} %bitcast.531), channel_id=1, source_target_pairs={{0,4},{1,5},{2,6},{3,7},{4,12},{5,13},{6,14},{7,15},{8,0},{9,1},{1... | collective-permute-start | bytes 3145736 | tf_op jit(solution)/shard_map/ppermute | solution.py:211
  317.2 35.8 %collective-permute-start.34 = (bf16[4,512,256]{2,1,0:T(8,128)(2,1)S(1)}, bf16[4,512,256]{2,1,0:T(8,128)(2,1)}, u32[]{:S(2)}, u32[]{:S(2)}) collective-permute-start(bf16[4,512,256]{2,1,0:T(8,128)(2,1)S(1)} %pad_maximum_fusion.7), channel_id=1, source_target_pairs={{0,8},{1,9},{2,10},{3,11},{4,12},{5,13},{6,14},{7,15},{8,0},{9,1},... | collective-permute-start | bytes 3145736 | tf_op jit(solution)/shard_map/ppermute | solution.py:211
  329.1 34.3 %collective-permute-start.42 = (bf16[1,1024,512]{2,1,0:T(8,128)(2,1)}, bf16[1,1024,512]{2,1,0:T(8,128)(2,1)S(1)}, u32[]{:S(2)}, u32[]{:S(2)}) collective-permute-start(bf16[1,1024,512]{2,1,0:T(8,128)(2,1)} %collective-permute-done.40.refs_2_.refs_5_), channel_id=1, source_target_pairs={{0,16},{1,17},{2,18},{3,19},{4,20},{5,21},{6,22},{7,23},{8,24},{9,... | collective-permute-start | bytes 3145736 | tf_op jit(solution)/shard_map/ppermute | solution.py:211
  339.6 31.3 %collective-permute-start.58 = (bf16[4,512,256]{2,1,0:T(8,128)(2,1)S(1)}, bf16[4,512,256]{2,1,0:T(8,128)(2,1)}, u32[]{:S(2)}, u32[]{:S(2)}) collective-permute-start(bf16[4,512,256]{2,1,0:T(8,128)(2,1)S(1)} %pad_maximum_fusion.8), channel_id=1, source_target_pairs={{0,8},{1,9},{2,10},{3,11},{4,12},{5,13},{6,14},{7,15},{8,0},{9,1},... | collective-permute-start | bytes 3145736 | tf_op jit(solution)/shard_map/ppermute | solution.py:211
  351.3 53.3 %collective-permute-start.88 = (bf16[4,512,256]{2,1,0:T(8,128)(2,1)}, bf16[4,512,256]{2,1,0:T(8,128)(2,1)}, u32[]{:S(2)}, u32[]{:S(2)}) collective-permute-start(bf16[4,512,256]{2,1,0:T(8,128)(2,1)} %pad_maximum_fusion.10), channel_id=1, source_target_pairs={{0,8},{1,9},{2,10},{3,11},{4,12},{5,13},{6,14},{7,15},{8,0},{9,1},... | collective-permute-start | bytes 3145736 | tf_op jit(solution)/shard_map/ppermute | solution.py:211
  352.5 35.3 %collective-permute-start.73 = (bf16[4,512,256]{2,1,0:T(8,128)(2,1)}, bf16[4,512,256]{2,1,0:T(8,128)(2,1)}, u32[]{:S(2)}, u32[]{:S(2)}) collective-permute-start(bf16[4,512,256]{2,1,0:T(8,128)(2,1)} %pad_maximum_fusion.9), channel_id=1, source_target_pairs={{0,8},{1,9},{2,10},{3,11},{4,12},{5,13},{6,14},{7,15},{8,0},{9,1},... | collective-permute-start | bytes 3145736 | tf_op jit(solution)/shard_map/ppermute | solution.py:211
  422.6 41.8 %collective-permute-start.46 = (bf16[2048,256]{1,0:T(8,128)(2,1)}, bf16[2048,256]{1,0:T(8,128)(2,1)S(1)}, u32[]{:S(2)}, u32[]{:S(2)}) collective-permute-start(bf16[2048,256]{1,0:T(8,128)(2,1)} %param.27), channel_id=1, source_target_pairs={{0,0},{1,1},{2,2},{3,3},{4,8},{5,9},{6,10},{7,11},{8,4},{9,5},{10,... | collective-permute-start | bytes 3145736 | tf_op jit(solution)/shard_map/ppermute | solution.py:211
  429.3 33.0 %collective-permute-start.60 = (bf16[2,512,256]{2,1,0:T(8,128)(2,1)S(1)}, bf16[2,512,256]{2,1,0:T(8,128)(2,1)S(1)}, u32[]{:S(2)}, u32[]{:S(2)}) collective-permute-start(bf16[2,512,256]{2,1,0:T(8,128)(2,1)S(1)} %slice.475), channel_id=1, source_target_pairs={{0,2},{1,3},{2,0},{3,1},{4,6},{5,7},{6,4},{7,5},{8,10},{9,11},{10,... | collective-permute-start | bytes 1572872 | tf_op jit(solution)/shard_map/ppermute | solution.py:211
  517.1 30.8 %collective-permute-start.104 = (bf16[4,512,256]{2,1,0:T(8,128)(2,1)}, bf16[4,512,256]{2,1,0:T(8,128)(2,1)S(1)}, u32[]{:S(2)}, u32[]{:S(2)}) collective-permute-start(bf16[4,512,256]{2,1,0:T(8,128)(2,1)} %pad_maximum_fusion.15), channel_id=1, source_target_pairs={{0,8},{1,9},{2,10},{3,11},{4,12},{5,13},{6,14},{7,15},{8,0},{9,1},... | collective-permute-start | bytes 3145736 | tf_op jit(solution)/shard_map/ppermute | solution.py:211
  527.4 57.7 %collective-permute-start.98 = (bf16[4,512,256]{2,1,0:T(8,128)(2,1)}, bf16[4,512,256]{2,1,0:T(8,128)(2,1)S(1)}, u32[]{:S(2)}, u32[]{:S(2)}) collective-permute-start(bf16[4,512,256]{2,1,0:T(8,128)(2,1)} %pad_maximum_fusion.13), channel_id=1, source_target_pairs={{0,8},{1,9},{2,10},{3,11},{4,12},{5,13},{6,14},{7,15},{8,0},{9,1},... | collective-permute-start | bytes 3145736 | tf_op jit(solution)/shard_map/ppermute | solution.py:211
  528.7 38.2 %collective-permute-start.101 = (bf16[4,512,256]{2,1,0:T(8,128)(2,1)}, bf16[4,512,256]{2,1,0:T(8,128)(2,1)}, u32[]{:S(2)}, u32[]{:S(2)}) collective-permute-start(bf16[4,512,256]{2,1,0:T(8,128)(2,1)} %pad_maximum_fusion.14), channel_id=1, source_target_pairs={{0,8},{1,9},{2,10},{3,11},{4,12},{5,13},{6,14},{7,15},{8,0},{9,1},... | collective-permute-start | bytes 3145736 | tf_op jit(solution)/shard_map/ppermute | solution.py:211
  566.6 38.1 %collective-permute-start.126 = (bf16[4,512,256]{2,1,0:T(8,128)(2,1)}, bf16[4,512,256]{2,1,0:T(8,128)(2,1)}, u32[]{:S(2)}, u32[]{:S(2)}) collective-permute-start(bf16[4,512,256]{2,1,0:T(8,128)(2,1)} %get-tuple-element.274), channel_id=1, source_target_pairs={{0,8},{1,9},{2,10},{3,11},{4,12},{5,13},{6,14},{7,15},{8,0},{9,1},... | collective-permute-start | bytes 3145736 | tf_op jit(solution)/shard_map/ppermute | solution.py:211
  671.1 48.4 %collective-permute-start.163 = (bf16[2,1,1024,512]{3,2,1,0:T(8,128)(2,1)}, bf16[2,1,1024,512]{3,2,1,0:T(8,128)(2,1)}, u32[]{:S(2)}, u32[]{:S(2)}) collective-permute-start(bf16[2,1,1024,512]{3,2,1,0:T(8,128)(2,1)} %get-tuple-element.329), channel_id=1, source_target_pairs={{0,16},{1,17},{2,18},{3,19},{4,20},{5,21},{6,22},{7,23},{8,24},{9,... | collective-permute-start | bytes 6291464 | tf_op jit(solution)/shard_map/ppermute | solution.py:211
  702.4 42.0 %collective-permute-start.95 = (bf16[2048,256]{1,0:T(8,128)(2,1)}, bf16[2048,256]{1,0:T(8,128)(2,1)}, u32[]{:S(2)}, u32[]{:S(2)}) collective-permute-start(bf16[2048,256]{1,0:T(8,128)(2,1)} %pad_maximum_fusion.11), channel_id=1, source_target_pairs={{0,0},{1,1},{2,2},{3,3},{8,4},{9,5},{10,6},{11,7},{4,8},{5,9},{6,1... | collective-permute-start | bytes 3145736 | tf_op jit(solution)/shard_map/ppermute | solution.py:211
  712.9 36.1 %collective-permute-start.143 = (bf16[4,512,256]{2,1,0:T(8,128)(2,1)}, bf16[4,512,256]{2,1,0:T(8,128)(2,1)}, u32[]{:S(2)}, u32[]{:S(2)}) collective-permute-start(bf16[4,512,256]{2,1,0:T(8,128)(2,1)} %pad_maximum_fusion.20), channel_id=1, source_target_pairs={{0,8},{1,9},{2,10},{3,11},{4,12},{5,13},{6,14},{7,15},{8,0},{9,1},... | collective-permute-start | bytes 3145736 | tf_op jit(solution)/shard_map/ppermute | solution.py:211
  714.1 40.8 %collective-permute-start.134 = (bf16[4,512,256]{2,1,0:T(8,128)(2,1)}, bf16[4,512,256]{2,1,0:T(8,128)(2,1)}, u32[]{:S(2)}, u32[]{:S(2)}) collective-permute-start(bf16[4,512,256]{2,1,0:T(8,128)(2,1)} %pad_maximum_fusion.19), channel_id=1, source_target_pairs={{0,8},{1,9},{2,10},{3,11},{4,12},{5,13},{6,14},{7,15},{8,0},{9,1},... | collective-permute-start | bytes 3145736 | tf_op jit(solution)/shard_map/ppermute | solution.py:211
  715.7 43.0 %collective-permute-start.125 = (bf16[4,512,256]{2,1,0:T(8,128)(2,1)}, bf16[4,512,256]{2,1,0:T(8,128)(2,1)}, u32[]{:S(2)}, u32[]{:S(2)}) collective-permute-start(bf16[4,512,256]{2,1,0:T(8,128)(2,1)} %pad_maximum_fusion.18), channel_id=1, source_target_pairs={{0,8},{1,9},{2,10},{3,11},{4,12},{5,13},{6,14},{7,15},{8,0},{9,1},... | collective-permute-start | bytes 3145736 | tf_op jit(solution)/shard_map/ppermute | solution.py:211
  719.5 43.0 %collective-permute-start.116 = (bf16[4,512,256]{2,1,0:T(8,128)(2,1)}, bf16[4,512,256]{2,1,0:T(8,128)(2,1)}, u32[]{:S(2)}, u32[]{:S(2)}) collective-permute-start(bf16[4,512,256]{2,1,0:T(8,128)(2,1)} %pad_maximum_fusion.17), channel_id=1, source_target_pairs={{0,8},{1,9},{2,10},{3,11},{4,12},{5,13},{6,14},{7,15},{8,0},{9,1},... | collective-permute-start | bytes 3145736 | tf_op jit(solution)/shard_map/ppermute | solution.py:211
  744.4 93.4 %collective-permute-start.164 = (bf16[2,2,512,1024]{3,2,1,0:T(8,128)(2,1)}, bf16[2,2,512,1024]{3,2,1,0:T(8,128)(2,1)}, u32[]{:S(2)}, u32[]{:S(2)}) collective-permute-start(bf16[2,2,512,1024]{3,2,1,0:T(8,128)(2,1)} %get-tuple-element.330), channel_id=1, source_target_pairs={{0,16},{1,17},{2,18},{3,19},{4,20},{5,21},{6,22},{7,23},{8,24},{9,... | collective-permute-start | bytes 12582920 | tf_op jit(solution)/shard_map/ppermute | solution.py:211
  749.0 52.0 %collective-permute-start.167 = (bf16[1,1024,512]{2,1,0:T(8,128)(2,1)}, bf16[1,1024,512]{2,1,0:T(8,128)(2,1)S(1)}, u32[]{:S(2)}, u32[]{:S(2)}) collective-permute-start(bf16[1,1024,512]{2,1,0:T(8,128)(2,1)} %get-tuple-element.336), channel_id=1, source_target_pairs={{0,0},{1,1},{2,2},{3,3},{8,4},{9,5},{10,6},{11,7},{4,8},{5,9},{6,1... | collective-permute-start | bytes 3145736 | tf_op jit(solution)/shard_map/ppermute | solution.py:211
  801.0 44.7 %collective-permute-start.168 = (bf16[1,1024,512]{2,1,0:T(8,128)(2,1)}, bf16[1,1024,512]{2,1,0:T(8,128)(2,1)S(1)}, u32[]{:S(2)}, u32[]{:S(2)}) collective-permute-start(bf16[1,1024,512]{2,1,0:T(8,128)(2,1)} %get-tuple-element.337), channel_id=1, source_target_pairs={{4,0},{5,1},{6,2},{7,3},{12,4},{13,5},{14,6},{15,7},{0,8},{1,9},{2... | collective-permute-start | bytes 3145736 | tf_op jit(solution)/shard_map/ppermute | solution.py:211
  822.6 48.3 %collective-permute-start.151 = (bf16[4,512,256]{2,1,0:T(8,128)(2,1)}, bf16[4,512,256]{2,1,0:T(8,128)(2,1)S(1)}, u32[]{:S(2)}, u32[]{:S(2)}) collective-permute-start(bf16[4,512,256]{2,1,0:T(8,128)(2,1)} %get-tuple-element.315), channel_id=1, source_target_pairs={{0,8},{1,9},{2,10},{3,11},{4,12},{5,13},{6,14},{7,15},{8,0},{9,1},... | collective-permute-start | bytes 3145736 | tf_op jit(solution)/shard_map/ppermute | solution.py:211
  828.6 44.1 %collective-permute-start.159 = (bf16[4,512,256]{2,1,0:T(8,128)(2,1)}, bf16[4,512,256]{2,1,0:T(8,128)(2,1)S(1)}, u32[]{:S(2)}, u32[]{:S(2)}) collective-permute-start(bf16[4,512,256]{2,1,0:T(8,128)(2,1)} %get-tuple-element.319), channel_id=1, source_target_pairs={{0,8},{1,9},{2,10},{3,11},{4,12},{5,13},{6,14},{7,15},{8,0},{9,1},... | collective-permute-start | bytes 3145736 | tf_op jit(solution)/shard_map/ppermute | solution.py:211
  845.7 33.7 %collective-permute-start.169 = (bf16[2,512,1024]{2,1,0:T(8,128)(2,1)}, bf16[2,512,1024]{2,1,0:T(8,128)(2,1)S(1)}, u32[]{:S(2)}, u32[]{:S(2)}) collective-permute-start(bf16[2,512,1024]{2,1,0:T(8,128)(2,1)} %get-tuple-element.338), channel_id=1, source_target_pairs={{0,0},{1,1},{2,2},{3,3},{8,4},{9,5},{10,6},{11,7},{4,8},{5,9},{6,1... | collective-permute-start | bytes 6291464 | tf_op jit(solution)/shard_map/ppermute | solution.py:211
  871.3 36.4 %collective-permute-start.152 = (bf16[2,512,256]{2,1,0:T(8,128)(2,1)S(1)}, bf16[2,512,256]{2,1,0:T(8,128)(2,1)S(1)}, u32[]{:S(2)}, u32[]{:S(2)}) collective-permute-start(bf16[2,512,256]{2,1,0:T(8,128)(2,1)S(1)} %slice.521), channel_id=1, source_target_pairs={{0,2},{1,3},{2,0},{3,1},{4,6},{5,7},{6,4},{7,5},{8,10},{9,11},{10,... | collective-permute-start | bytes 1572872 | tf_op jit(solution)/shard_map/ppermute | solution.py:211
  873.0 45.1 %collective-permute-start.160 = (bf16[2,512,256]{2,1,0:T(8,128)(2,1)S(1)}, bf16[2,512,256]{2,1,0:T(8,128)(2,1)S(1)}, u32[]{:S(2)}, u32[]{:S(2)}) collective-permute-start(bf16[2,512,256]{2,1,0:T(8,128)(2,1)S(1)} %slice.527), channel_id=1, source_target_pairs={{0,2},{1,3},{2,0},{3,1},{4,6},{5,7},{6,4},{7,5},{8,10},{9,11},{10,... | collective-permute-start | bytes 1572872 | tf_op jit(solution)/shard_map/ppermute | solution.py:211
  875.6 44.8 %collective-permute-start.148 = (bf16[2,512,256]{2,1,0:T(8,128)(2,1)S(1)}, bf16[2,512,256]{2,1,0:T(8,128)(2,1)S(1)}, u32[]{:S(2)}, u32[]{:S(2)}) collective-permute-start(bf16[2,512,256]{2,1,0:T(8,128)(2,1)S(1)} %slice.421), channel_id=1, source_target_pairs={{0,1},{1,0},{2,3},{3,2},{4,5},{5,4},{6,7},{7,6},{8,9},{9,8},{10,11... | collective-permute-start | bytes 1572872 | tf_op jit(solution)/shard_map/ppermute | solution.py:211
  878.1 58.5 %collective-permute-start.156 = (bf16[2,512,256]{2,1,0:T(8,128)(2,1)S(1)}, bf16[2,512,256]{2,1,0:T(8,128)(2,1)S(1)}, u32[]{:S(2)}, u32[]{:S(2)}) collective-permute-start(bf16[2,512,256]{2,1,0:T(8,128)(2,1)S(1)} %slice.429), channel_id=1, source_target_pairs={{0,1},{1,0},{2,3},{3,2},{4,5},{5,4},{6,7},{7,6},{8,9},{9,8},{10,11... | collective-permute-start | bytes 1572872 | tf_op jit(solution)/shard_map/ppermute | solution.py:211
  879.5 39.5 %collective-permute-start.165 = (bf16[2,1,256,512]{3,2,1,0:T(8,128)(2,1)S(1)}, bf16[2,1,256,512]{3,2,1,0:T(8,128)(2,1)S(1)}, u32[]{:S(2)}, u32[]{:S(2)}) collective-permute-start(bf16[2,1,256,512]{3,2,1,0:T(8,128)(2,1)S(1)} %copy-done.130), channel_id=1, source_target_pairs={{0,16},{1,17},{2,18},{3,19},{4,20},{5,21},{6,22},{7,23},{8,24},{9,... | collective-permute-start | bytes 1572872 | tf_op jit(solution)/shard_map/ppermute | solution.py:211
  907.7 59.6 %collective-permute-start.170 = (bf16[2,512,1024]{2,1,0:T(8,128)(2,1)S(1)}, bf16[2,512,1024]{2,1,0:T(8,128)(2,1)S(1)}, u32[]{:S(2)}, u32[]{:S(2)}) collective-permute-start(bf16[2,512,1024]{2,1,0:T(8,128)(2,1)S(1)} %copy-done.97), channel_id=1, source_target_pairs={{4,0},{5,1},{6,2},{7,3},{12,4},{13,5},{14,6},{15,7},{0,8},{1,9},{2... | collective-permute-start | bytes 6291464 | tf_op jit(solution)/shard_map/ppermute | solution.py:211
  920.4 47.6 %collective-permute-start.166 = (bf16[2,3,512,256]{3,2,1,0:T(8,128)(2,1)S(1)}, bf16[2,3,512,256]{3,2,1,0:T(8,128)(2,1)S(1)}, u32[]{:S(2)}, u32[]{:S(2)}) collective-permute-start(bf16[2,3,512,256]{3,2,1,0:T(8,128)(2,1)S(1)} %copy-done.128), channel_id=1, source_target_pairs={{0,16},{1,17},{2,18},{3,19},{4,20},{5,21},{6,22},{7,23},{8,24},{9,... | collective-permute-start | bytes 4718600 | tf_op jit(solution)/shard_map/ppermute | solution.py:211
  936.8 49.8 %collective-permute-start.157 = (bf16[1,512,256]{2,1,0:T(8,128)(2,1)S(1)}, bf16[1,512,256]{2,1,0:T(8,128)(2,1)S(1)}, u32[]{:S(2)}, u32[]{:S(2)}) collective-permute-start(bf16[1,512,256]{2,1,0:T(8,128)(2,1)S(1)} %slice.525), channel_id=1, source_target_pairs={{0,2},{1,3},{2,0},{3,1},{4,6},{5,7},{6,4},{7,5},{8,10},{9,11},{10,... | collective-permute-start | bytes 786440 | tf_op jit(solution)/shard_map/ppermute | solution.py:211
  938.3 50.6 %collective-permute-start.175 = (f32[4,256]{1,0:T(4,128)S(1)}, f32[4,256]{1,0:T(4,128)S(1)}, u32[]{:S(2)}, u32[]{:S(2)}) collective-permute-start(f32[4,256]{1,0:T(4,128)S(1)} %pad_maximum_fusion.46), channel_id=1, source_target_pairs={{0,4},{1,5},{2,6},{3,7},{4,0},{5,1},{6,2},{7,3},{8,12},{9,13},{10,... | collective-permute-start | bytes 12296 | tf_op jit(solution)/shard_map/ppermute | solution.py:211
  992.5 29.3 %collective-permute-start.177 = (f32[4,256]{1,0:T(4,128)S(1)}, f32[4,256]{1,0:T(4,128)S(1)}, u32[]{:S(2)}, u32[]{:S(2)}) collective-permute-start(f32[4,256]{1,0:T(4,128)S(1)} %add.771), channel_id=1, source_target_pairs={{0,0},{1,1},{2,2},{3,3},{8,4},{9,5},{10,6},{11,7},{4,8},{5,9},{6,1... | collective-permute-start | bytes 12296 | tf_op jit(solution)/shard_map/ppermute | solution.py:211
  994.3 45.7 %collective-permute-start.174 = (bf16[3,512,256]{2,1,0:T(8,128)(2,1)S(1)}, bf16[3,512,256]{2,1,0:T(8,128)(2,1)S(1)}, u32[]{:S(2)}, u32[]{:S(2)}) collective-permute-start(bf16[3,512,256]{2,1,0:T(8,128)(2,1)S(1)} %get-tuple-element.343), channel_id=1, source_target_pairs={{4,0},{5,1},{6,2},{7,3},{12,4},{13,5},{14,6},{15,7},{0,8},{1,9},{2... | collective-permute-start | bytes 2359304 | tf_op jit(solution)/shard_map/ppermute | solution.py:211
  (263 other events, 3775.8 us)
